TPU v7x, 32 devices: a whole 2x2x4 slice. The times are simulated.
32 devices in a mesh: ctx: 8 (over y, x, core), head: 4 (over z).
Axes of the slice: x: 2, y: 2, z: 4, core: 2. Of those that a mesh axis runs over, the one named last changes fastest.
Arguments:
- queries: bfloat16 [1024, 8192], P('ctx', 'head'), may hold values from -6 to 6
- keys_in: bfloat16 [1024, 1024], P('ctx', 'head'), may hold values from -6 to 6
- values_in: bfloat16 [1024, 1024], P('ctx', 'head'), may hold values from -6 to 6
- attn_cotan: bfloat16 [1024, 8192], P('ctx', 'head'), may hold values from -6 to 6
- doc_ids: int32 [1024], P('ctx'), may hold values from 0 to 5, never falling along the last dimension, each value on 1 to 512 neighbouring positions
- ssd_input: bfloat16 [1024, 16384], P('ctx', 'head'), may hold values from -0.29882812 to 0.29882812
- state_write: bfloat16 [1024, 256], P('ctx'), may hold values from -0.375 to 0.375
- state_read: bfloat16 [1024, 256], P('ctx'), may hold values from -6 to 6
- log_decay: float32 [1024, 256], P('ctx', 'head'), may hold values from -1.3 to 0
- ssd_cotan: bfloat16 [1024, 16384], P('ctx', 'head'), may hold values from -0.119628906 to 0.119628906
Outputs:
- attn_out: bfloat16 [1024, 8192], P('ctx', 'head')
- ssd_out: bfloat16 [1024, 16384], P('ctx', 'head')
- grad_q: bfloat16 [1024, 8192], P('ctx', 'head')
- grad_k: bfloat16 [1024, 1024], P('ctx', 'head')
- grad_v: bfloat16 [1024, 1024], P('ctx', 'head')
- grad_x: bfloat16 [1024, 16384], P('ctx', 'head')
- grad_b: bfloat16 [1024, 256], P(('ctx', 'head'))
- grad_c: bfloat16 [1024, 256], P(('ctx', 'head'))
Inputs may be any that keep to these rules, and one draw needn't show every extreme that they name: doc_ids never fall along the sequence; each document has 1 to 512 tokens and one has exactly that many.
All inputs are finite; a program needn't handle non-finite values.
Results may differ from a plain program's by a relative error of at most 0.035.
Values may be sent and summed in bfloat16 or wider, within the bound.
No kernel may reach another device: no remote copies, remote signals or barrier semaphores. Data moves between devices by JAX's collectives and lax.ppermute only.
A program may use at most 128 MiB of HBM per device.

v0:
```python
import math

import jax
import jax.numpy as jnp
from jax import lax
from jax.sharding import PartitionSpec as P

HD = 128
P_SIZE = 64
N = 256


floor_score = -1e30
highest = lax.Precision.HIGHEST


def prefix(x, axis, combine, identity, reverse):
    devices, position = (lax.axis_size(axis), lax.axis_index(axis))
    everything = jax.tree.map(
        lambda part, kind: lax.all_gather(part.astype(kind), axis),
        x,
        (jnp.bfloat16, jnp.bfloat16, jnp.bfloat16, jnp.bfloat16),
    )
    start = jax.tree.map(
        lambda part, zero: jnp.broadcast_to(jnp.asarray(zero, part.dtype), part.shape), x, identity
    )

    def hop(k, before):
        at = devices - 1 - k if reverse else k
        reached = at > position if reverse else at < position
        new = combine(
            before, jax.tree.map(lambda part, own: part[at].astype(own.dtype), everything, x)
        )
        return jax.tree.map(lambda a, b: jnp.where(reached, a, b), new, before)

    return lax.fori_loop(0, devices, hop, start)


def block_width(row_span):
    return math.gcd(row_span, 1024)


def block_scores(query_block, key_block, query_pos, key_pos, query_doc, key_doc):
    scores = jnp.einsum(
        "tkgd,skd->kgts", query_block, key_block, preferred_element_type=jnp.float32
    ) * HD ** (-0.5)
    allowed = (key_pos[None, :] <= query_pos[:, None]) & (key_doc[None, :] == query_doc[:, None])
    return (scores, allowed)


def block_grads(
    query_block,
    cotan_block,
    key_block,
    value_block,
    query_pos,
    key_pos,
    query_doc,
    key_doc,
    log_total,
    row_inner,
):
    scores, allowed = block_scores(query_block, key_block, query_pos, key_pos, query_doc, key_doc)
    attn_prob = jnp.where(allowed, jnp.exp(scores - log_total[..., None]), 0.0)
    prob_grad = jnp.einsum(
        "tkgd,skd->kgts", cotan_block, value_block, preferred_element_type=jnp.float32
    )
    dscore = (attn_prob * (prob_grad - row_inner[..., None])).astype(jnp.bfloat16)
    return (attn_prob.astype(jnp.bfloat16), dscore)


def forward_join(lower, upper):
    first_low, last_low, decay_low, state_low = lower
    first_up, last_up, decay_up, state_up = upper
    linked = (first_up == last_up) & (last_low == first_up)
    passing = jnp.where(first_up < 0, 1.0, jnp.where(linked, decay_up, 0.0))
    return (
        jnp.where(first_low < 0, first_up, first_low),
        jnp.where(last_up < 0, last_low, last_up),
        decay_low * decay_up,
        passing[:, None, None] * state_low + state_up,
    )


def backward_join(higher, lower):
    first_up, last_up, decay_up, grad_up = higher
    first_low, last_low, decay_low, grad_low = lower
    linked = (first_low == last_low) & (last_low == first_up)
    passing = jnp.where(first_low < 0, 1.0, jnp.where(linked, decay_low, 0.0))
    return (
        jnp.where(first_low < 0, first_up, first_low),
        jnp.where(last_up < 0, last_low, last_up),
        decay_low * decay_up,
        grad_low + passing[:, None, None] * grad_up,
    )


def body(
    queries,
    keys_in,
    values_in,
    attn_cotan,
    doc_ids,
    ssd_input,
    state_write,
    state_read,
    log_decay,
    ssd_cotan,
):
    row_count = doc_ids.shape[0]
    kv_local = keys_in.shape[1] // HD
    group_size = queries.shape[1] // keys_in.shape[1]
    query_heads = queries.reshape(row_count, kv_local, group_size, HD)
    cotan_heads = attn_cotan.reshape(row_count, kv_local, group_size, HD)
    query_pos = lax.axis_index("ctx") * row_count + jnp.arange(row_count, dtype=jnp.int32)
    start_state = (
        jnp.full((kv_local, group_size, row_count), floor_score, jnp.float32),
        jnp.zeros((kv_local, group_size, row_count), jnp.float32),
        jnp.zeros((kv_local, group_size, row_count, HD), jnp.float32),
    )
    key_all = lax.all_gather(keys_in, "ctx", axis=0, tiled=True)
    value_all = lax.all_gather(values_in, "ctx", axis=0, tiled=True)
    doc_all = lax.all_gather(doc_ids, "ctx", axis=0, tiled=True)
    row_span = key_all.shape[0]
    block_rows = block_width(row_span)

    def visit_block(block_index, running):
        row_top, row_total, weighted_sum = running
        first_row = block_index * block_rows
        key_block = lax.dynamic_slice_in_dim(key_all, first_row, block_rows, 0).reshape(
            block_rows, kv_local, HD
        )
        value_block = lax.dynamic_slice_in_dim(value_all, first_row, block_rows, 0).reshape(
            block_rows, kv_local, HD
        )
        doc_block = lax.dynamic_slice_in_dim(doc_all, first_row, block_rows, 0)
        key_pos = first_row + jnp.arange(block_rows, dtype=jnp.int32)
        scores, allowed = block_scores(
            query_heads, key_block, query_pos, key_pos, doc_ids, doc_block
        )
        masked = jnp.where(allowed, scores, floor_score)
        new_top = jnp.maximum(row_top, jnp.max(masked, axis=-1))
        weights = jnp.where(allowed, jnp.exp(masked - new_top[..., None]), 0.0)
        shrink = jnp.exp(row_top - new_top)
        row_total = row_total * shrink + jnp.sum(weights, axis=-1)
        weighted_sum = weighted_sum * shrink[..., None] + jnp.einsum(
            "kgts,skd->kgtd",
            weights.astype(jnp.bfloat16),
            value_block,
            preferred_element_type=jnp.float32,
        )
        return (new_top, row_total, weighted_sum)

    row_top, row_total, weighted_sum = lax.fori_loop(
        0, row_span // block_rows, visit_block, start_state
    )
    key_whole, value_whole, doc_whole = (
        lax.all_gather(keys_in, "ctx", axis=0, tiled=True),
        lax.all_gather(values_in, "ctx", axis=0, tiled=True),
        lax.all_gather(doc_ids, "ctx", axis=0, tiled=True),
    )
    attn_heads = weighted_sum / row_total[..., None]
    attn_out = attn_heads.transpose(2, 0, 1, 3).reshape(row_count, -1).astype(jnp.bfloat16)
    log_total = row_top + jnp.log(row_total)
    row_inner = jnp.sum(
        cotan_heads.astype(jnp.float32)
        * attn_out.reshape(row_count, kv_local, group_size, HD).astype(jnp.float32),
        axis=-1,
    ).transpose(1, 2, 0)
    key_total = key_whole.shape[0]
    key_rows = block_width(key_total)

    def key_slices(first_row, block_rows):
        key_block = lax.dynamic_slice_in_dim(key_whole, first_row, block_rows, 0).reshape(
            block_rows, kv_local, HD
        )
        value_block = lax.dynamic_slice_in_dim(value_whole, first_row, block_rows, 0).reshape(
            block_rows, kv_local, HD
        )
        doc_block = lax.dynamic_slice_in_dim(doc_whole, first_row, block_rows, 0)
        return (key_block, value_block, doc_block)

    def query_visit(block_index, grad_running):
        first_row = block_index * key_rows
        key_block, value_block, doc_block = key_slices(first_row, key_rows)
        key_pos = first_row + jnp.arange(key_rows, dtype=jnp.int32)
        _, dscore = block_grads(
            query_heads,
            cotan_heads,
            key_block,
            value_block,
            query_pos,
            key_pos,
            doc_ids,
            doc_block,
            log_total,
            row_inner,
        )
        return grad_running + jnp.einsum(
            "kgts,skd->tkgd", dscore, key_block, preferred_element_type=jnp.float32
        )

    grad_q_sum = lax.fori_loop(
        0,
        key_total // key_rows,
        query_visit,
        jnp.zeros((row_count, kv_local, group_size, HD), jnp.float32),
    )
    grad_q = (grad_q_sum * HD ** (-0.5)).reshape(row_count, -1).astype(jnp.bfloat16)
    key_block_rows = block_width(lax.axis_size("ctx") * row_count)

    def one_block(block_index):
        first_row = block_index * key_block_rows
        key_block, value_block, doc_block = key_slices(first_row, key_block_rows)
        key_pos = first_row + jnp.arange(key_block_rows, dtype=jnp.int32)
        prob_low, dscore = block_grads(
            query_heads,
            cotan_heads,
            key_block,
            value_block,
            query_pos,
            key_pos,
            doc_ids,
            doc_block,
            log_total,
            row_inner,
        )
        part_key = jnp.einsum(
            "kgts,tkgd->skd", dscore, query_heads, preferred_element_type=jnp.float32
        ) * HD ** (-0.5)
        part_value = jnp.einsum(
            "kgts,tkgd->skd", prob_low, cotan_heads, preferred_element_type=jnp.float32
        )
        return jnp.concatenate(
            [part_key.reshape(key_block_rows, -1), part_value.reshape(key_block_rows, -1)], axis=1
        )

    summed = lax.psum_scatter(
        lax.map(
            one_block,
            jnp.arange(lax.axis_size("ctx") * row_count // key_block_rows, dtype=jnp.int32),
        )
        .reshape(lax.axis_size("ctx") * row_count, -1)
        .astype(jnp.bfloat16),
        "ctx",
        scatter_dimension=0,
        tiled=True,
    ).astype(jnp.float32)
    grad_k = summed[:, : kv_local * HD].astype(jnp.bfloat16)
    grad_v = summed[:, kv_local * HD :].astype(jnp.bfloat16)
    heads_local = log_decay.shape[1]
    input_low = ssd_input.reshape(row_count, heads_local, P_SIZE)
    cotan_low = ssd_cotan.reshape(row_count, heads_local, P_SIZE)
    input_wide = input_low.astype(jnp.float32)
    cotan_wide = cotan_low.astype(jnp.float32)
    write_wide = state_write.astype(jnp.float32)
    read_wide = state_read.astype(jnp.float32)
    cum_decay = jnp.cumsum(log_decay, axis=0)
    local_pos = jnp.arange(row_count, dtype=jnp.int32)
    linked_rows = (doc_ids[:, None] == doc_ids[None, :]) & (
        local_pos[None, :] <= local_pos[:, None]
    )
    log_gap = cum_decay.T[:, :, None] - cum_decay.T[:, None, :]
    kernel = jnp.where(linked_rows[None], jnp.exp(jnp.where(linked_rows[None], log_gap, 0.0)), 0.0)
    gram_matrix = jnp.dot(state_read, state_write.T, preferred_element_type=jnp.float32)
    mixing = kernel * gram_matrix[None]
    doc_float = doc_ids.astype(jnp.float32)
    first_doc = doc_float[:1]
    last_doc = doc_float[-1:]
    tail_decay = cum_decay[-1]
    end_weight = jnp.where(
        doc_ids[:, None] == doc_ids[-1], jnp.exp(tail_decay[None, :] - cum_decay), 0.0
    )
    start_weight = jnp.where(doc_ids[:, None] == doc_ids[0], jnp.exp(cum_decay), 0.0)
    state_sum = jnp.einsum(
        "shp,sn->hpn", end_weight[:, :, None] * input_wide, write_wide, precision=highest
    )
    grad_sum = jnp.einsum(
        "thp,tn->hpn", start_weight[:, :, None] * cotan_wide, read_wide, precision=highest
    )
    decay_all = jnp.exp(tail_decay)
    identity = (
        jnp.full((1,), -1.0, jnp.float32),
        jnp.full((1,), -1.0, jnp.float32),
        jnp.ones((heads_local,), jnp.float32),
        jnp.zeros((heads_local, P_SIZE, N), jnp.float32),
    )
    _, enter_doc, _, state_in = prefix(
        (first_doc, last_doc, decay_all, state_sum), "ctx", forward_join, identity, False
    )
    next_doc, _, _, grad_in = prefix(
        (first_doc, last_doc, decay_all, grad_sum), "ctx", backward_join, identity, True
    )
    enter_weight = jnp.where(doc_float[:, None] == enter_doc, jnp.exp(cum_decay), 0.0)
    exit_weight = jnp.where(
        doc_float[:, None] == next_doc, jnp.exp(tail_decay[None, :] - cum_decay), 0.0
    )
    ssd_local = jnp.einsum("hts,shp->thp", mixing, input_wide, precision=highest)
    ssd_full = ssd_local + enter_weight[:, :, None] * jnp.einsum(
        "tn,hpn->thp", read_wide, state_in, precision=highest
    )
    ssd_out = ssd_full.reshape(row_count, -1).astype(jnp.bfloat16)
    grad_input = jnp.einsum("hts,thp->shp", mixing, cotan_wide, precision=highest)
    grad_input = grad_input + exit_weight[:, :, None] * jnp.einsum(
        "sn,hpn->shp", write_wide, grad_in, precision=highest
    )
    grad_x = grad_input.reshape(row_count, -1).astype(jnp.bfloat16)
    pair_inner = jnp.einsum(
        "thp,shp->hts", cotan_low, input_low, preferred_element_type=jnp.float32
    )
    weighted = kernel * pair_inner
    write_terms = jnp.einsum("hts,tn->sn", weighted, read_wide, precision=highest)
    write_terms = write_terms + jnp.einsum(
        "shp,hpn->sn", exit_weight[:, :, None] * input_wide, grad_in, precision=highest
    )
    read_terms = jnp.einsum("hts,sn->tn", weighted, write_wide, precision=highest)
    read_terms = read_terms + jnp.einsum(
        "thp,hpn->tn", enter_weight[:, :, None] * cotan_wide, state_in, precision=highest
    )
    grad_b_sum, grad_c_sum = (
        lax.psum_scatter(
            write_terms.astype(jnp.bfloat16), "head", scatter_dimension=0, tiled=True
        ).astype(jnp.float32),
        lax.psum_scatter(
            read_terms.astype(jnp.bfloat16), "head", scatter_dimension=0, tiled=True
        ).astype(jnp.float32),
    )
    grad_b = grad_b_sum.astype(jnp.bfloat16)
    grad_c = grad_c_sum.astype(jnp.bfloat16)
    return (attn_out, ssd_out, grad_q, grad_k, grad_v, grad_x, grad_b, grad_c)


def solution(mesh):
    in_specs = (
        P("ctx", "head"),
        P("ctx", "head"),
        P("ctx", "head"),
        P("ctx", "head"),
        P("ctx"),
        P("ctx", "head"),
        P("ctx", None),
        P("ctx", None),
        P("ctx", "head"),
        P("ctx", "head"),
    )
    out_specs = (
        P("ctx", "head"),
        P("ctx", "head"),
        P("ctx", "head"),
        P("ctx", "head"),
        P("ctx", "head"),
        P("ctx", "head"),
        P(("ctx", "head"), None),
        P(("ctx", "head"), None),
    )
    return jax.shard_map(body, mesh=mesh, in_specs=in_specs, out_specs=out_specs, check_vma=False)
```

profile of v0, /device:TPU:23, one launch (start us, length us, event | category | flops | bytes accessed | tf_op | source)
XLA Modules:
  0.0 395.0 jit_solution(1529374442707623125)
XLA Ops:
  7.2 0.9 copy.76
  8.2 1.3 fusion.87
  9.5 1.3 broadcast_compare_fusion
  11.2 1.6 copy.91
  12.8 4.0 %fusion.43 = bf16[64,64,256]{2,1,0:T(8,128)(2,1)} fusion(bf16[128,64,64]{0,2,1:T(8,128)(2,1)S(1)} %bitcast.222, f32[128,64]{0,1:T(8,128)S(1)} %copy.92, bf16[128,256]{1,0:T(8,128)(2,1)} %param.21), kind=kOutput, calls=%fused_computation.63 | convolution fusion | flops 1612709888 | bytes 3244032 | tf_op jit(solution)/shard_map/thp,tn->hpn/dot_general | solution.py:278
  17.4 9.4 %all_gather.48 = bf16[1024,256]{1,0:T(8,128)(2,1)S(1)} all-gather(bf16[128,256]{1,0:T(8,128)(2,1)S(1)} %copy-done.9), channel_id=1, replica_groups=mesh['ctx'=8,'head'=4] {'ctx'}, dimensions={0}, use_global_device_ids=true | all-gather | bytes 589824 | tf_op jit(solution)/shard_map/all_gather | solution.py:122
  26.8 1.0 copy.74
  28.1 8.7 %all-gather.4 = s32[8,1,128]{2,1,0:T(1,128)S(1)} all-gather(s32[1,1,128]{2,1,0:T(1,128)S(1)} %bitcast.249), channel_id=1, replica_groups=mesh['ctx'=8,'head'=4] {'ctx'}, dimensions={0}, use_global_device_ids=true | all-gather | bytes 4608 | tf_op jit(solution)/shard_map/all_gather | solution.py:123
  36.8 11.7 %all_gather.47 = bf16[1024,256]{0,1:T(8,128)(2,1)S(1)} all-gather(bf16[128,256]{0,1:T(8,128)(2,1)S(1)} %copy.71), channel_id=1, replica_groups=mesh['ctx'=8,'head'=4] {'ctx'}, dimensions={0}, use_global_device_ids=true | all-gather | bytes 589824 | tf_op jit(solution)/shard_map/all_gather | solution.py:121
  48.7 1.4 fusion.10
  50.2 2.0 fusion.12
  52.2 3.2 multiply_reduce_fusion.1
  55.4 2.9 fusion.7
  58.3 2.0 copy-done.2
  60.2 1.5 fusion.55
  61.9 6.4 %fusion.57 = bf16[2,1024,128]{1,2,0:T(8,128)(2,1)S(1)} fusion(bf16[128,2,8,128]{0,3,2,1:T(8,128)(2,1)} %bitcast.243, f32[2,1024,128,8]{2,1,3,0:T(8,128)} %copy-done.1, f32[2,8,128]{2,1,0:T(8,128)S(1)} %get-tuple-element.575, pred[128,1024]{0,1:T(8,128)(4,1)S(1)} %fusion.70), kind=kOutput, calls=%fused_computation.73 | convolution fusion | flops 545521664 | bytes 9576448 | tf_op jit(solution)/shard_map/while/body/eval_jaxpr/kgts,tkgd->skd/dot_general | solution.py:231
  68.6 1.1 pad_maximum_fusion
  70.3 8.0 %all-gather.5 = bf16[8,1,64]{2,1,0:T(2,128)(2,1)S(1)} all-gather(bf16[1,1,64]{2,1,0:T(2,128)(2,1)S(1)} %get-tuple-element.574), channel_id=1, replica_groups=mesh['ctx'=8,'head'=4] {'ctx'}, dimensions={0}, use_global_device_ids=true | all-gather | bytes 1152 | tf_op jit(solution)/shard_map/all_gather | solution.py:20
  78.9 1.4 dynamic-update-slice
  80.3 1.4 dynamic-update-slice.1
  81.7 1.6 copy.79
  83.4 11.8 %all-reduce.2 = (bf16[8]{0:T(256)(128)(2,1)S(1)}, bf16[8]{0:T(256)(128)(2,1)S(1)}) all-reduce(bf16[8]{0:T(256)(128)(2,1)S(1)} %dynamic-update-slice, bf16[8]{0:T(256)(128)(2,1)S(1)} %dynamic-update-slice.1), channel_id=2, replica_groups=mesh['ctx'=8,'head'=4] {'ctx'}, use_global_device_ids=true, to_apply=%add | all-reduce | flops 16 | bytes 64
  95.2 14.5 %all-gather.11.cloned.1.call-done = bf16[512,64,256]{2,1,0:T(8,128)(2,1)} async-done(((bf16[64,64,256]{2,1,0:T(8,128)(2,1)}), bf16[512,64,256]{2,1,0:T(8,128)(2,1)}) %all-gather.11.cloned.1.call-update) | async-done | bytes 16777232 | tf_op jit(solution)/shard_map/all_gather | solution.py:20
  109.7 77.8 %while.23 = (s32[]{:T(128)}, f32[1]{0:T(128)}, f32[64,64,256]{2,1,0:T(8,128)}, s32[]{:T(128)}, bf16[8,1]{0,1:T(2,128)(2,1)S(1)}, /*index=5*/bf16[8,64,64,256]{3,...) while((s32[]{:T(128)}, f32[1]{0:T(128)}, ...), condition=%wide.region_8.9_spmd.clone, body=%wide.region_7.8_spmd.clone.sunk | while | flops 5243086 | bytes 10486659 | solution.py:36
  112.9 4.7 %fusion.121 = f32[64,64,256]{2,1,0:T(8,128)} fusion(f32[64,64,256]{2,1,0:T(8,128)} %get-tuple-element.708, f32[64]{0:T(128)S(1)} %fusion.120, bf16[8,64,64,256]{3,2,1,0:T(8,128)(2,1)} %get-tuple-element.724, s32[]{:T(128)S(6)} %select_n.352, pred[]{:T(512)S(6)} %compare.7, pred[]{:T(512)} %gt.12), kind=kLoop, calls=%fused_computation.10.clone.1 | loop fusion | flops 5242880 | bytes 10486022 | tf_op jit(solution)/shard_map/while/body/eval_jaxpr/jit(_where)/select_n | solution.py:34
  121.5 6.1 %fusion.121 = f32[64,64,256]{2,1,0:T(8,128)} fusion(f32[64,64,256]{2,1,0:T(8,128)} %get-tuple-element.708, f32[64]{0:T(128)S(1)} %fusion.120, bf16[8,64,64,256]{3,2,1,0:T(8,128)(2,1)} %get-tuple-element.724, s32[]{:T(128)S(6)} %select_n.352, pred[]{:T(512)S(6)} %compare.7, pred[]{:T(512)} %gt.12), kind=kLoop, calls=%fused_computation.10.clone.1 | loop fusion | flops 5242880 | bytes 10486022 | tf_op jit(solution)/shard_map/while/body/eval_jaxpr/jit(_where)/select_n | solution.py:34
  131.5 6.0 %fusion.121 = f32[64,64,256]{2,1,0:T(8,128)} fusion(f32[64,64,256]{2,1,0:T(8,128)} %get-tuple-element.708, f32[64]{0:T(128)S(1)} %fusion.120, bf16[8,64,64,256]{3,2,1,0:T(8,128)(2,1)} %get-tuple-element.724, s32[]{:T(128)S(6)} %select_n.352, pred[]{:T(512)S(6)} %compare.7, pred[]{:T(512)} %gt.12), kind=kLoop, calls=%fused_computation.10.clone.1 | loop fusion | flops 5242880 | bytes 10486022 | tf_op jit(solution)/shard_map/while/body/eval_jaxpr/jit(_where)/select_n | solution.py:34
  141.4 6.0 %fusion.121 = f32[64,64,256]{2,1,0:T(8,128)} fusion(f32[64,64,256]{2,1,0:T(8,128)} %get-tuple-element.708, f32[64]{0:T(128)S(1)} %fusion.120, bf16[8,64,64,256]{3,2,1,0:T(8,128)(2,1)} %get-tuple-element.724, s32[]{:T(128)S(6)} %select_n.352, pred[]{:T(512)S(6)} %compare.7, pred[]{:T(512)} %gt.12), kind=kLoop, calls=%fused_computation.10.clone.1 | loop fusion | flops 5242880 | bytes 10486022 | tf_op jit(solution)/shard_map/while/body/eval_jaxpr/jit(_where)/select_n | solution.py:34
  151.3 6.0 %fusion.121 = f32[64,64,256]{2,1,0:T(8,128)} fusion(f32[64,64,256]{2,1,0:T(8,128)} %get-tuple-element.708, f32[64]{0:T(128)S(1)} %fusion.120, bf16[8,64,64,256]{3,2,1,0:T(8,128)(2,1)} %get-tuple-element.724, s32[]{:T(128)S(6)} %select_n.352, pred[]{:T(512)S(6)} %compare.7, pred[]{:T(512)} %gt.12), kind=kLoop, calls=%fused_computation.10.clone.1 | loop fusion | flops 5242880 | bytes 10486022 | tf_op jit(solution)/shard_map/while/body/eval_jaxpr/jit(_where)/select_n | solution.py:34
  161.1 6.0 %fusion.121 = f32[64,64,256]{2,1,0:T(8,128)} fusion(f32[64,64,256]{2,1,0:T(8,128)} %get-tuple-element.708, f32[64]{0:T(128)S(1)} %fusion.120, bf16[8,64,64,256]{3,2,1,0:T(8,128)(2,1)} %get-tuple-element.724, s32[]{:T(128)S(6)} %select_n.352, pred[]{:T(512)S(6)} %compare.7, pred[]{:T(512)} %gt.12), kind=kLoop, calls=%fused_computation.10.clone.1 | loop fusion | flops 5242880 | bytes 10486022 | tf_op jit(solution)/shard_map/while/body/eval_jaxpr/jit(_where)/select_n | solution.py:34
  171.0 6.0 %fusion.121 = f32[64,64,256]{2,1,0:T(8,128)} fusion(f32[64,64,256]{2,1,0:T(8,128)} %get-tuple-element.708, f32[64]{0:T(128)S(1)} %fusion.120, bf16[8,64,64,256]{3,2,1,0:T(8,128)(2,1)} %get-tuple-element.724, s32[]{:T(128)S(6)} %select_n.352, pred[]{:T(512)S(6)} %compare.7, pred[]{:T(512)} %gt.12), kind=kLoop, calls=%fused_computation.10.clone.1 | loop fusion | flops 5242880 | bytes 10486022 | tf_op jit(solution)/shard_map/while/body/eval_jaxpr/jit(_where)/select_n | solution.py:34
  180.9 6.0 %fusion.121 = f32[64,64,256]{2,1,0:T(8,128)} fusion(f32[64,64,256]{2,1,0:T(8,128)} %get-tuple-element.708, f32[64]{0:T(128)S(1)} %fusion.120, bf16[8,64,64,256]{3,2,1,0:T(8,128)(2,1)} %get-tuple-element.724, s32[]{:T(128)S(6)} %select_n.352, pred[]{:T(512)S(6)} %compare.7, pred[]{:T(512)} %gt.12), kind=kLoop, calls=%fused_computation.10.clone.1 | loop fusion | flops 5242880 | bytes 10486022 | tf_op jit(solution)/shard_map/while/body/eval_jaxpr/jit(_where)/select_n | solution.py:34
  188.3 3.1 fusion.44
  191.6 2.9 fusion.56
  194.6 1.0 copy.96
  195.6 2.0 copy.94
  197.9 4.4 %fusion.15 = f32[64,128,64]{1,2,0:T(8,128)} fusion(bf16[128,64,64]{0,2,1:T(8,128)(2,1)S(1)} %bitcast.223, f32[128,128]{1,0:T(8,128)S(1)} %fusion.89, f32[64,128]{1,0:T(8,128)S(1)} %copy.77, pred[128,128]{1,0:T(8,128)(4,1)S(1)} %fusion.75), kind=kOutput, calls=%fused_computation.33 | convolution fusion | flops 809500672 | bytes 3260416 | tf_op jit(solution)/shard_map/hts,thp->shp/dot_general | solution.py:303
  202.3 6.2 %fusion.17 = f32[64,128,64]{1,2,0:T(8,128)} fusion(bf16[128,64,64]{0,2,1:T(8,128)(2,1)S(1)} %bitcast.227, f32[128,128]{1,0:T(8,128)S(1)} %fusion.89, f32[64,128]{1,0:T(8,128)S(1)} %copy.77, pred[128,128]{1,0:T(8,128)(4,1)S(1)} %fusion.75), kind=kOutput, calls=%fused_computation.34 | convolution fusion | flops 809500672 | bytes 3260416 | tf_op jit(solution)/shard_map/hts,shp->thp/dot_general | solution.py:298
  208.5 2.2 multiply_reduce_fusion
  210.7 1.5 fusion.86
  212.3 4.9 %fusion.30 = bf16[128,64,64]{0,2,1:T(8,128)(2,1)S(1)} fusion(f32[64,128,64]{1,2,0:T(8,128)} %fusion.15, f32[64,64,256]{2,1,0:T(8,128)} %get-tuple-element.452, f32[128,64]{0,1:T(8,128)S(1)} %copy.93, bf16[128,256]{1,0:T(8,128)(2,1)S(1)} %copy-done), kind=kOutput, calls=%fused_computation.49 | convolution fusion | flops 1612185600 | bytes 7438336 | tf_op jit(solution)/shard_map/sn,hpn->shp/dot_general | solution.py:304
  217.1 1.3 copy.97
  218.4 5.8 %fusion.61 = f32[128,256]{1,0:T(8,128)S(1)} fusion(f32[64,64,256]{2,1,0:T(8,128)} %get-tuple-element.452, bf16[128,64,64]{0,2,1:T(8,128)(2,1)S(1)} %bitcast.229, f32[128,64]{0,1:T(8,128)S(1)} %copy.93), kind=kOutput, calls=%fused_computation.77 | convolution fusion | flops 1611661312 | bytes 5406720 | tf_op jit(solution)/shard_map/shp,hpn->sn/dot_general | solution.py:313
  224.3 0.9 fusion.62
  225.5 56.1 %all-gather.9.cloned.1.call-done = bf16[512,64,256]{2,1,0:T(8,128)(2,1)} async-done(((bf16[64,64,256]{2,1,0:T(8,128)(2,1)}), bf16[512,64,256]{2,1,0:T(8,128)(2,1)}) %all-gather.9.cloned.1.call-update) | async-done | bytes 16777232 | tf_op jit(solution)/shard_map/all_gather | solution.py:20
  281.7 84.2 %while.22 = (s32[]{:T(128)}, f32[1]{0:T(128)}, f32[64,64,256]{2,1,0:T(8,128)}, s32[]{:T(128)}, bf16[8,1]{0,1:T(2,128)(2,1)S(1)}, /*index=5*/bf16[8,1]{0,1:T(2,12...) while((s32[]{:T(128)}, f32[1]{0:T(128)}, ...), condition=%wide.region_4.5_spmd.clone, body=%wide.region_3.4_spmd.clone.sunk | while | flops 5243083 | bytes 10486604 | solution.py:36
  285.0 4.7 %fusion.119 = f32[64,64,256]{2,1,0:T(8,128)} fusion(f32[64,64,256]{2,1,0:T(8,128)} %get-tuple-element.745, bf16[8,64,64,256]{3,2,1,0:T(8,128)(2,1)} %get-tuple-element.761, s32[]{:T(128)} %get-tuple-element.743, f32[64]{0:T(128)S(1)} %fusion.118, pred[]{:T(512)S(6)} %compare.6, pred[]{:T(512)} %lt.94), kind=kLoop, calls=%fused_computation.1.clone.1 | loop fusion | flops 5242880 | bytes 10486022 | tf_op jit(solution)/shard_map/while/body/eval_jaxpr/jit(_where)/select_n | solution.py:34
  291.1 0.7 constant_dynamic-slice_fusion.8
  294.4 6.0 %fusion.119 = f32[64,64,256]{2,1,0:T(8,128)} fusion(f32[64,64,256]{2,1,0:T(8,128)} %get-tuple-element.745, bf16[8,64,64,256]{3,2,1,0:T(8,128)(2,1)} %get-tuple-element.761, s32[]{:T(128)} %get-tuple-element.743, f32[64]{0:T(128)S(1)} %fusion.118, pred[]{:T(512)S(6)} %compare.6, pred[]{:T(512)} %lt.94), kind=kLoop, calls=%fused_computation.1.clone.1 | loop fusion | flops 5242880 | bytes 10486022 | tf_op jit(solution)/shard_map/while/body/eval_jaxpr/jit(_where)/select_n | solution.py:34
  305.1 5.9 %fusion.119 = f32[64,64,256]{2,1,0:T(8,128)} fusion(f32[64,64,256]{2,1,0:T(8,128)} %get-tuple-element.745, bf16[8,64,64,256]{3,2,1,0:T(8,128)(2,1)} %get-tuple-element.761, s32[]{:T(128)} %get-tuple-element.743, f32[64]{0:T(128)S(1)} %fusion.118, pred[]{:T(512)S(6)} %compare.6, pred[]{:T(512)} %lt.94), kind=kLoop, calls=%fused_computation.1.clone.1 | loop fusion | flops 5242880 | bytes 10486022 | tf_op jit(solution)/shard_map/while/body/eval_jaxpr/jit(_where)/select_n | solution.py:34
  312.5 0.7 constant_dynamic-slice_fusion.8
  315.8 5.9 %fusion.119 = f32[64,64,256]{2,1,0:T(8,128)} fusion(f32[64,64,256]{2,1,0:T(8,128)} %get-tuple-element.745, bf16[8,64,64,256]{3,2,1,0:T(8,128)(2,1)} %get-tuple-element.761, s32[]{:T(128)} %get-tuple-element.743, f32[64]{0:T(128)S(1)} %fusion.118, pred[]{:T(512)S(6)} %compare.6, pred[]{:T(512)} %lt.94), kind=kLoop, calls=%fused_computation.1.clone.1 | loop fusion | flops 5242880 | bytes 10486022 | tf_op jit(solution)/shard_map/while/body/eval_jaxpr/jit(_where)/select_n | solution.py:34
  323.1 0.7 constant_dynamic-slice_fusion.8
  326.5 5.9 %fusion.119 = f32[64,64,256]{2,1,0:T(8,128)} fusion(f32[64,64,256]{2,1,0:T(8,128)} %get-tuple-element.745, bf16[8,64,64,256]{3,2,1,0:T(8,128)(2,1)} %get-tuple-element.761, s32[]{:T(128)} %get-tuple-element.743, f32[64]{0:T(128)S(1)} %fusion.118, pred[]{:T(512)S(6)} %compare.6, pred[]{:T(512)} %lt.94), kind=kLoop, calls=%fused_computation.1.clone.1 | loop fusion | flops 5242880 | bytes 10486022 | tf_op jit(solution)/shard_map/while/body/eval_jaxpr/jit(_where)/select_n | solution.py:34
  333.8 0.7 constant_dynamic-slice_fusion.8
  337.2 5.9 %fusion.119 = f32[64,64,256]{2,1,0:T(8,128)} fusion(f32[64,64,256]{2,1,0:T(8,128)} %get-tuple-element.745, bf16[8,64,64,256]{3,2,1,0:T(8,128)(2,1)} %get-tuple-element.761, s32[]{:T(128)} %get-tuple-element.743, f32[64]{0:T(128)S(1)} %fusion.118, pred[]{:T(512)S(6)} %compare.6, pred[]{:T(512)} %lt.94), kind=kLoop, calls=%fused_computation.1.clone.1 | loop fusion | flops 5242880 | bytes 10486022 | tf_op jit(solution)/shard_map/while/body/eval_jaxpr/jit(_where)/select_n | solution.py:34
  347.8 5.9 %fusion.119 = f32[64,64,256]{2,1,0:T(8,128)} fusion(f32[64,64,256]{2,1,0:T(8,128)} %get-tuple-element.745, bf16[8,64,64,256]{3,2,1,0:T(8,128)(2,1)} %get-tuple-element.761, s32[]{:T(128)} %get-tuple-element.743, f32[64]{0:T(128)S(1)} %fusion.118, pred[]{:T(512)S(6)} %compare.6, pred[]{:T(512)} %lt.94), kind=kLoop, calls=%fused_computation.1.clone.1 | loop fusion | flops 5242880 | bytes 10486022 | tf_op jit(solution)/shard_map/while/body/eval_jaxpr/jit(_where)/select_n | solution.py:34
  355.2 0.7 constant_dynamic-slice_fusion.8
  358.5 5.9 %fusion.119 = f32[64,64,256]{2,1,0:T(8,128)} fusion(f32[64,64,256]{2,1,0:T(8,128)} %get-tuple-element.745, bf16[8,64,64,256]{3,2,1,0:T(8,128)(2,1)} %get-tuple-element.761, s32[]{:T(128)} %get-tuple-element.743, f32[64]{0:T(128)S(1)} %fusion.118, pred[]{:T(512)S(6)} %compare.6, pred[]{:T(512)} %lt.94), kind=kLoop, calls=%fused_computation.1.clone.1 | loop fusion | flops 5242880 | bytes 10486022 | tf_op jit(solution)/shard_map/while/body/eval_jaxpr/jit(_where)/select_n | solution.py:34
  366.0 6.0 %fusion.60 = f32[128,256]{1,0:T(8,128)S(1)} fusion(f32[64,64,256]{2,1,0:T(8,128)} %get-tuple-element.450, bf16[128,64,64]{0,2,1:T(8,128)(2,1)S(1)} %bitcast.225, f32[128,64]{0,1:T(8,128)S(1)} %copy.81), kind=kOutput, calls=%fused_computation.76 | convolution fusion | flops 1611661312 | bytes 5406720 | tf_op jit(solution)/shard_map/thp,hpn->tn/dot_general | solution.py:317
  372.0 0.8 fusion.63
  372.9 4.2 %fusion.32 = bf16[128,64,64]{0,2,1:T(8,128)(2,1)S(1)} fusion(f32[64,128,64]{1,2,0:T(8,128)S(1)} %copy-done.3, f32[64,64,256]{2,1,0:T(8,128)} %get-tuple-element.450, f32[128,64]{0,1:T(8,128)S(1)} %copy.81, bf16[128,256]{1,0:T(8,128)(2,1)S(1)} %copy-done.4), kind=kOutput, calls=%fused_computation.52 | convolution fusion | flops 1612185600 | bytes 7438336 | tf_op jit(solution)/shard_map/tn,hpn->thp/dot_general | solution.py:299
  377.0 1.3 copy.95
  378.3 10.1 %reduce-scatter.8.cloned.1.call-done = bf16[32,256]{1,0:T(8,128)(2,1)} async-done(((bf16[128,256]{1,0:T(8,128)(2,1)}), bf16[32,256]{1,0:T(8,128)(2,1)}) %reduce-scatter.8.cloned.1.call-update) | async-done | bytes 16400 | tf_op jit(solution)/shard_map/reduce_scatter | solution.py:324
  (96 shorter events, 11.7 us)
Async XLA Ops:
  7.2 181.2 %copy-start = (bf16[128,256]{1,0:T(8,128)(2,1)S(1)}, bf16[128,256]{1,0:T(8,128)(2,1)}, u32[]{:S(2)}) copy-start(bf16[128,256]{1,0:T(8,128)(2,1)} %param.20) | copy-start | bytes 196612
  7.2 9.8 %copy-start.10 = (bf16[128,256]{1,0:T(8,128)(2,1)S(1)}, bf16[128,256]{1,0:T(8,128)(2,1)}, u32[]{:S(2)}) copy-start(bf16[128,256]{1,0:T(8,128)(2,1)} %param.15) | copy-start | bytes 196612
  7.2 9.9 %copy-start.5 = (bf16[128,2048]{1,0:T(8,128)(2,1)S(1)}, bf16[128,2048]{1,0:T(8,128)(2,1)}, u32[]{:S(2)}) copy-start(bf16[128,2048]{1,0:T(8,128)(2,1)} %param.14) | copy-start | bytes 1572868
  7.2 102.5 %all-gather.11.cloned.1.call-start = ((), (), s32[]{:S(2)}) async-start(), calls=%async_computation.7 | async-start | bytes 18874368 | tf_op jit(solution)/shard_map/all_gather | solution.py:20
  11.1 6.2 %copy-start.9 = (bf16[128,256]{1,0:T(8,128)(2,1)S(1)}, bf16[128,256]{1,0:T(8,128)(2,1)}, u32[]{:S(2)}) copy-start(bf16[128,256]{1,0:T(8,128)(2,1)} %param.16) | copy-start | bytes 196612
  12.8 15.0 %copy-start.6 = (bf16[128,2048]{1,0:T(8,128)(2,1)S(1)}, bf16[128,2048]{1,0:T(8,128)(2,1)}, u32[]{:S(2)}) copy-start(bf16[128,2048]{1,0:T(8,128)(2,1)} %param.17) | copy-start | bytes 1572868
  12.8 15.2 %copy-start.11 = (s32[128]{0:T(128)S(1)}, s32[128]{0:T(128)}, u32[]{:S(2)}) copy-start(s32[128]{0:T(128)} %param.18) | copy-start | bytes 1540
  16.9 193.8 %reduce-scatter.4.cloned.1.call-start = ((), (), s32[]{:S(2)}) async-start(), calls=%async_computation.3 | async-start | bytes 1179648 | tf_op jit(solution)/shard_map/reduce_scatter | solution.py:238
  28.1 27.3 %copy-start.7 = (bf16[128,2048]{0,1:T(8,128)(2,1)}, bf16[128,2048]{0,1:T(8,128)(2,1)S(1)}, u32[]{:S(2)}) copy-start(bf16[128,2048]{0,1:T(8,128)(2,1)S(1)} %copy.82) | copy-start | bytes 1572868
  50.1 5.2 %copy-start.1 = (f32[2,1024,128,8]{2,1,3,0:T(8,128)}, f32[2,1024,128,8]{2,1,3,0:T(8,128)S(1)}, u32[]{:S(2)}) copy-start(f32[2,1024,128,8]{2,1,3,0:T(8,128)S(1)} %get-tuple-element.584) | copy-start | bytes 25165828
  50.1 2.1 copy-start.8
  58.3 2.0 copy-start.2
  68.4 10.0 %copy-start.12 = (u32[32]{0:T(128)S(1)}, u32[32]{0:T(128)}, u32[]{:S(2)}) copy-start(u32[32]{0:T(128)} %constant.183) | copy-start | bytes 388
  69.6 212.0 %all-gather.9.cloned.1.call-start = ((), (), s32[]{:S(2)}) async-start(), calls=%async_computation.6 | async-start | bytes 18874368 | tf_op jit(solution)/shard_map/all_gather | solution.py:20
  191.5 6.2 %copy-start.4 = (bf16[128,256]{1,0:T(8,128)(2,1)S(1)}, bf16[128,256]{1,0:T(8,128)(2,1)}, u32[]{:S(2)}) copy-start(bf16[128,256]{1,0:T(8,128)(2,1)} %param.21) | copy-start | bytes 196612
  191.5 186.8 %reduce-scatter.6.cloned.1.call-start = ((), (), s32[]{:S(2)}) async-start(), calls=%async_computation.4 | async-start | bytes 81920 | tf_op jit(solution)/shard_map/reduce_scatter | solution.py:321
  225.2 163.2 %reduce-scatter.8.cloned.1.call-start = ((), (), s32[]{:S(2)}) async-start(), calls=%async_computation.5 | async-start | bytes 81920 | tf_op jit(solution)/shard_map/reduce_scatter | solution.py:324
  365.9 7.0 %copy-start.3 = (f32[64,128,64]{1,2,0:T(8,128)S(1)}, f32[64,128,64]{1,2,0:T(8,128)}, u32[]{:S(2)}) copy-start(f32[64,128,64]{1,2,0:T(8,128)} %fusion.17) | copy-start | bytes 6291460
Sparse Core Ops, SparseCore 0:
  17.0 92.6 all-gather.10
  113.4 35.5 reduce-scatter.3
  191.6 89.9 all-gather.8
  284.3 15.4 reduce-scatter.5
  373.0 15.3 reduce-scatter.7
where the time goes:
time: 402 us; the launch traced here: 395 us
  other arithmetic  98.7 us (25%)
  waiting for transfers between devices  80.9 us (20%)
  matrix products  60.9 us (15%)
  loops' own time  59 us (15%)
  blocking collectives  49.6 us (12%)
  local copies, waits for them, and re-layouts  31.2 us (8%)
  between operations  14.2 us (4%)
    select_n x16, other arithmetic, hop(): return jax.tree.map(lambda a, b: jnp.where(reached, a, b), new, before)  92.8 us
    all_gather x2, waiting for transfers between devices, prefix(): lax.all_gather(part.astype(kind), axis)  70.7 us
    another operation x2, loops' own time, prefix(): return lax.fori_loop(0, devices, hop, start)  59 us
    unnamed x41, local copies, waits for them, and re-layouts  15.7 us
    unnamed x1, blocking collectives  11.8 us
    all_gather x1, blocking collectives, body(): key_all = lax.all_gather(keys_in, 'ctx', axis=0, tiled=True)  11.7 us
    dynamic_slice x16, local copies, waits for them, and re-layouts, hop(): part[at].astype(own.dtype)  10.1 us
    reduce_scatter x1, waiting for transfers between devices, body(): lax.psum_scatter(read_terms.astype(jnp.bfloat16), 'head', scatter_dimensi...  10.1 us
  transfers between devices with their start and end apart: 5, of which 3 were waited for; matrix products, arithmetic and copies ran while one was open for 45% of the time, Pallas kernels for 0%

commit v1 on v0

v1 whole, which is shorter than its diff:
```python
import jax
import jax.numpy as jnp
from jax import lax
from jax.experimental import pallas as pl
from jax.experimental.pallas import tpu as pltpu
from jax.sharding import PartitionSpec as P

HD = 128
P_SIZE = 64
N = 256
AUX = 16
GROUP = 8
WIDTH = GROUP * P_SIZE
FLOOR = -1e30
F32 = jnp.float32
BF16 = jnp.bfloat16
highest = lax.Precision.HIGHEST
BRIEF = pl.CostEstimate(flops=1, bytes_accessed=1, transcendentals=0)


SCALAR = pl.BlockSpec(memory_space=pltpu.SMEM)
WHOLE = pl.BlockSpec(memory_space=pltpu.VMEM)
ANYWHERE = pl.BlockSpec(memory_space=pl.ANY)


def dot(a, b):
    return jnp.dot(a, b, preferred_element_type=F32)


def dot_nt(a, b):
    return lax.dot_general(a, b, (((1,), (1,)), ((), ())), preferred_element_type=F32)


def flip(a):
    return a.astype(F32).T.astype(BF16)


def running_decay(ld):
    rows = ld.shape[1]
    upper = lax.broadcasted_iota(jnp.int32, (rows, rows), 0) <= lax.broadcasted_iota(
        jnp.int32, (rows, rows), 1
    )
    return jnp.dot(ld, upper.astype(F32), preferred_element_type=F32, precision=highest)


def doc_row_col(doc_ref):
    row = doc_ref[...].astype(F32) + 1.0
    rows = row.shape[1]
    grid = jnp.broadcast_to(row, (rows, rows))
    return row, grid.T


def split(value):
    high = value.astype(BF16)
    return high, (value - high.astype(F32)).astype(BF16)


def spread(heads, first_head):
    row = lax.broadcasted_iota(jnp.int32, (heads, WIDTH), 0)
    col = lax.broadcasted_iota(jnp.int32, (heads, WIDTH), 1)
    return (lax.shift_right_logical(col, 6) + first_head == row).astype(F32).astype(BF16)


def params(mib):
    return pltpu.CompilerParams(vmem_limit_bytes=mib * 1024 * 1024)


def aux_block(decay, leaving, far):
    high, low = split(decay)
    place = lax.broadcasted_iota(jnp.int32, (AUX, decay.shape[1]), 0)
    wide = jnp.where(place == 0, high.astype(F32), low.astype(F32))
    return jnp.where(
        place < 2, wide, jnp.where(place == 2, leaving, jnp.where(place == 3, far, 0.0))
    ).astype(BF16)


def aux_rows(part):
    part = part.astype(F32)
    return part[0:1] + part[1:2], part[2:3], part[3:4]


def states_kernel(kind, x, dy, b, c, ld, doc, *refs):
    keys, values, out, packet = refs[:4] if len(refs) > 6 else (None, None, refs[0], None)
    z_in, side, ld_in, doc_in, sems = refs[-5:]
    heads = ld.shape[0]
    cols = out.shape[1]
    forward = kind[0] == 0
    part = min(cols, 2 * WIDTH)

    def copies(z, matrix):
        yield pltpu.make_async_copy(matrix, side, sems.at[2])
        for k in range(cols // part):
            to = pl.ds(k * part, part)
            source = z.at[:, pl.ds(k * part, part)]
            yield pltpu.make_async_copy(source, z_in.at[:, to], sems.at[3 + k])

    small = [
        pltpu.make_async_copy(ld, ld_in, sems.at[0]),
        pltpu.make_async_copy(doc, doc_in, sems.at[1]),
    ]
    for copy in small:
        copy.start()
    if packet is not None:
        rows, width = keys.shape
        moves = [
            pltpu.make_async_copy(part, packet.at[pl.ds(0, rows), pl.ds(k * width, width)], sem)
            for k, (part, sem) in enumerate(((keys, sems.at[sems.shape[0] - 2]), (values, sems.at[sems.shape[0] - 1])))
        ]
        for copy in moves:
            copy.start()

    @pl.when(forward)
    def _():
        for copy in copies(x, b):
            copy.start()

    @pl.when(jnp.logical_not(forward))
    def _():
        for copy in copies(dy, c):
            copy.start()

    large = list(copies(x, b))
    for copy in small:
        copy.wait()
    row, col = doc_row_col(doc_in)
    first = jnp.min(row, axis=1, keepdims=True)
    last = jnp.max(row, axis=1, keepdims=True)
    leaving, far = jnp.where(forward, last, first), jnp.where(forward, first, last)
    cum = running_decay(ld_in[...]).T
    end = cum[-1:, :]
    gap = jnp.where(forward, end - cum, cum)
    weight = jnp.where(col[:, :heads] == leaving, jnp.exp(gap), 0.0).astype(BF16)
    high, low = split(jnp.exp(jnp.broadcast_to(end, (8, heads))))
    large[0].wait()
    turned = flip(side[...])
    for t in range(cols // WIDTH):
        if t * WIDTH % part == 0:
            large[1 + t * WIDTH // part].wait()
        at = slice(t * WIDTH, (t + 1) * WIDTH)
        e = spread(heads, t * GROUP)
        z = (z_in[:, at].astype(F32) * dot(weight, e)).astype(BF16)
        out[:N, at] = dot(turned, z).astype(BF16)
        decay = dot(high, e) + dot(low, e)
        out[N:, at] = aux_block(decay[0:1], leaving, far)
    if packet is not None:
        for copy in moves:
            copy.wait()
        docs = jnp.concatenate([row] * (2 * width // rows), axis=1)
        packet[rows:, :] = jnp.broadcast_to(docs, (AUX, 2 * width)).astype(BF16)


def states(kind, x, dy, b, c, ld, doc, kv=()):
    rows, cols = x.shape
    heads = ld.shape[0]
    hbm = pl.BlockSpec(memory_space=pltpu.HBM)
    whole = lambda a: pl.BlockSpec(a.shape, lambda j, s: (0,) * a.ndim)
    shapes = [jax.ShapeDtypeStruct((N + AUX, cols), BF16)]
    if kv:
        shapes.append(jax.ShapeDtypeStruct((rows + AUX, 2 * kv[0].shape[1]), BF16))

    return pl.pallas_call(
        states_kernel,
        grid_spec=pltpu.PrefetchScalarGridSpec(
            num_scalar_prefetch=1,
            grid=(1,),
            in_specs=[hbm] * (6 + len(kv)),
            out_specs=[whole(a) for a in shapes],
            scratch_shapes=[
                pltpu.VMEM((rows, cols), BF16),
                pltpu.VMEM((rows, N), BF16),
                pltpu.VMEM((heads, rows), F32),
                pltpu.VMEM((1, rows), jnp.int32),
                pltpu.SemaphoreType.DMA((5 + max(1, cols // (2 * WIDTH)),)),
            ],
        ),
        out_shape=shapes,
        compiler_params=params(10),
        cost_estimate=BRIEF,
        name="chunk_states",
    )(kind, x, dy, b, c, ld, doc, *kv)


def merge_kernel(mine, got, out, low):
    cols = out.shape[2]
    for t in range(2 * cols // WIDTH):
        at = slice(t * WIDTH, (t + 1) * WIDTH)
        half, first = t * WIDTH // cols, t * WIDTH // cols * cols
        to = slice(t * WIDTH - first, (t + 1) * WIDTH - first)
        decay, leaving, far = aux_rows(mine[N:, at])
        decay_got, leaving_got, far_got = aux_rows(got[N:, at])
        linked = (leaving_got == far_got) & (leaving == far_got)
        total = jnp.where(linked, decay_got, 0.0) * mine[:N, at].astype(F32)
        total = (got[:N, at].astype(F32) + total).astype(BF16)
        aux = aux_block(decay * decay_got, leaving_got, far)
        out[half, :N, to] = total
        out[half, N:, to] = aux
        if half == 0:
            low[:N, to] = total
            low[N:, to] = aux


def merge(mine, got):
    rows, cols = mine.shape
    return pl.pallas_call(
        merge_kernel,
        out_shape=[
            jax.ShapeDtypeStruct((2, rows, cols // 2), BF16),
            jax.ShapeDtypeStruct((rows, cols // 2), BF16),
        ],
        compiler_params=params(4),
        cost_estimate=BRIEF,
        name="pair_merge",
    )(mine, got)


def carry_kernel(half, mine, near, extra, *refs):
    (relay, *others), (keep, out, send, sems) = refs[:-4], refs[-4:]
    cols = keep.shape[1]
    span, copies = min(cols, 2 * WIDTH), []
    for t in range(cols // WIDTH):
        at = slice(t * WIDTH, (t + 1) * WIDTH)
        own = slice(half * cols + t * WIDTH, half * cols + (t + 1) * WIDTH)
        here = near[half, :, at].astype(F32) + extra[:, at].astype(F32)
        total, coefficient, now = here[:N], None, aux_rows(here[N:])
        entering = now[1]
        for k, part in enumerate(others):
            there = part[half, :, at].astype(F32)
            if k == 0:
                there = there + relay[half, :, at].astype(F32)
            after = aux_rows(there[N:])
            step = jnp.where((now[1] == now[2]) & (after[1] == now[2]), now[0], 0.0)
            coefficient = step if coefficient is None else coefficient * step
            total = total + coefficient * there[:N]
            now = after
        decay, leaving, far = aux_rows(mine[N:, own])
        linked = (leaving == far) & (entering == far)
        passed = mine[:N, own].astype(F32) + jnp.where(linked, decay, 0.0) * total
        keep[:N, at] = total.astype(BF16)
        keep[N:, at] = aux_block(jnp.zeros_like(decay), entering, entering)
        send[:N, at] = passed.astype(BF16)
        send[N:, at] = aux_block(jnp.zeros_like(decay), leaving, leaving)
        if (t + 1) * WIDTH % span == 0:
            n = (t + 1) * WIDTH // span - 1
            piece = (slice(None), pl.ds(n * span, span))
            copies.append(pltpu.make_async_copy(send.at[piece], out.at[piece], sems.at[n]))
            copies[-1].start()
    for copy in copies:
        copy.wait()


def carries(half, mine, near, extra, others):
    out = pltpu.VMEM(extra.shape, BF16)

    def kernel(*refs):
        carry_kernel(half, *refs)

    return pl.pallas_call(
        kernel,
        in_specs=[WHOLE] * (3 + len(others)),
        out_specs=[WHOLE, ANYWHERE],
        out_shape=[out, jax.ShapeDtypeStruct(extra.shape, BF16)],
        scratch_shapes=[pltpu.VMEM(extra.shape, BF16), pltpu.SemaphoreType.DMA((4,))],
        compiler_params=params(6),
        cost_estimate=BRIEF,
        name="carry_states",
    )(mine, near, extra, *others)


def inside_kernel(
    x, dy, b, c, ld, doc, y, dx, acc, decays, cum_col, cum_row, gram, gram_t, veil, veil_t, total
):
    j = pl.program_id(0)
    heads, rows = ld.shape
    here = x.shape[1] // P_SIZE

    @pl.when(j == 0)
    def _():
        across_tokens = running_decay(ld[...])
        cum_row[...] = across_tokens
        cum = across_tokens.T
        for k in range(heads // here):
            cum_col[k] = cum[:, k * here : (k + 1) * here]
        row, col = doc_row_col(doc)
        decays[0] = jnp.exp(cum)
        decays[1] = jnp.exp(cum[-1:, :] - cum)
        decays[2] = col[:, :heads]
        places = [lax.broadcasted_iota(jnp.int32, (rows, rows), k) for k in range(2)]
        same = col == row
        veil[...] = jnp.where(same & (places[0] >= places[1]), 0.0, FLOOR)
        veil_t[...] = jnp.where(same & (places[0] <= places[1]), 0.0, FLOOR)
        gram[...] = dot_nt(c[...], b[...])
        gram_t[...] = dot_nt(b[...], c[...])
        total[...] = jnp.zeros_like(total)

    lane = lax.broadcasted_iota(jnp.int32, (1, 2 * P_SIZE), 1)
    left = (lane < P_SIZE).astype(F32).astype(BF16)
    right = (lane >= P_SIZE).astype(F32).astype(BF16)
    col_block = cum_col[j]
    row_block = cum_row[pl.ds(pl.multiple_of(j * here, here), here), :]
    for pair in range(here // 2):
        at = slice(pair * 2 * P_SIZE, (pair + 1) * 2 * P_SIZE)
        x_pair, y_pair = x[:, at], dy[:, at]
        x_both = jnp.concatenate([x_pair * left, x_pair * right], axis=0)
        y_both = jnp.concatenate([y_pair * left, y_pair * right], axis=0)
        inner = dot_nt(y_both, x_pair)
        mixed, turned, sums = [], [], 0.0
        for k in range(2):
            head = 2 * pair + k
            gap = col_block[:, head : head + 1] - row_block[head : head + 1, :]
            decay = jnp.exp(gap + veil[...])
            sums = sums + decay * inner[k * rows : (k + 1) * rows]
            mixed.append((decay * gram[...]).astype(BF16))
            turned.append((jnp.exp(veil_t[...] - gap) * gram_t[...]).astype(BF16))
        total[...] += sums
        y[:, at] = dot(jnp.concatenate(mixed, axis=1), x_both).astype(BF16)
        dx[:, at] = dot(jnp.concatenate(turned, axis=1), y_both).astype(BF16)

    @pl.when(j == pl.num_programs(0) - 1)
    def _():
        weighted = total[...]
        acc[0] = dot(weighted.T.astype(BF16), c[...])
        acc[1] = dot(weighted.astype(BF16), b[...])


def inside(x, dy, b, c, ld, doc):
    rows, cols = x.shape
    heads = ld.shape[0]
    span = min(cols, 4 * WIDTH)
    here = span // P_SIZE
    whole = lambda a: pl.BlockSpec(a.shape, lambda j: (0,) * a.ndim)
    block = pl.BlockSpec((rows, span), lambda j: (0, j))
    shapes = [
        jax.ShapeDtypeStruct((rows, cols), BF16),
        jax.ShapeDtypeStruct((rows, cols), BF16),
        jax.ShapeDtypeStruct((2, rows, N), F32),
        jax.ShapeDtypeStruct((3, rows, heads), F32),
    ]
    square = pltpu.VMEM((rows, rows), F32)
    return pl.pallas_call(
        inside_kernel,
        grid=(cols // span,),
        in_specs=[block, block, whole(b), whole(c), whole(ld), whole(doc)],
        out_specs=[block, block, whole(shapes[2]), whole(shapes[3])],
        out_shape=shapes,
        scratch_shapes=[
            pltpu.VMEM((heads // here, rows, here), F32),
            pltpu.VMEM((heads, rows), F32),
            *[square] * 5,
        ],
        compiler_params=params(10),
        cost_estimate=BRIEF,
        name="inside_chunk",
    )(x, dy, b, c, ld, doc)


def carried_weight(forward, carried, decays):
    doc = carried[N:, :HD].astype(F32)[2:3, 0:1]
    decay = jnp.where(forward, decays[0], decays[1])
    return jnp.where(decays[2] == doc, decay, 0.0).astype(BF16)


def sums_kernel(half, ranks, kind, side, x, dy, decays, carried, acc_in, *refs):
    heads = decays.shape[2]
    cols = carried.shape[1]
    forward = kind[0] == 0
    weight = carried_weight(forward, carried, decays)
    total = 0.0
    for t in range(cols // WIDTH):
        at = slice(t * WIDTH, (t + 1) * WIDTH)
        to = slice(half * cols + t * WIDTH, half * cols + (t + 1) * WIDTH)
        e = spread(heads, half * (heads // 2) + t * GROUP)
        z = jnp.where(forward, dy[:, to], x[:, to]).astype(F32)
        total = total + dot_nt((z * dot(weight, e)).astype(BF16), carried[:N, at])
    acc = refs[-1]
    acc[0] = acc_in[0] + jnp.where(forward, 0.0, total)
    acc[1] = acc_in[1] + jnp.where(forward, total, 0.0)
    if ranks > 1:
        divide(side, acc, *refs[:2])


def divide(side, acc, kept, away):
    rows = kept.shape[1]
    kept[...] = acc[:, pl.ds(pl.multiple_of(side[0] * rows, rows), rows), :]
    away[...] = acc[:, pl.ds(pl.multiple_of((1 - side[0]) * rows, rows), rows), :].astype(BF16)


def halves(acc):
    shape = (acc.shape[0], acc.shape[1] // 2, acc.shape[2])
    return [jax.ShapeDtypeStruct(shape, F32), jax.ShapeDtypeStruct(shape, BF16)]


def across_sums(half, kind, x, dy, decays, carried, acc, side=None):
    last = side is not None

    def kernel(*refs):
        sums_kernel(half, 2 if last else 1, *refs)

    return pl.pallas_call(
        kernel,
        in_specs=[SCALAR, SCALAR] + [WHOLE] * 5,
        out_specs=[WHOLE, WHOLE] if last else WHOLE,
        out_shape=halves(acc) if last else jax.ShapeDtypeStruct(acc.shape, F32),
        scratch_shapes=[pltpu.VMEM(acc.shape, F32)] if last else [],
        compiler_params=params(4),
        cost_estimate=BRIEF,
        name="across_sums",
    )(kind, side if last else kind, x, dy, decays, carried, acc)


def fetch_given(sources, buffer, sems):
    part = min(sources[0].shape[1], 2 * WIDTH)
    waits, place = [], 0
    for source in sources:
        for first in range(0, source.shape[1], part):
            piece = source.at[:, pl.ds(first, part)]
            target = buffer.at[:, pl.ds(place, part)]
            waits.append(pltpu.make_async_copy(piece, target, sems.at[place // part]))
            waits[-1].start()
            place += part
    return waits, part


def given_kernel(kind, side, x, dy, decays, acc_in, low, high, kept, away, acc, carried, sems):
    heads = decays.shape[2]
    forward = kind[0] == 0
    waits, part = fetch_given((low, high), carried, sems)
    total = 0.0
    for t in range(carried.shape[1] // WIDTH):
        if t * WIDTH % part == 0:
            waits[t * WIDTH // part].wait()
        if t == 0:
            weight = carried_weight(forward, carried, decays)
        at = slice(t * WIDTH, (t + 1) * WIDTH)
        z = jnp.where(forward, dy[:, at], x[:, at]).astype(F32)
        z = (z * dot(weight, spread(heads, t * GROUP))).astype(BF16)
        total = total + dot_nt(z, carried[:N, at])
    acc[0] = acc_in[0] + jnp.where(forward, 0.0, total)
    acc[1] = acc_in[1] + jnp.where(forward, total, 0.0)
    divide(side, acc, kept, away)


def given_sums(kind, side, x, dy, decays, low, high, acc):
    return pl.pallas_call(
        given_kernel,
        in_specs=[SCALAR, SCALAR] + [WHOLE] * 4 + [ANYWHERE] * 2,
        out_specs=[WHOLE, WHOLE],
        out_shape=halves(acc),
        scratch_shapes=[
            pltpu.VMEM(acc.shape, F32),
            pltpu.VMEM((low.shape[0], 2 * low.shape[1]), BF16),
            pltpu.SemaphoreType.DMA((8,)),
        ],
        compiler_params=params(8),
        cost_estimate=BRIEF,
        name="given_sums",
    )(kind, side, x, dy, decays, acc, low, high)


def fold_kernel(side, kept_in, moved, kept, away, acc):
    acc[...] = kept_in[...] + moved[...].astype(F32)
    divide(side, acc, kept, away)


def fold(side, kept, moved):
    return pl.pallas_call(
        fold_kernel,
        in_specs=[SCALAR, WHOLE, WHOLE],
        out_specs=[WHOLE, WHOLE],
        out_shape=halves(kept),
        scratch_shapes=[pltpu.VMEM(kept.shape, F32)],
        compiler_params=params(2),
        cost_estimate=BRIEF,
        name="sums_fold",
    )(side, kept, moved)


def outputs_kernel(half, wanted, core, b, c, decays, keep, source, y_in, dx_in, *refs):
    outs, (buffer, sems, given, arrivals) = refs[-4 - len(wanted) : -4], refs[-4:]
    waits, piece = fetch_given((source,), given, arrivals)
    heads = decays.shape[2]
    cols = keep.shape[1]
    lower = core[0] == 0
    part = min(cols, 2 * WIDTH)
    copies, weights = [], {}
    for t in range(cols // WIDTH):
        if t * WIDTH % piece == 0:
            waits[t * WIDTH // piece].wait()
        at = slice(t * WIDTH, (t + 1) * WIDTH)
        to = slice(half * cols + t * WIDTH, half * cols + (t + 1) * WIDTH)
        e = spread(heads, half * (heads // 2) + t * GROUP)
        for out, name in zip(outs, wanted):
            k = "yx".index(name)
            carried = (keep, given) if k == 0 else (given, keep)
            side, old, decay = ((c, y_in, decays[0]), (b, dx_in, decays[1]))[k]
            if t == 0:
                docs = [part_of[N:, :HD].astype(F32)[2:3, 0:1] for part_of in carried]
                doc = jnp.where(lower, docs[0], docs[1])
                weights[k] = jnp.where(decays[2] == doc, decay, 0.0).astype(BF16)
            state = jnp.where(lower, carried[0][:N, at], carried[1][:N, at])
            term = dot(weights[k], e) * dot(side[...], state)
            buffer[k, :, at] = (old[:, to].astype(F32) + term).astype(BF16)
            if (t + 1) * WIDTH % part == 0:
                n = (t + 1) * WIDTH // part - 1
                source_part = buffer.at[k, :, pl.ds(n * part, part)]
                target = out.at[:, pl.ds(half * cols + n * part, part)]
                copies.append(pltpu.make_async_copy(source_part, target, sems.at[k, n]))
                copies[-1].start()
    for copy in copies:
        copy.wait()


def across_outputs(half, wanted, core, b, c, decays, keep, given, y, dx, done=()):
    rows, cols = y.shape
    parts = max(1, cols // 2 // (2 * WIDTH))
    anywhere = pl.BlockSpec(memory_space=pl.ANY)

    def kernel(*refs):
        outputs_kernel(half, wanted, *refs)

    return pl.pallas_call(
        kernel,
        in_specs=[SCALAR] + [WHOLE] * 4 + [ANYWHERE] + [WHOLE] * 2 + [anywhere for _ in done],
        out_specs=[anywhere for _ in wanted],
        out_shape=[jax.ShapeDtypeStruct(y.shape, BF16) for _ in wanted],
        scratch_shapes=[
            pltpu.VMEM((2, rows, cols // 2), BF16),
            pltpu.SemaphoreType.DMA((2, parts)),
            pltpu.VMEM(given.shape, BF16),
            pltpu.SemaphoreType.DMA((4,)),
        ],
        input_output_aliases={8 + k: k for k in range(len(done))},
        compiler_params=params(8),
        cost_estimate=BRIEF,
        name="across_outputs",
    )(core, b, c, decays, keep, given, y, dx, *done)


def partner_kernel(other, upper, *refs):
    parts, out = refs[:-1], refs[-1]
    out[...] = (
        sum(part[pl.ds(other[0], 1)][0].astype(F32) for part in parts) + upper[...].astype(F32)
    ).astype(BF16)


def partner_part(other, upper, parts):
    return pl.pallas_call(
        partner_kernel,
        in_specs=[SCALAR] + [WHOLE] * (1 + len(parts)),
        out_specs=WHOLE,
        out_shape=jax.ShapeDtypeStruct(upper.shape, BF16),
        compiler_params=params(2),
        cost_estimate=BRIEF,
        name="partner_part",
    )(other, upper, *parts)


def finish_kernel(core, own, swapped, kept, moved, *refs):
    parts, (grad_k, grad_v, grad_b, grad_c) = refs[:-4], refs[-4:]
    cols = grad_k.shape[1]
    total = own[...] + swapped[...].astype(F32)
    total = total + sum(part[pl.ds(core[0], 1)][0].astype(F32) for part in parts)
    grad_k[...] = total[:, :cols].astype(BF16)
    grad_v[...] = total[:, cols:].astype(BF16)
    grad_b[...] = (kept[0] + moved[0].astype(F32)).astype(BF16)
    grad_c[...] = (kept[1] + moved[1].astype(F32)).astype(BF16)


def finish(core, own, swapped, kept, moved, parts):
    rows, cols = own.shape
    key = jax.ShapeDtypeStruct((rows, cols // 2), BF16)
    shared = jax.ShapeDtypeStruct(kept.shape[1:], BF16)
    return pl.pallas_call(
        finish_kernel,
        in_specs=[SCALAR] + [WHOLE] * (4 + len(parts)),
        out_shape=[key, key, shared, shared],
        compiler_params=params(2),
        cost_estimate=BRIEF,
        name="last_sums",
    )(core, own, swapped, kept, moved, *parts)


def key_blocks(lower, packet, partner, far, other, reach):
    blocks = [packet[...]]
    for k in range(1, reach + 1):
        if k % 2 == 0:
            blocks.append(far[k // 2 - 1][...])
        else:
            up = partner if k == 1 else other[k // 2 - 1]
            blocks.append(jnp.where(lower, other[k // 2][...], up[...]))
    return blocks


def attention_kernel(reach, group, kv_local, core, q, do, doc, packet, partner, *refs):
    count = len(refs) - 6 - 5
    far, other = refs[: count // 2], refs[count // 2 : count]
    o, dq, own, hold, send, upper = refs[count : count + 6]
    keys, values, veil, probs, grads = refs[count + 6 :]
    lower = core[0] == 0
    rows = q.shape[0]
    scale = HD ** (-0.5)
    row, _ = doc_row_col(doc)
    packets = key_blocks(lower, packet, partner, far, other, reach)
    for k, block in enumerate(packets):
        at = slice(k * rows, (k + 1) * rows)
        key_row = block[rows:, :HD].astype(F32)[0:1, :]
        seen = jnp.broadcast_to(key_row, (rows, rows)).T == row
        if k == 0:
            seen = seen & (
                lax.broadcasted_iota(jnp.int32, (rows, rows), 0)
                <= lax.broadcasted_iota(jnp.int32, (rows, rows), 1)
            )
        veil[at, :] = jnp.where(seen, 0.0, FLOOR)
        for g in range(kv_local):
            keys[g, at, :] = block[:rows, g * HD : (g + 1) * HD]
            values[g, at, :] = block[:rows, (kv_local + g) * HD : (kv_local + g + 1) * HD]
    for g in range(kv_local):
        k_all, v_all = keys[g], values[g]
        k_turned, v_turned = flip(k_all), flip(v_all)
        dk = dv = 0.0
        for h in range(0, group, 2):
            ats = [slice((g * group + h + i) * HD, (g * group + h + i + 1) * HD) for i in range(2)]
            q_two = jnp.concatenate([q[:, at] for at in ats], axis=0)
            do_two = jnp.concatenate([do[:, at] for at in ats], axis=0)
            do_turned = do_two.astype(F32).T
            mask = jnp.concatenate([veil[...]] * 2, axis=1)
            scores = dot(k_all, flip(q_two)) * scale + mask
            top = jnp.max(scores, axis=0, keepdims=True)
            weights = jnp.exp(scores - top)
            over = 1.0 / jnp.sum(weights, axis=0, keepdims=True)
            out = (dot(v_turned, weights.astype(BF16)) * over).astype(BF16).astype(F32)
            inner = jnp.sum(do_turned * out, axis=0, keepdims=True)
            prob = weights * over
            prob_grad = dot(v_all, do_turned.astype(BF16))
            dscore = (prob * (prob_grad - inner)).astype(BF16)
            probs[...] = prob.astype(BF16)
            grads[...] = dscore
            dq_turned = dot(k_turned, dscore) * scale
            for i, at in enumerate(ats):
                o[:, at] = out[:, i * rows : (i + 1) * rows].T.astype(BF16)
                dq[:, at] = dq_turned[:, i * rows : (i + 1) * rows].T.astype(BF16)
            dk = dk + dot(grads[...], q_two)
            dv = dv + dot(probs[...], do_two)
        for part, col in ((dk * scale, g), (dv, kv_local + g)):
            cols = slice(col * HD, (col + 1) * HD)
            own[:, cols] = part[:rows]

            def of(k):
                return part[k * rows : (k + 1) * rows] if k <= reach else jnp.zeros((rows, HD), F32)

            upper[:, cols] = jnp.where(lower, 0.0, of(1)).astype(BF16)
            for m in range(reach // 4):
                odd, even = 2 * m + 1, 2 * m + 2
                for place in range(2):
                    low_odd, up_odd = of(2 * odd - place), of(2 * odd + 1 - place)
                    low_even, up_even = of(2 * even - place), of(2 * even + 1 - place)
                    hold[m, place, :, cols] = jnp.where(lower, low_odd, up_even).astype(BF16)
                    send[m, place, :, cols] = jnp.where(lower, low_even, up_odd).astype(BF16)


def attention(core, q, do, doc, packet, partner, far, other, reach):
    rows, cols = q.shape
    kv_cols = packet.shape[1]
    kv_local = kv_cols // (2 * HD)
    group = cols // (kv_local * HD)
    blocks = reach + 1
    args = (q, do, doc, packet, partner, *far, *other)

    def kernel(*refs):
        attention_kernel(reach, group, kv_local, *refs)

    whole = lambda a: pl.BlockSpec(a.shape, lambda j, s: (0,) * a.ndim)
    shapes = [
        jax.ShapeDtypeStruct((rows, cols), BF16),
        jax.ShapeDtypeStruct((rows, cols), BF16),
        jax.ShapeDtypeStruct((rows, kv_cols), F32),
        jax.ShapeDtypeStruct((reach // 4, 2, rows, kv_cols), BF16),
        jax.ShapeDtypeStruct((reach // 4, 2, rows, kv_cols), BF16),
        jax.ShapeDtypeStruct((rows, kv_cols), BF16),
    ]
    return pl.pallas_call(
        kernel,
        grid_spec=pltpu.PrefetchScalarGridSpec(
            num_scalar_prefetch=1,
            grid=(1,),
            in_specs=[whole(a) for a in args],
            out_specs=[whole(a) for a in shapes],
            scratch_shapes=[
                pltpu.VMEM((kv_local, blocks * rows, HD), BF16),
                pltpu.VMEM((kv_local, blocks * rows, HD), BF16),
                pltpu.VMEM((blocks * rows, rows), F32),
                pltpu.VMEM((blocks * rows, 2 * rows), BF16),
                pltpu.VMEM((blocks * rows, 2 * rows), BF16),
            ],
        ),
        out_shape=shapes,
        compiler_params=params(14),
        cost_estimate=BRIEF,
        name="packed_attention",
    )(core, *args)


def shift(x, axis, by):
    count = lax.axis_size(axis)
    hops = [(i, i + by) for i in range(count) if 0 <= i + by < count]
    return lax.ppermute(x, axis, hops)


def swap(x):
    count = lax.axis_size("ctx")
    return lax.ppermute(x, "ctx", [(i, i ^ 1) for i in range(count)])


def onward(x, route):
    pairs = lax.axis_size("ctx") // 2
    hops = [(2 * p + c, 2 * route(p, c) + c) for p in range(pairs) for c in range(2)]
    return lax.ppermute(x, "ctx", [(i, k) for i, k in hops if 0 <= k < 2 * pairs])


NOWHERE = -1


def ahead(by):
    return lambda p, c: p + by * (1 - 2 * c)


def ahead_in_row(p, c):
    return ahead(1)(p, c) if p % 2 == c else NOWHERE


def ahead_to_relay(p, c):
    return ahead(2)(p, c) if p % 2 != c else NOWHERE


def ahead_direct(p, c):
    return ahead(2)(p, c) if p % 2 == c else NOWHERE


def ahead_across(p, c):
    return ahead(1)(p, c) if p % 2 != c else NOWHERE


def ahead_by_relay(pairs):
    def route(p, c):
        source = p - 2 * (1 - 2 * c)
        relayed = p % 2 != c and 0 <= source < pairs
        return p - (1 - 2 * c) if relayed else NOWHERE

    return route


def body(
    queries,
    keys_in,
    values_in,
    attn_cotan,
    doc_ids,
    ssd_input,
    state_write,
    state_read,
    log_decay,
    ssd_cotan,
):
    rows = doc_ids.shape[0]
    kv_cols = keys_in.shape[1]
    devices = lax.axis_size("ctx")
    pairs = devices // 2
    hops = pairs // 2
    reach = 2 * hops
    doc = doc_ids.reshape(1, rows)
    core = lax.rem(lax.axis_index("ctx"), 2).astype(jnp.int32).reshape(1)
    other = 1 - core

    args = (ssd_input, ssd_cotan, state_write, state_read, log_decay.T, doc)
    pinned = [pltpu.with_memory_space_constraint(a, pltpu.HBM) for a in args]
    kv = [pltpu.with_memory_space_constraint(a, pltpu.HBM) for a in (keys_in, values_in)]
    sent, packet = states(other, *pinned, kv=kv)
    got = swap(sent)
    (mine,) = states(core, *pinned)
    far = [shift(packet, "ctx", 2 * k) for k in range(1, hops + 1)]
    far, mine = lax.optimization_barrier((far, mine))
    pair, low = merge(mine, got)
    near = onward(pair, ahead_in_row)
    to_relay = onward(pair, ahead_to_relay)
    others = [onward(pair, ahead_direct)]
    others += [onward(pair, ahead(k)) for k in range(3, hops + 1)]
    partner = swap(packet)
    far_other = [swap(part) for part in far]

    _, doc_then = lax.optimization_barrier((pair, doc))
    y, dx, acc, decays = inside(*args[:5], doc_then)
    _, core_then = lax.optimization_barrier((acc, core))
    attn_out, grad_q, own, hold, send, upper = attention(
        core_then, queries, attn_cotan, doc, packet, partner, far, far_other, reach
    )
    low, own = lax.optimization_barrier((low, own))
    straight = onward(low, ahead_across)
    relayed = onward(to_relay[1], ahead_by_relay(pairs))
    hold = (hold.astype(F32) + swap(send).astype(F32)).astype(BF16)

    mine, near, straight, relayed, to_relay, others, acc, hold = lax.optimization_barrier(
        (mine, near, straight, relayed, to_relay, others, acc, hold)
    )
    others = [to_relay, *others]
    back = [onward(hold[m], lambda p, c: p - (2 * m + 1 + c)) for m in range(hops // 2)]
    keep_low, give_low = carries(0, mine, near, straight, others)
    keep, give = carries(1, mine, near, relayed, others)
    given_low, given = swap(give_low), swap(give)
    acc = across_sums(0, core, ssd_input, ssd_cotan, decays, keep_low, acc)
    acc = across_sums(1, core, ssd_input, ssd_cotan, decays, keep, acc)

    def outputs(half, after, keep, given, done=()):
        _, core_then = lax.optimization_barrier((after, core))
        return across_outputs(
            half, "yx", core_then, state_write, state_read, decays, keep, given, y, dx, done
        )

    position = lax.axis_index("head").astype(jnp.int32)
    ranks = lax.axis_size("head")

    def side_at(step):
        return lax.rem(position // step, 2).reshape(1)

    step = ranks // 2
    kept, away = given_sums(
        other, side_at(step), ssd_input, ssd_cotan, decays, given_low, given, acc
    )
    done = ()
    for half in range(ranks.bit_length() - 1):
        moved = lax.ppermute(away, "head", [(i, i ^ step) for i in range(ranks)])
        if half < 2:
            states_of = ((keep_low, given_low), (keep, given))[half]
            done = outputs(half, kept, *states_of, done)
            moved, done, back = lax.optimization_barrier((moved, done, back))
            if half == 0:
                swapped = swap(partner_part(other, upper, back))
            else:
                moved, done, swapped = lax.optimization_barrier((moved, done, swapped))
        step //= 2
        if step:
            kept, away = fold(side_at(step), kept, moved)

    grads = finish(core, own, swapped, kept, moved, back)
    return (attn_out, done[0], grad_q, grads[0], grads[1], done[1], grads[2], grads[3])


def solution(mesh):
    tokens = P("ctx", "head")
    shared = P("ctx", None)
    in_specs = (
        tokens,
        tokens,
        tokens,
        tokens,
        P("ctx"),
        tokens,
        shared,
        shared,
        tokens,
        tokens,
    )
    out_specs = (tokens,) * 6 + (P(("ctx", "head"), None),) * 2
    return jax.shard_map(body, mesh=mesh, in_specs=in_specs, out_specs=out_specs, check_vma=False)
```

time: 402 us -> 89.3 us (0.22); the launches traced: 395 us -> 88.9 us
  other arithmetic: 98.7 us -> 0.79 us
  waiting for transfers between devices: 80.9 us -> 5.41 us
  matrix products: 60.9 us -> 0 us
  loops' own time: 59 us -> 0 us
  blocking collectives: 49.6 us -> 0 us
  starting transfers between devices: 0.46 us -> 38.2 us
  Pallas kernels: 0 us -> 37.7 us
  local copies, waits for them, and re-layouts: 31.2 us -> 5.82 us
  between operations: 14.2 us -> 1.02 us
    select_n x35 -> x0, other arithmetic: 93.2 us -> none  [the longest x16 92.8 us: hop(): return jax.tree.map(lambda a, b: jnp.where(reached, a, b), new, before)]
    all_gather x2 -> x0, waiting for transfers between devices: 70.7 us -> none  [prefix(): lax.all_gather(part.astype(kind), axis)]
    dot_general x18 -> x0, matrix products: 60.9 us -> none  [the longest x1 6.4 us: one_block(): jnp.einsum('kgts,tkgd->skd', prob_low, cotan_heads, preferred_element_typ...]
    another operation x2 -> x0, loops' own time: 59 us -> none  [prefix(): return lax.fori_loop(0, devices, hop, start)]
    ppermute x0 -> x18, starting transfers between devices: none -> 38.2 us  [the longest x8 18.4 us: swap(): return lax.ppermute(x, 'ctx', [(i, i ^ 1) for i in range(count)])]
    all_gather x4 -> x0, blocking collectives: 37.8 us -> none  [the longest x1 11.7 us: body(): key_all = lax.all_gather(keys_in, 'ctx', axis=0, tiled=True)]
    pallas_call x0 -> x15, Pallas kernels: none -> 37.7 us  [the longest x1 8.93 us: attention(): pl.pallas_call(kernel, grid_spec=pltpu.PrefetchScalarGridSpec(num_scalar_...]
    unnamed x1 -> x0, blocking collectives: 11.8 us -> none
  transfers between devices with their start and end apart: 5 -> 18, of which waited for: 3 -> 5; matrix products, arithmetic and copies ran while one was open for 45% -> 1% of each run, Pallas kernels for 0% -> 32%
where the time goes in v1:
time: 89.3 us; the launch traced here: 88.9 us
  starting transfers between devices  38.2 us (43%)
  Pallas kernels  37.7 us (42%)
  local copies, waits for them, and re-layouts  5.82 us (7%)
  waiting for transfers between devices  5.41 us (6%)
  between operations  1.02 us (1%)
    ppermute x8, starting transfers between devices, swap(): return lax.ppermute(x, 'ctx', [(i, i ^ 1) for i in range(count)])  18.4 us
    ppermute x6, starting transfers between devices, onward(): lax.ppermute(x, 'ctx', [(i, k) for i, k in hops if 0 <= k < 2 * pairs])  14.6 us
    pallas_call x1, Pallas kernels, attention(): pl.pallas_call(kernel, grid_spec=pltpu.PrefetchScalarGridSpec(num_scalar_...  8.93 us
    pallas_call x2, Pallas kernels, states(): pl.pallas_call(states_kernel, grid_spec=pltpu.PrefetchScalarGridSpec(num_...  7.61 us
    unnamed x40, local copies, waits for them, and re-layouts  5.71 us
    pallas_call x2, Pallas kernels, across_outputs(): pl.pallas_call(kernel, in_specs=[SCALAR] + [WHOLE] * 4 + [ANYWHERE] + [WH...  5.66 us
    pallas_call x1, Pallas kernels, inside(): pl.pallas_call(inside_kernel, grid=(cols // span,), in_specs=[block, bloc...  3.95 us
    pallas_call x2, Pallas kernels, carries(): pl.pallas_call(kernel, in_specs=[WHOLE] * (3 + len(others)), out_specs=[W...  3.43 us
  transfers between devices with their start and end apart: 18, of which 5 were waited for; matrix products, arithmetic and copies ran while one was open for 1% of the time, Pallas kernels for 32%

profile of v1, /device:TPU:23, one launch (start us, length us, event | category | flops | bytes accessed | tf_op | source)
XLA Modules:
  0.0 88.9 jit_solution(11539309348788630569)
XLA Ops:
  0.6 3.8 %chunk_states.2 = (bf16[272,4096]{1,0:T(8,128)(2,1)S(1)}, bf16[144,512]{1,0:T(8,128)(2,1)S(1)}) custom-call(s32[1]{0:T(128)S(6)} %sub.8.kind.other, bf16[128,4096]{1,0:T(8,128)(2,1)} %x.7, bf16[128,4096]{1,0:T(8,128)(2,1)} %dy.7, bf16[128,256]{1,0:T(8,128)(2,1)} %refs_1_.7, bf16[128,256]{1,0:T(8,128)(2,1)} %refs_2_.9, f32[64,128]{1,0:T(8,128)} %bitcast.8, ...), custom_call_target="tpu_custom_call" | custom-call | flops 1 | bytes 1 | tf_op jit(solution)/shard_map/chunk_states/pallas_call | solution.py:161
  4.5 0.7 collective-permute-start.2
  5.2 1.3 %collective-permute-start = (bf16[144,512]{1,0:T(8,128)(2,1)S(1)}, bf16[144,512]{1,0:T(8,128)(2,1)S(1)}, u32[]{:S(2)}, u32[]{:S(2)}) collective-permute-start(bf16[144,512]{1,0:T(8,128)(2,1)S(1)} %get-tuple-element.67.refs_4_), channel_id=1, source_target_pairs={{0,8},{4,12},{8,16},{12,20},{16,24},{20,28},{1,9},{5,13},{9,17},{1... | collective-permute-start | bytes 442376 | tf_op jit(solution)/shard_map/ppermute | solution.py:705
  6.5 1.3 %collective-permute-start.1 = (bf16[144,512]{1,0:T(8,128)(2,1)S(1)}, bf16[144,512]{1,0:T(8,128)(2,1)S(1)}, u32[]{:S(2)}, u32[]{:S(2)}) collective-permute-start(bf16[144,512]{1,0:T(8,128)(2,1)S(1)} %get-tuple-element.67.refs_4_), channel_id=1, source_target_pairs={{0,16},{4,20},{8,24},{12,28},{1,17},{5,21},{9,25},{13,29},{2,18},{... | collective-permute-start | bytes 442376 | tf_op jit(solution)/shard_map/ppermute | solution.py:705
  7.8 3.8 %chunk_states.3.mine.refs_0_ = bf16[272,4096]{1,0:T(8,128)(2,1)S(1)} custom-call(s32[1]{0:T(128)} %bitcast.1.kind.refs_0_.refs_1_.core, bf16[128,4096]{1,0:T(8,128)(2,1)} %x.7, bf16[128,4096]{1,0:T(8,128)(2,1)} %dy.7, bf16[128,256]{1,0:T(8,128)(2,1)} %refs_1_.7, bf16[128,256]{1,0:T(8,128)(2,1)} %refs_2_.9, f32[64,128]{1,0:T(8,128)} %bitcast.9, s32[1,128]{1,0:T(1,128)} %bitcast.12), custom_call_target="tpu_custom_call" | custom-call | flops 1 | bytes 1 | tf_op jit(solution)/shard_map/chunk_states/pallas_call | solution.py:161
  11.6 0.0 copy-start
  11.6 0.0 copy-start.1
  11.6 0.0 copy-start.8
  11.6 0.0 copy-start.9
  11.6 0.0 copy-start.12
  11.6 0.0 copy-start.19
  11.7 0.9 collective-permute-done.refs_6_
  12.5 1.3 %collective-permute-done.1.refs_7_ = bf16[144,512]{1,0:T(8,128)(2,1)S(1)} collective-permute-done((bf16[144,512]{1,0:T(8,128)(2,1)S(1)}, bf16[144,512]{1,0:T(8,128)(2,1)S(1)}, u32[]{:S(2)}, u32[]{:S(2)}) %collective-permute-start.1) | collective-permute-done | bytes 147488 | tf_op jit(solution)/shard_map/ppermute | solution.py:705
  13.8 0.0 collective-permute-done.2.got
  13.8 0.7 pair_merge.1
  14.6 0.0 copy-start.10
  14.6 0.0 copy-start.11
  14.6 0.9 %collective-permute-start.8 = (bf16[2,272,2048]{2,1,0:T(8,128)(2,1)S(1)}, bf16[2,272,2048]{2,1,0:T(8,128)(2,1)S(1)}, u32[]{:S(2)}, u32[]{:S(2)}) collective-permute-start(bf16[2,272,2048]{2,1,0:T(8,128)(2,1)S(1)} %get-tuple-element.70), channel_id=1, source_target_pairs={{8,24},{20,4},{9,25},{21,5},{10,26},{22,6},{11,27},{23,7}} | collective-permute-start | bytes 6684680 | tf_op jit(solution)/shard_map/ppermute | solution.py:716
  15.5 2.0 %collective-permute-start.10 = (bf16[2,272,2048]{2,1,0:T(8,128)(2,1)S(1)}, bf16[2,272,2048]{2,1,0:T(8,128)(2,1)S(1)}, u32[]{:S(2)}, u32[]{:S(2)}) collective-permute-start(bf16[2,272,2048]{2,1,0:T(8,128)(2,1)S(1)} %get-tuple-element.70), channel_id=1, source_target_pairs={{0,16},{28,12},{1,17},{29,13},{2,18},{30,14},{3,19},{31,15}} | collective-permute-start | bytes 6684680 | tf_op jit(solution)/shard_map/ppermute | solution.py:716
  17.5 5.0 %collective-permute-start.6 = (bf16[2,272,2048]{2,1,0:T(8,128)(2,1)S(1)}, bf16[2,272,2048]{2,1,0:T(8,128)(2,1)S(1)}, u32[]{:S(2)}, u32[]{:S(2)}) collective-permute-start(bf16[2,272,2048]{2,1,0:T(8,128)(2,1)S(1)} %get-tuple-element.70), channel_id=1, source_target_pairs={{0,8},{12,4},{16,24},{28,20},{1,9},{13,5},{17,25},{29,21},{2,10},{... | collective-permute-start | bytes 6684680 | tf_op jit(solution)/shard_map/ppermute | solution.py:716
  22.6 0.1 collective-permute-start.3
  22.6 0.5 collective-permute-start.4
  23.1 0.9 collective-permute-done.3.refs_5_
  24.0 0.1 collective-permute-start.5
  24.2 3.9 %inside_chunk.1 = (bf16[128,4096]{1,0:T(8,128)(2,1)S(1)}, bf16[128,4096]{1,0:T(8,128)(2,1)S(1)}, f32[2,128,256]{2,1,0:T(8,128)S(1)}, f32[3,128,64]{2,1,0:T(8,128)S(1)}) custom-call(bf16[128,4096]{1,0:T(8,128)(2,1)S(1)} %copy-done, bf16[128,4096]{1,0:T(8,128)(2,1)S(1)} %copy-done.1, bf16[128,256]{1,0:T(8,128)(2,1)S(1)} %copy-done.8, ...), custom_call_target="tpu_custom_call" | custom-call | flops 1 | bytes 1 | tf_op jit(solution)/shard_map/inside_chunk/pallas_call | solution.py:339
  28.1 0.0 copy-start.4
  28.1 1.0 %copy-done.4 = bf16[128,4096]{1,0:T(8,128)(2,1)} copy-done((bf16[128,4096]{1,0:T(8,128)(2,1)}, bf16[128,4096]{1,0:T(8,128)(2,1)S(1)}, u32[]{:S(2)}) %copy-start.4) | copy-done | bytes 1048600
  29.1 1.0 %copy-done.6 = bf16[128,4096]{1,0:T(8,128)(2,1)} copy-done((bf16[128,4096]{1,0:T(8,128)(2,1)}, bf16[128,4096]{1,0:T(8,128)(2,1)S(1)}, u32[]{:S(2)}) %copy-start.6) | copy-done | bytes 1048600
  30.1 0.0 collective-permute-done.4.refs_8_
  30.1 0.0 collective-permute-done.5.refs_9_
  30.1 8.9 %packed_attention.1 = (bf16[128,2048]{1,0:T(8,128)(2,1)}, bf16[128,2048]{1,0:T(8,128)(2,1)}, f32[128,512]{1,0:T(8,128)S(1)}, bf16[1,2,128,512]{3,2,1,0:T(8,128)(...) custom-call(s32[1]{0:T(128)} %bitcast.1.kind.refs_0_.refs_1_.core, ...), custom_call_target="tpu_custom_call" | custom-call | flops 1 | bytes 1 | tf_op jit(solution)/shard_map/packed_attention/pallas_call | solution.py:680
  39.0 0.7 copy-done.15
  39.7 0.6 copy-done.17
  40.4 0.7 collective-permute-start.7
  41.1 0.0 collective-permute-done.8.refs_3_
  41.1 0.1 slice_bitcast_fusion
  41.3 0.7 collective-permute-start.9
  42.0 4.4 %collective-permute-start.11 = (bf16[1,2,128,512]{3,2,1,0:T(8,128)(2,1)S(1)}, bf16[1,2,128,512]{3,2,1,0:T(8,128)(2,1)S(1)}, u32[]{:S(2)}, u32[]{:S(2)}) collective-permute-start(bf16[1,2,128,512]{3,2,1,0:T(8,128)(2,1)S(1)} %get-tuple-element.82), channel_id=1, source_target_pairs={{0,4},{4,0},{8,12},{12,8},{16,20},{20,16},{24,28},{28,24},{1,5},{5... | collective-permute-start | bytes 786440 | tf_op jit(solution)/shard_map/ppermute | solution.py:710
  46.4 1.2 %collective-permute-done.11 = bf16[1,2,128,512]{3,2,1,0:T(8,128)(2,1)S(1)} collective-permute-done((bf16[1,2,128,512]{3,2,1,0:T(8,128)(2,1)S(1)}, bf16[1,2,128,512]{3,2,1,0:T(8,128)(2,1)S(1)}, u32[]{:S(2)}, u32[]{:S(2)}) %collective-permute-start.11) | collective-permute-done | bytes 262176 | tf_op jit(solution)/shard_map/ppermute | solution.py:710
  47.6 0.8 add_convert_fusion
  48.4 0.0 collective-permute-done.9.refs_2_
  48.4 1.7 %carry_states.3 = (bf16[272,2048]{1,0:T(8,128)(2,1)S(1)}, bf16[272,2048]{1,0:T(8,128)(2,1)}) custom-call(bf16[272,4096]{1,0:T(8,128)(2,1)S(1)} %chunk_states.3.mine.refs_0_, bf16[2,272,2048]{2,1,0:T(8,128)(2,1)S(1)} %collective-permute-done.6.refs_1_, bf16[272,2048]{1,0:T(8,128)(2,1)S(1)} %collective-permute-done.7.refs_2_, ...), custom_call_target="tpu_custom_call" | custom-call | flops 1 | bytes 1 | tf_op jit(solution)/shard_map/carry_states/pallas_call | solution.py:257
  50.1 11.0 %collective-permute-start.12 = (bf16[272,2048]{1,0:T(8,128)(2,1)}, bf16[272,2048]{1,0:T(8,128)(2,1)}, u32[]{:S(2)}, u32[]{:S(2)}) collective-permute-start(bf16[272,2048]{1,0:T(8,128)(2,1)} %get-tuple-element.92), channel_id=1, source_target_pairs={{0,4},{4,0},{8,12},{12,8},{16,20},{20,16},{24,28},{28,24},{1,5},{5... | collective-permute-start | bytes 3342344 | tf_op jit(solution)/shard_map/ppermute | solution.py:710
  61.1 1.7 %carry_states.2 = (bf16[272,2048]{1,0:T(8,128)(2,1)S(1)}, bf16[272,2048]{1,0:T(8,128)(2,1)}) custom-call(bf16[272,4096]{1,0:T(8,128)(2,1)S(1)} %chunk_states.3.mine.refs_0_, bf16[2,272,2048]{2,1,0:T(8,128)(2,1)S(1)} %collective-permute-done.6.refs_1_, bf16[272,2048]{1,0:T(8,128)(2,1)S(1)} %collective-permute-done.9.refs_2_, ...), custom_call_target="tpu_custom_call" | custom-call | flops 1 | bytes 1 | tf_op jit(solution)/shard_map/carry_states/pallas_call | solution.py:257
  62.8 1.0 %copy-done.2 = bf16[272,2048]{1,0:T(8,128)(2,1)} copy-done((bf16[272,2048]{1,0:T(8,128)(2,1)}, bf16[272,2048]{1,0:T(8,128)(2,1)S(1)}, u32[]{:S(2)}) %copy-start.2) | copy-done | bytes 1114136
  63.8 0.0 collective-permute-start.13
  63.8 5.2 %collective-permute-start.15 = (bf16[2,128,512]{2,1,0:T(8,128)(2,1)}, bf16[2,128,512]{2,1,0:T(8,128)(2,1)}, u32[]{:S(2)}, u32[]{:S(2)}) collective-permute-start(bf16[2,128,512]{2,1,0:T(8,128)(2,1)} %bitcast.6), channel_id=1, source_target_pairs={{8,0},{16,8},{20,4},{24,16},{28,12},{9,1},{17,9},{21,5},{25,17},{2... | collective-permute-start | bytes 786440 | tf_op jit(solution)/shard_map/ppermute | solution.py:716
  69.0 0.9 %copy-done.14 = f32[2,128,256]{2,1,0:T(8,128)S(1)} copy-done((f32[2,128,256]{2,1,0:T(8,128)S(1)}, f32[2,128,256]{2,1,0:T(8,128)}, u32[]{:S(2)}) %copy-start.14) | copy-done | bytes 262168
  70.0 0.9 across_sums.2.refs_6_
  70.9 0.4 copy-done.3
  71.2 0.9 across_sums.3.acc_in
  72.1 0.0 collective-permute-done.12.low.refs_5_
  72.1 0.0 collective-permute-done.13.high.refs_5_
  72.1 0.0 copy-start.5
  72.1 0.0 copy-start.7
  72.1 3.0 %given_sums.1 = (f32[2,64,256]{2,1,0:T(8,128)S(1)}, bf16[2,64,256]{2,1,0:T(8,128)(2,1)S(1)}) custom-call(s32[1]{0:T(128)S(6)} %sub.8.kind.other, s32[1]{0:T(128)} %bitcast.4.side, bf16[128,4096]{1,0:T(8,128)(2,1)S(1)} %copy-done, bf16[128,4096]{1,0:T(8,128)(2,1)S(1)} %copy-done.1, f32[3,128,64]{2,1,0:T(8,128)S(1)} %get-tuple-element.77.refs_4_.decays.refs_3_, ...), custom_call_target="tpu_custom_call" | custom-call | flops 1 | bytes 1 | tf_op jit(solution)/shard_map/given_sums/pallas_call | solution.py:443
  75.2 0.1 collective-permute-start.14
  75.3 2.8 %across_outputs.2 = (bf16[128,4096]{1,0:T(8,128)(2,1)}, bf16[128,4096]{1,0:T(8,128)(2,1)}) custom-call(s32[1]{0:T(128)} %bitcast.1.kind.refs_0_.refs_1_.core, bf16[128,256]{1,0:T(8,128)(2,1)S(1)} %copy-done.8, bf16[128,256]{1,0:T(8,128)(2,1)S(1)} %copy-done.9, f32[3,128,64]{2,1,0:T(8,128)S(1)} %get-tuple-element.77.refs_4_.decays.refs_3_, ...), custom_call_target="tpu_custom_call" | custom-call | flops 1 | bytes 1 | tf_op jit(solution)/shard_map/across_outputs/pallas_call | solution.py:520
  78.1 1.2 %collective-permute-done.14.moved = bf16[2,64,256]{2,1,0:T(8,128)(2,1)S(1)} collective-permute-done((bf16[2,64,256]{2,1,0:T(8,128)(2,1)S(1)}, bf16[2,64,256]{2,1,0:T(8,128)(2,1)S(1)}, u32[]{:S(2)}, u32[]{:S(2)}) %collective-permute-start.14) | collective-permute-done | bytes 65568 | tf_op jit(solution)/shard_map/ppermute | solution.py:829
  79.3 1.0 %partner_part.1 = bf16[128,512]{1,0:T(8,128)(2,1)S(1)} custom-call(s32[1]{0:T(128)S(6)} %sub.8.kind.other, bf16[128,512]{1,0:T(8,128)(2,1)S(1)} %copy-done.18, bf16[2,128,512]{2,1,0:T(8,128)(2,1)} %collective-permute-done.15.refs_0_), custom_call_target="tpu_custom_call" | custom-call | flops 1 | bytes 1 | tf_op jit(solution)/shard_map/partner_part/pallas_call | solution.py:546
  80.3 1.5 %collective-permute-start.17 = (bf16[128,512]{1,0:T(8,128)(2,1)S(1)}, bf16[128,512]{1,0:T(8,128)(2,1)S(1)}, u32[]{:S(2)}, u32[]{:S(2)}) collective-permute-start(bf16[128,512]{1,0:T(8,128)(2,1)S(1)} %partner_part.1), channel_id=1, source_target_pairs={{0,4},{4,0},{8,12},{12,8},{16,20},{20,16},{24,28},{28,24},{1,5},{5... | collective-permute-start | bytes 393224 | tf_op jit(solution)/shard_map/ppermute | solution.py:710
  81.9 2.5 %collective-permute-start.16 = (bf16[2,32,256]{2,1,0:T(8,128)(2,1)S(1)}, bf16[2,32,256]{2,1,0:T(8,128)(2,1)S(1)}, u32[]{:S(2)}, u32[]{:S(2)}) collective-permute-start(bf16[2,32,256]{2,1,0:T(8,128)(2,1)S(1)} %get-tuple-element.103), channel_id=1, source_target_pairs={{0,1},{1,0},{2,3},{3,2},{4,5},{5,4},{6,7},{7,6},{8,9},{9,8},{10,11... | collective-permute-start | bytes 98312 | tf_op jit(solution)/shard_map/ppermute | solution.py:829
  84.4 2.8 %across_outputs.3 = (bf16[128,4096]{1,0:T(8,128)(2,1)}, bf16[128,4096]{1,0:T(8,128)(2,1)}) custom-call(s32[1]{0:T(128)} %bitcast.1.kind.refs_0_.refs_1_.core, bf16[128,256]{1,0:T(8,128)(2,1)S(1)} %copy-done.8, bf16[128,256]{1,0:T(8,128)(2,1)S(1)} %copy-done.9, ...), custom_call_target="tpu_custom_call", output_to_operand_aliasing={{0}: (8, {}), {1}: (9, {})} | custom-call | flops 1 | bytes 1 | tf_op jit(solution)/shard_map/across_outputs/pallas_call | solution.py:520
  87.3 1.6 %last_sums.1 = (bf16[128,256]{1,0:T(8,128)(2,1)}, bf16[128,256]{1,0:T(8,128)(2,1)}, bf16[32,256]{1,0:T(8,128)(2,1)}, bf16[32,256]{1,0:T(8,128)(2,1)}) custom-call(s32[1]{0:T(128)} %bitcast.1.kind.refs_0_.refs_1_.core, f32[128,512]{1,0:T(8,128)S(1)} %copy-done.16, bf16[128,512]{1,0:T(8,128)(2,1)S(1)} %collective-permute-done.17.swapped, ...), custom_call_target="tpu_custom_call" | custom-call | flops 1 | bytes 1 | tf_op jit(solution)/shard_map/last_sums/pallas_call | solution.py:572
  (29 shorter events, 0.1 us)
Async XLA Ops:
  4.5 9.4 %collective-permute-start.2 = (bf16[272,4096]{1,0:T(8,128)(2,1)S(1)}, bf16[272,4096]{1,0:T(8,128)(2,1)S(1)}, u32[]{:S(2)}, u32[]{:S(2)}) collective-permute-start(bf16[272,4096]{1,0:T(8,128)(2,1)S(1)} %get-tuple-element.69), channel_id=1, source_target_pairs={{0,4},{4,0},{8,12},{12,8},{16,20},{20,16},{24,28},{28,24},{1,5},{5... | collective-permute-start | bytes 6684680 | tf_op jit(solution)/shard_map/ppermute | solution.py:710
  5.2 7.3 %collective-permute-start = (bf16[144,512]{1,0:T(8,128)(2,1)S(1)}, bf16[144,512]{1,0:T(8,128)(2,1)S(1)}, u32[]{:S(2)}, u32[]{:S(2)}) collective-permute-start(bf16[144,512]{1,0:T(8,128)(2,1)S(1)} %get-tuple-element.67.refs_4_), channel_id=1, source_target_pairs={{0,8},{4,12},{8,16},{12,20},{16,24},{20,28},{1,9},{5,13},{9,17},{1... | collective-permute-start | bytes 442376 | tf_op jit(solution)/shard_map/ppermute | solution.py:705
  6.5 7.4 %collective-permute-start.1 = (bf16[144,512]{1,0:T(8,128)(2,1)S(1)}, bf16[144,512]{1,0:T(8,128)(2,1)S(1)}, u32[]{:S(2)}, u32[]{:S(2)}) collective-permute-start(bf16[144,512]{1,0:T(8,128)(2,1)S(1)} %get-tuple-element.67.refs_4_), channel_id=1, source_target_pairs={{0,16},{4,20},{8,24},{12,28},{1,17},{5,21},{9,25},{13,29},{2,18},{... | collective-permute-start | bytes 442376 | tf_op jit(solution)/shard_map/ppermute | solution.py:705
  11.6 12.6 %copy-start = (bf16[128,4096]{1,0:T(8,128)(2,1)S(1)}, bf16[128,4096]{1,0:T(8,128)(2,1)}, u32[]{:S(2)}) copy-start(bf16[128,4096]{1,0:T(8,128)(2,1)} %x.7) | copy-start | bytes 3145732
  11.6 12.5 %copy-start.1 = (bf16[128,4096]{1,0:T(8,128)(2,1)S(1)}, bf16[128,4096]{1,0:T(8,128)(2,1)}, u32[]{:S(2)}) copy-start(bf16[128,4096]{1,0:T(8,128)(2,1)} %dy.7) | copy-start | bytes 3145732
  11.6 12.5 %copy-start.8 = (bf16[128,256]{1,0:T(8,128)(2,1)S(1)}, bf16[128,256]{1,0:T(8,128)(2,1)}, u32[]{:S(2)}) copy-start(bf16[128,256]{1,0:T(8,128)(2,1)} %refs_1_.7) | copy-start | bytes 196612
  11.6 12.5 %copy-start.9 = (bf16[128,256]{1,0:T(8,128)(2,1)S(1)}, bf16[128,256]{1,0:T(8,128)(2,1)}, u32[]{:S(2)}) copy-start(bf16[128,256]{1,0:T(8,128)(2,1)} %refs_2_.9) | copy-start | bytes 196612
  11.6 12.5 %copy-start.12 = (f32[128,64]{0,1:T(8,128)S(1)}, f32[128,64]{0,1:T(8,128)}, u32[]{:S(2)}) copy-start(f32[128,64]{0,1:T(8,128)} %param.18) | copy-start | bytes 98308
  11.6 12.5 %copy-start.19 = (s32[128]{0:T(128)S(1)}, s32[128]{0:T(128)}, u32[]{:S(2)}) copy-start(s32[128]{0:T(128)} %param.14) | copy-start | bytes 1540
  14.6 15.5 %copy-start.10 = (bf16[128,2048]{1,0:T(8,128)(2,1)S(1)}, bf16[128,2048]{1,0:T(8,128)(2,1)}, u32[]{:S(2)}) copy-start(bf16[128,2048]{1,0:T(8,128)(2,1)} %refs_1_.5) | copy-start | bytes 1572868
  14.6 15.5 %copy-start.11 = (bf16[128,2048]{1,0:T(8,128)(2,1)S(1)}, bf16[128,2048]{1,0:T(8,128)(2,1)}, u32[]{:S(2)}) copy-start(bf16[128,2048]{1,0:T(8,128)(2,1)} %refs_2_.5) | copy-start | bytes 1572868
  14.6 26.5 %collective-permute-start.8 = (bf16[2,272,2048]{2,1,0:T(8,128)(2,1)S(1)}, bf16[2,272,2048]{2,1,0:T(8,128)(2,1)S(1)}, u32[]{:S(2)}, u32[]{:S(2)}) collective-permute-start(bf16[2,272,2048]{2,1,0:T(8,128)(2,1)S(1)} %get-tuple-element.70), channel_id=1, source_target_pairs={{8,24},{20,4},{9,25},{21,5},{10,26},{22,6},{11,27},{23,7}} | collective-permute-start | bytes 6684680 | tf_op jit(solution)/shard_map/ppermute | solution.py:716
  15.5 32.8 %collective-permute-start.10 = (bf16[2,272,2048]{2,1,0:T(8,128)(2,1)S(1)}, bf16[2,272,2048]{2,1,0:T(8,128)(2,1)S(1)}, u32[]{:S(2)}, u32[]{:S(2)}) collective-permute-start(bf16[2,272,2048]{2,1,0:T(8,128)(2,1)S(1)} %get-tuple-element.70), channel_id=1, source_target_pairs={{0,16},{28,12},{1,17},{29,13},{2,18},{30,14},{3,19},{31,15}} | collective-permute-start | bytes 6684680 | tf_op jit(solution)/shard_map/ppermute | solution.py:716
  17.5 30.8 %collective-permute-start.6 = (bf16[2,272,2048]{2,1,0:T(8,128)(2,1)S(1)}, bf16[2,272,2048]{2,1,0:T(8,128)(2,1)S(1)}, u32[]{:S(2)}, u32[]{:S(2)}) collective-permute-start(bf16[2,272,2048]{2,1,0:T(8,128)(2,1)S(1)} %get-tuple-element.70), channel_id=1, source_target_pairs={{0,8},{12,4},{16,24},{28,20},{1,9},{13,5},{17,25},{29,21},{2,10},{... | collective-permute-start | bytes 6684680 | tf_op jit(solution)/shard_map/ppermute | solution.py:716
  22.6 1.4 %collective-permute-start.3 = (bf16[144,512]{1,0:T(8,128)(2,1)S(1)}, bf16[144,512]{1,0:T(8,128)(2,1)S(1)}, u32[]{:S(2)}, u32[]{:S(2)}) collective-permute-start(bf16[144,512]{1,0:T(8,128)(2,1)S(1)} %get-tuple-element.67.refs_4_), channel_id=1, source_target_pairs={{0,4},{4,0},{8,12},{12,8},{16,20},{20,16},{24,28},{28,24},{1,5},{5... | collective-permute-start | bytes 442376 | tf_op jit(solution)/shard_map/ppermute | solution.py:710
  22.6 7.4 %collective-permute-start.4 = (bf16[144,512]{1,0:T(8,128)(2,1)S(1)}, bf16[144,512]{1,0:T(8,128)(2,1)S(1)}, u32[]{:S(2)}, u32[]{:S(2)}) collective-permute-start(bf16[144,512]{1,0:T(8,128)(2,1)S(1)} %collective-permute-done.refs_6_), channel_id=1, source_target_pairs={{0,4},{4,0},{8,12},{12,8},{16,20},{20,16},{24,28},{28,24},{1,5},{5... | collective-permute-start | bytes 442376 | tf_op jit(solution)/shard_map/ppermute | solution.py:710
  24.0 6.1 %collective-permute-start.5 = (bf16[144,512]{1,0:T(8,128)(2,1)S(1)}, bf16[144,512]{1,0:T(8,128)(2,1)S(1)}, u32[]{:S(2)}, u32[]{:S(2)}) collective-permute-start(bf16[144,512]{1,0:T(8,128)(2,1)S(1)} %collective-permute-done.1.refs_7_), channel_id=1, source_target_pairs={{0,4},{4,0},{8,12},{12,8},{16,20},{20,16},{24,28},{28,24},{1,5},{5... | collective-permute-start | bytes 442376 | tf_op jit(solution)/shard_map/ppermute | solution.py:710
  28.1 1.0 %copy-start.4 = (bf16[128,4096]{1,0:T(8,128)(2,1)}, bf16[128,4096]{1,0:T(8,128)(2,1)S(1)}, u32[]{:S(2)}) copy-start(bf16[128,4096]{1,0:T(8,128)(2,1)S(1)} %get-tuple-element.97.refs_6_) | copy-start | bytes 3145732
  29.1 1.0 %copy-start.6 = (bf16[128,4096]{1,0:T(8,128)(2,1)}, bf16[128,4096]{1,0:T(8,128)(2,1)S(1)}, u32[]{:S(2)}) copy-start(bf16[128,4096]{1,0:T(8,128)(2,1)S(1)} %get-tuple-element.98.refs_7_) | copy-start | bytes 3145732
  30.1 10.3 %copy-start.13 = (f32[2,128,256]{2,1,0:T(8,128)}, f32[2,128,256]{2,1,0:T(8,128)S(1)}, u32[]{:S(2)}) copy-start(f32[2,128,256]{2,1,0:T(8,128)S(1)} %get-tuple-element.91.refs_6_) | copy-start | bytes 786436
  39.0 0.7 copy-start.15
  39.7 0.7 copy-start.17
  40.4 8.0 %collective-permute-start.7 = (bf16[272,2048]{1,0:T(8,128)(2,1)S(1)}, bf16[272,2048]{1,0:T(8,128)(2,1)S(1)}, u32[]{:S(2)}, u32[]{:S(2)}) collective-permute-start(bf16[272,2048]{1,0:T(8,128)(2,1)S(1)} %get-tuple-element.80), channel_id=1, source_target_pairs={{8,16},{20,12},{9,17},{21,13},{10,18},{22,14},{11,19},{23,15}} | collective-permute-start | bytes 3342344 | tf_op jit(solution)/shard_map/ppermute | solution.py:716
  41.3 7.1 %collective-permute-start.9 = (bf16[272,2048]{1,0:T(8,128)(2,1)S(1)}, bf16[272,2048]{1,0:T(8,128)(2,1)S(1)}, u32[]{:S(2)}, u32[]{:S(2)}) collective-permute-start(bf16[272,2048]{1,0:T(8,128)(2,1)S(1)} %slice_bitcast_fusion), channel_id=1, source_target_pairs={{4,12},{24,16},{5,13},{25,17},{6,14},{26,18},{7,15},{27,19}} | collective-permute-start | bytes 3342344 | tf_op jit(solution)/shard_map/ppermute | solution.py:716
  42.0 5.6 %collective-permute-start.11 = (bf16[1,2,128,512]{3,2,1,0:T(8,128)(2,1)S(1)}, bf16[1,2,128,512]{3,2,1,0:T(8,128)(2,1)S(1)}, u32[]{:S(2)}, u32[]{:S(2)}) collective-permute-start(bf16[1,2,128,512]{3,2,1,0:T(8,128)(2,1)S(1)} %get-tuple-element.82), channel_id=1, source_target_pairs={{0,4},{4,0},{8,12},{12,8},{16,20},{20,16},{24,28},{28,24},{1,5},{5... | collective-permute-start | bytes 786440 | tf_op jit(solution)/shard_map/ppermute | solution.py:710
  50.1 22.0 %collective-permute-start.12 = (bf16[272,2048]{1,0:T(8,128)(2,1)}, bf16[272,2048]{1,0:T(8,128)(2,1)}, u32[]{:S(2)}, u32[]{:S(2)}) collective-permute-start(bf16[272,2048]{1,0:T(8,128)(2,1)} %get-tuple-element.92), channel_id=1, source_target_pairs={{0,4},{4,0},{8,12},{12,8},{16,20},{20,16},{24,28},{28,24},{1,5},{5... | collective-permute-start | bytes 3342344 | tf_op jit(solution)/shard_map/ppermute | solution.py:710
  62.8 1.0 %copy-start.2 = (bf16[272,2048]{1,0:T(8,128)(2,1)}, bf16[272,2048]{1,0:T(8,128)(2,1)S(1)}, u32[]{:S(2)}) copy-start(bf16[272,2048]{1,0:T(8,128)(2,1)S(1)} %get-tuple-element.88.refs_5_.refs_4_) | copy-start | bytes 3342340
  63.8 8.3 %collective-permute-start.13 = (bf16[272,2048]{1,0:T(8,128)(2,1)}, bf16[272,2048]{1,0:T(8,128)(2,1)}, u32[]{:S(2)}, u32[]{:S(2)}) collective-permute-start(bf16[272,2048]{1,0:T(8,128)(2,1)} %get-tuple-element.93), channel_id=1, source_target_pairs={{0,4},{4,0},{8,12},{12,8},{16,20},{20,16},{24,28},{28,24},{1,5},{5... | collective-permute-start | bytes 3342344 | tf_op jit(solution)/shard_map/ppermute | solution.py:710
  63.8 14.3 %collective-permute-start.15 = (bf16[2,128,512]{2,1,0:T(8,128)(2,1)}, bf16[2,128,512]{2,1,0:T(8,128)(2,1)}, u32[]{:S(2)}, u32[]{:S(2)}) collective-permute-start(bf16[2,128,512]{2,1,0:T(8,128)(2,1)} %bitcast.6), channel_id=1, source_target_pairs={{8,0},{16,8},{20,4},{24,16},{28,12},{9,1},{17,9},{21,5},{25,17},{2... | collective-permute-start | bytes 786440 | tf_op jit(solution)/shard_map/ppermute | solution.py:716
  69.0 0.9 %copy-start.14 = (f32[2,128,256]{2,1,0:T(8,128)S(1)}, f32[2,128,256]{2,1,0:T(8,128)}, u32[]{:S(2)}) copy-start(f32[2,128,256]{2,1,0:T(8,128)} %copy-done.13) | copy-start | bytes 786436
  70.0 1.2 %copy-start.3 = (bf16[272,2048]{1,0:T(8,128)(2,1)S(1)}, bf16[272,2048]{1,0:T(8,128)(2,1)}, u32[]{:S(2)}) copy-start(bf16[272,2048]{1,0:T(8,128)(2,1)} %copy-done.2) | copy-start | bytes 3342340
  72.1 3.2 %copy-start.5 = (bf16[128,4096]{1,0:T(8,128)(2,1)S(1)}, bf16[128,4096]{1,0:T(8,128)(2,1)}, u32[]{:S(2)}) copy-start(bf16[128,4096]{1,0:T(8,128)(2,1)} %copy-done.4) | copy-start | bytes 3145732
  72.1 3.2 %copy-start.7 = (bf16[128,4096]{1,0:T(8,128)(2,1)S(1)}, bf16[128,4096]{1,0:T(8,128)(2,1)}, u32[]{:S(2)}) copy-start(bf16[128,4096]{1,0:T(8,128)(2,1)} %copy-done.6) | copy-start | bytes 3145732
  75.2 4.1 %collective-permute-start.14 = (bf16[2,64,256]{2,1,0:T(8,128)(2,1)S(1)}, bf16[2,64,256]{2,1,0:T(8,128)(2,1)S(1)}, u32[]{:S(2)}, u32[]{:S(2)}) collective-permute-start(bf16[2,64,256]{2,1,0:T(8,128)(2,1)S(1)} %get-tuple-element.95), channel_id=1, source_target_pairs={{0,2},{1,3},{2,0},{3,1},{4,6},{5,7},{6,4},{7,5},{8,10},{9,11},{10,... | collective-permute-start | bytes 196616 | tf_op jit(solution)/shard_map/ppermute | solution.py:829
  75.3 4.0 %copy-start.18 = (bf16[128,512]{1,0:T(8,128)(2,1)S(1)}, bf16[128,512]{1,0:T(8,128)(2,1)}, u32[]{:S(2)}) copy-start(bf16[128,512]{1,0:T(8,128)(2,1)} %copy-done.17) | copy-start | bytes 393220
  80.3 6.9 %collective-permute-start.17 = (bf16[128,512]{1,0:T(8,128)(2,1)S(1)}, bf16[128,512]{1,0:T(8,128)(2,1)S(1)}, u32[]{:S(2)}, u32[]{:S(2)}) collective-permute-start(bf16[128,512]{1,0:T(8,128)(2,1)S(1)} %partner_part.1), channel_id=1, source_target_pairs={{0,4},{4,0},{8,12},{12,8},{16,20},{20,16},{24,28},{28,24},{1,5},{5... | collective-permute-start | bytes 393224 | tf_op jit(solution)/shard_map/ppermute | solution.py:710
  81.9 5.4 %collective-permute-start.16 = (bf16[2,32,256]{2,1,0:T(8,128)(2,1)S(1)}, bf16[2,32,256]{2,1,0:T(8,128)(2,1)S(1)}, u32[]{:S(2)}, u32[]{:S(2)}) collective-permute-start(bf16[2,32,256]{2,1,0:T(8,128)(2,1)S(1)} %get-tuple-element.103), channel_id=1, source_target_pairs={{0,1},{1,0},{2,3},{3,2},{4,5},{5,4},{6,7},{7,6},{8,9},{9,8},{10,11... | collective-permute-start | bytes 98312 | tf_op jit(solution)/shard_map/ppermute | solution.py:829
  84.4 2.9 %copy-start.16 = (f32[128,512]{1,0:T(8,128)S(1)}, f32[128,512]{1,0:T(8,128)}, u32[]{:S(2)}) copy-start(f32[128,512]{1,0:T(8,128)} %copy-done.15) | copy-start | bytes 786436

commit v2 on v1

--- a/solution.py
+++ b/solution.py
@@ -359,23 +359,40 @@
     return jnp.where(decays[2] == doc, decay, 0.0).astype(BF16)
 
 
-def sums_kernel(half, ranks, kind, side, x, dy, decays, carried, acc_in, *refs):
+def begin(picked, one, two, target, sem):
+    copies = [pltpu.make_async_copy(source, target, sem) for source in (one, two)]
+
+    @pl.when(picked)
+    def _():
+        copies[1].start()
+
+    @pl.when(jnp.logical_not(picked))
+    def _():
+        copies[0].start()
+
+    return copies[0]
+
+
+def sums_kernel(half, kind, x, dy, decays, carried, acc_in, acc, z_in, sems):
     heads = decays.shape[2]
     cols = carried.shape[1]
+    part = min(cols, 2 * WIDTH)
     forward = kind[0] == 0
+    waits = []
+    for n in range(cols // part):
+        source = [a.at[:, pl.ds(half * cols + n * part, part)] for a in (x, dy)]
+        waits.append(begin(forward, *source, z_in.at[:, pl.ds(n * part, part)], sems.at[n]))
     weight = carried_weight(forward, carried, decays)
     total = 0.0
     for t in range(cols // WIDTH):
+        if t * WIDTH % part == 0:
+            waits[t * WIDTH // part].wait()
         at = slice(t * WIDTH, (t + 1) * WIDTH)
-        to = slice(half * cols + t * WIDTH, half * cols + (t + 1) * WIDTH)
         e = spread(heads, half * (heads // 2) + t * GROUP)
-        z = jnp.where(forward, dy[:, to], x[:, to]).astype(F32)
-        total = total + dot_nt((z * dot(weight, e)).astype(BF16), carried[:N, at])
-    acc = refs[-1]
+        z = (z_in[:, at].astype(F32) * dot(weight, e)).astype(BF16)
+        total = total + dot_nt(z, carried[:N, at])
     acc[0] = acc_in[0] + jnp.where(forward, 0.0, total)
     acc[1] = acc_in[1] + jnp.where(forward, total, 0.0)
-    if ranks > 1:
-        divide(side, acc, *refs[:2])
 
 
 def divide(side, acc, kept, away):
@@ -389,22 +406,23 @@
     return [jax.ShapeDtypeStruct(shape, F32), jax.ShapeDtypeStruct(shape, BF16)]
 
 
-def across_sums(half, kind, x, dy, decays, carried, acc, side=None):
-    last = side is not None
-
+def across_sums(half, kind, x, dy, decays, carried, acc):
     def kernel(*refs):
-        sums_kernel(half, 2 if last else 1, *refs)
+        sums_kernel(half, *refs)
 
     return pl.pallas_call(
         kernel,
-        in_specs=[SCALAR, SCALAR] + [WHOLE] * 5,
-        out_specs=[WHOLE, WHOLE] if last else WHOLE,
-        out_shape=halves(acc) if last else jax.ShapeDtypeStruct(acc.shape, F32),
-        scratch_shapes=[pltpu.VMEM(acc.shape, F32)] if last else [],
-        compiler_params=params(4),
+        in_specs=[SCALAR, ANYWHERE, ANYWHERE, WHOLE, WHOLE, WHOLE],
+        out_specs=WHOLE,
+        out_shape=jax.ShapeDtypeStruct(acc.shape, F32),
+        scratch_shapes=[
+            pltpu.VMEM((x.shape[0], carried.shape[1]), BF16),
+            pltpu.SemaphoreType.DMA((4,)),
+        ],
+        compiler_params=params(5),
         cost_estimate=BRIEF,
         name="across_sums",
-    )(kind, side if last else kind, x, dy, decays, carried, acc)
+    )(kind, x, dy, decays, carried, acc)
 
 
 def fetch_given(sources, buffer, sems):
@@ -420,18 +438,25 @@
     return waits, part
 
 
-def given_kernel(kind, side, x, dy, decays, acc_in, low, high, kept, away, acc, carried, sems):
+def given_kernel(
+    kind, side, x, dy, decays, acc_in, low, high, kept, away, acc, carried, sems, z_in, z_sems
+):
     heads = decays.shape[2]
     forward = kind[0] == 0
     waits, part = fetch_given((low, high), carried, sems)
+    z_waits = []
+    for n in range(len(waits)):
+        piece = (slice(None), pl.ds(n * part, part))
+        z_waits.append(begin(forward, x.at[piece], dy.at[piece], z_in.at[piece], z_sems.at[n]))
     total = 0.0
     for t in range(carried.shape[1] // WIDTH):
         if t * WIDTH % part == 0:
             waits[t * WIDTH // part].wait()
+            z_waits[t * WIDTH // part].wait()
         if t == 0:
             weight = carried_weight(forward, carried, decays)
         at = slice(t * WIDTH, (t + 1) * WIDTH)
-        z = jnp.where(forward, dy[:, at], x[:, at]).astype(F32)
+        z = z_in[:, at].astype(F32)
         z = (z * dot(weight, spread(heads, t * GROUP))).astype(BF16)
         total = total + dot_nt(z, carried[:N, at])
     acc[0] = acc_in[0] + jnp.where(forward, 0.0, total)
@@ -442,12 +467,14 @@
 def given_sums(kind, side, x, dy, decays, low, high, acc):
     return pl.pallas_call(
         given_kernel,
-        in_specs=[SCALAR, SCALAR] + [WHOLE] * 4 + [ANYWHERE] * 2,
+        in_specs=[SCALAR, SCALAR, ANYWHERE, ANYWHERE, WHOLE, WHOLE, ANYWHERE, ANYWHERE],
         out_specs=[WHOLE, WHOLE],
         out_shape=halves(acc),
         scratch_shapes=[
             pltpu.VMEM(acc.shape, F32),
             pltpu.VMEM((low.shape[0], 2 * low.shape[1]), BF16),
+            pltpu.SemaphoreType.DMA((8,)),
+            pltpu.VMEM(x.shape, BF16),
             pltpu.SemaphoreType.DMA((8,)),
         ],
         compiler_params=params(8),
@@ -795,6 +822,7 @@
     low, own = lax.optimization_barrier((low, own))
     straight = onward(low, ahead_across)
     relayed = onward(to_relay[1], ahead_by_relay(pairs))
+    near, send = lax.optimization_barrier((near, send))
     hold = (hold.astype(F32) + swap(send).astype(F32)).astype(BF16)
 
     mine, near, straight, relayed, to_relay, others, acc, hold = lax.optimization_barrier(
@@ -805,8 +833,8 @@
     keep_low, give_low = carries(0, mine, near, straight, others)
     keep, give = carries(1, mine, near, relayed, others)
     given_low, given = swap(give_low), swap(give)
-    acc = across_sums(0, core, ssd_input, ssd_cotan, decays, keep_low, acc)
-    acc = across_sums(1, core, ssd_input, ssd_cotan, decays, keep, acc)
+    acc = across_sums(0, core, *pinned[:2], decays, keep_low, acc)
+    acc = across_sums(1, core, *pinned[:2], decays, keep, acc)
 
     def outputs(half, after, keep, given, done=()):
         _, core_then = lax.optimization_barrier((after, core))
@@ -822,7 +850,7 @@
 
     step = ranks // 2
     kept, away = given_sums(
-        other, side_at(step), ssd_input, ssd_cotan, decays, given_low, given, acc
+        other, side_at(step), *pinned[:2], decays, given_low, given, acc
     )
     done = ()
     for half in range(ranks.bit_length() - 1):

time: 89.3 us -> 87.9 us (0.984)
  waiting for transfers between devices: 5.41 us -> 18.9 us
  starting transfers between devices: 38.2 us -> 25.9 us
  local copies, waits for them, and re-layouts: 5.82 us -> 3.82 us
    ppermute x6, waiting for transfers between devices: 0.02 us -> 12.5 us  [onward(): lax.ppermute(x, 'ctx', [(i, k) for i, k in hops if 0 <= k < 2 * pairs])]
    ppermute x8, starting transfers between devices: 18.4 us -> 7.22 us  [swap(): return lax.ppermute(x, 'ctx', [(i, i ^ 1) for i in range(count)])]
    pallas_call x3, Pallas kernels: 4.73 us -> 7.04 us  [the longest x2 4 us: across_sums(): pl.pallas_call(kernel, in_specs=[SCALAR, ANYWHERE, ANYWHERE, WHOLE, WHOLE...]
    unnamed x40 -> x36, local copies, waits for them, and re-layouts: 5.71 us -> 3.71 us
    ppermute x2, waiting for transfers between devices: 1.19 us -> 2.21 us  [body(): moved = lax.ppermute(away, 'head', [(i, i ^ step) for i in range(ranks)])]
    pallas_call x2, Pallas kernels: 5.66 us -> 4.65 us  [across_outputs(): pl.pallas_call(kernel, in_specs=[SCALAR] + [WHOLE] * 4 + [ANYWHERE] + [WH...]
    pallas_call x1, Pallas kernels: 1.64 us -> 0.69 us  [finish(): pl.pallas_call(finish_kernel, in_specs=[SCALAR] + [WHOLE] * (4 + len(part...]
    pallas_call x1, Pallas kernels: 0.98 us -> 0.03 us  [partner_part(): pl.pallas_call(partner_kernel, in_specs=[SCALAR] + [WHOLE] * (1 + len(par...]
  transfers between devices with their start and end apart: 18 -> 18, of which waited for: 5 -> 7; matrix products, arithmetic and copies ran while one was open for 1% -> 1% of each run, Pallas kernels for 32% -> 34%
where the time goes in v2:
time: 87.9 us; the launch traced here: 87.6 us
  Pallas kernels  37.1 us (42%)
  starting transfers between devices  25.9 us (29%)
  waiting for transfers between devices  18.9 us (22%)
  local copies, waits for them, and re-layouts  3.82 us (4%)
  between operations  1.07 us (1%)
    ppermute x6, starting transfers between devices, onward(): lax.ppermute(x, 'ctx', [(i, k) for i, k in hops if 0 <= k < 2 * pairs])  14.1 us
    ppermute x6, waiting for transfers between devices, onward(): lax.ppermute(x, 'ctx', [(i, k) for i, k in hops if 0 <= k < 2 * pairs])  12.5 us
    pallas_call x1, Pallas kernels, attention(): pl.pallas_call(kernel, grid_spec=pltpu.PrefetchScalarGridSpec(num_scalar_...  8.93 us
    pallas_call x2, Pallas kernels, states(): pl.pallas_call(states_kernel, grid_spec=pltpu.PrefetchScalarGridSpec(num_...  7.61 us
    ppermute x8, starting transfers between devices, swap(): return lax.ppermute(x, 'ctx', [(i, i ^ 1) for i in range(count)])  7.22 us
    pallas_call x2, Pallas kernels, across_outputs(): pl.pallas_call(kernel, in_specs=[SCALAR] + [WHOLE] * 4 + [ANYWHERE] + [WH...  4.65 us
    pallas_call x2, Pallas kernels, across_sums(): pl.pallas_call(kernel, in_specs=[SCALAR, ANYWHERE, ANYWHERE, WHOLE, WHOLE...  4 us
    pallas_call x1, Pallas kernels, inside(): pl.pallas_call(inside_kernel, grid=(cols // span,), in_specs=[block, bloc...  3.94 us
  transfers between devices with their start and end apart: 18, of which 7 were waited for; matrix products, arithmetic and copies ran while one was open for 1% of the time, Pallas kernels for 34%

profile of v2, /device:TPU:23, one launch (start us, length us, event | category | flops | bytes accessed | tf_op | source)
XLA Modules:
  0.0 87.6 jit_solution(17574002271397682704)
XLA Ops:
  0.6 3.8 %chunk_states.2 = (bf16[272,4096]{1,0:T(8,128)(2,1)S(1)}, bf16[144,512]{1,0:T(8,128)(2,1)S(1)}) custom-call(s32[1]{0:T(128)S(6)} %sub.8.kind.other, bf16[128,4096]{1,0:T(8,128)(2,1)} %x.7, bf16[128,4096]{1,0:T(8,128)(2,1)} %dy.7, bf16[128,256]{1,0:T(8,128)(2,1)} %refs_1_.11, bf16[128,256]{1,0:T(8,128)(2,1)} %refs_2_.9, f32[64,128]{1,0:T(8,128)} %bitcast.8, ...), custom_call_target="tpu_custom_call" | custom-call | flops 1 | bytes 1 | tf_op jit(solution)/shard_map/chunk_states/pallas_call | solution.py:161
  4.5 0.7 collective-permute-start.2
  5.2 1.3 %collective-permute-start = (bf16[144,512]{1,0:T(8,128)(2,1)S(1)}, bf16[144,512]{1,0:T(8,128)(2,1)S(1)}, u32[]{:S(2)}, u32[]{:S(2)}) collective-permute-start(bf16[144,512]{1,0:T(8,128)(2,1)S(1)} %get-tuple-element.69.refs_4_), channel_id=1, source_target_pairs={{0,8},{4,12},{8,16},{12,20},{16,24},{20,28},{1,9},{5,13},{9,17},{1... | collective-permute-start | bytes 442376 | tf_op jit(solution)/shard_map/ppermute | solution.py:732
  6.5 1.3 %collective-permute-start.1 = (bf16[144,512]{1,0:T(8,128)(2,1)S(1)}, bf16[144,512]{1,0:T(8,128)(2,1)S(1)}, u32[]{:S(2)}, u32[]{:S(2)}) collective-permute-start(bf16[144,512]{1,0:T(8,128)(2,1)S(1)} %get-tuple-element.69.refs_4_), channel_id=1, source_target_pairs={{0,16},{4,20},{8,24},{12,28},{1,17},{5,21},{9,25},{13,29},{2,18},{... | collective-permute-start | bytes 442376 | tf_op jit(solution)/shard_map/ppermute | solution.py:732
  7.8 3.8 %chunk_states.3.mine.refs_0_ = bf16[272,4096]{1,0:T(8,128)(2,1)S(1)} custom-call(s32[1]{0:T(128)} %bitcast.1.kind.refs_0_.core, bf16[128,4096]{1,0:T(8,128)(2,1)} %x.7, bf16[128,4096]{1,0:T(8,128)(2,1)} %dy.7, bf16[128,256]{1,0:T(8,128)(2,1)} %refs_1_.11, bf16[128,256]{1,0:T(8,128)(2,1)} %refs_2_.9, f32[64,128]{1,0:T(8,128)} %bitcast.9, s32[1,128]{1,0:T(1,128)} %bitcast.12), custom_call_target="tpu_custom_call" | custom-call | flops 1 | bytes 1 | tf_op jit(solution)/shard_map/chunk_states/pallas_call | solution.py:161
  11.6 0.0 copy-start
  11.6 0.0 copy-start.1
  11.6 0.0 copy-start.8
  11.6 0.0 copy-start.9
  11.6 0.0 copy-start.12
  11.6 0.0 copy-start.17
  11.7 0.9 collective-permute-done.refs_6_
  12.5 1.3 %collective-permute-done.1.refs_7_ = bf16[144,512]{1,0:T(8,128)(2,1)S(1)} collective-permute-done((bf16[144,512]{1,0:T(8,128)(2,1)S(1)}, bf16[144,512]{1,0:T(8,128)(2,1)S(1)}, u32[]{:S(2)}, u32[]{:S(2)}) %collective-permute-start.1) | collective-permute-done | bytes 147488 | tf_op jit(solution)/shard_map/ppermute | solution.py:732
  13.8 0.0 collective-permute-done.2.got
  13.8 0.7 pair_merge.1
  14.6 0.0 copy-start.10
  14.6 0.0 copy-start.11
  14.6 0.9 %collective-permute-start.8 = (bf16[2,272,2048]{2,1,0:T(8,128)(2,1)S(1)}, bf16[2,272,2048]{2,1,0:T(8,128)(2,1)S(1)}, u32[]{:S(2)}, u32[]{:S(2)}) collective-permute-start(bf16[2,272,2048]{2,1,0:T(8,128)(2,1)S(1)} %get-tuple-element.72), channel_id=1, source_target_pairs={{8,24},{20,4},{9,25},{21,5},{10,26},{22,6},{11,27},{23,7}} | collective-permute-start | bytes 6684680 | tf_op jit(solution)/shard_map/ppermute | solution.py:743
  15.5 6.0 %collective-permute-start.6 = (bf16[2,272,2048]{2,1,0:T(8,128)(2,1)S(1)}, bf16[2,272,2048]{2,1,0:T(8,128)(2,1)S(1)}, u32[]{:S(2)}, u32[]{:S(2)}) collective-permute-start(bf16[2,272,2048]{2,1,0:T(8,128)(2,1)S(1)} %get-tuple-element.72), channel_id=1, source_target_pairs={{0,8},{12,4},{16,24},{28,20},{1,9},{13,5},{17,25},{29,21},{2,10},{... | collective-permute-start | bytes 6684680 | tf_op jit(solution)/shard_map/ppermute | solution.py:743
  21.6 1.6 %collective-permute-start.10 = (bf16[2,272,2048]{2,1,0:T(8,128)(2,1)S(1)}, bf16[2,272,2048]{2,1,0:T(8,128)(2,1)S(1)}, u32[]{:S(2)}, u32[]{:S(2)}) collective-permute-start(bf16[2,272,2048]{2,1,0:T(8,128)(2,1)S(1)} %get-tuple-element.72), channel_id=1, source_target_pairs={{0,16},{28,12},{1,17},{29,13},{2,18},{30,14},{3,19},{31,15}} | collective-permute-start | bytes 6684680 | tf_op jit(solution)/shard_map/ppermute | solution.py:743
  23.2 0.1 collective-permute-start.3
  23.3 0.5 collective-permute-start.4
  23.8 0.9 collective-permute-done.3.refs_5_
  24.6 0.1 collective-permute-start.5
  24.8 3.9 %inside_chunk.1 = (bf16[128,4096]{1,0:T(8,128)(2,1)S(1)}, bf16[128,4096]{1,0:T(8,128)(2,1)S(1)}, f32[2,128,256]{2,1,0:T(8,128)S(1)}, f32[3,128,64]{2,1,0:T(8,128)S(1)}) custom-call(bf16[128,4096]{1,0:T(8,128)(2,1)S(1)} %copy-done, bf16[128,4096]{1,0:T(8,128)(2,1)S(1)} %copy-done.1, bf16[128,256]{1,0:T(8,128)(2,1)S(1)} %copy-done.8, ...), custom_call_target="tpu_custom_call" | custom-call | flops 1 | bytes 1 | tf_op jit(solution)/shard_map/inside_chunk/pallas_call | solution.py:339
  28.8 0.0 copy-start.4
  28.8 1.0 %copy-done.4 = bf16[128,4096]{1,0:T(8,128)(2,1)} copy-done((bf16[128,4096]{1,0:T(8,128)(2,1)}, bf16[128,4096]{1,0:T(8,128)(2,1)S(1)}, u32[]{:S(2)}) %copy-start.4) | copy-done | bytes 1048600
  29.7 1.0 %copy-done.6 = bf16[128,4096]{1,0:T(8,128)(2,1)} copy-done((bf16[128,4096]{1,0:T(8,128)(2,1)}, bf16[128,4096]{1,0:T(8,128)(2,1)S(1)}, u32[]{:S(2)}) %copy-start.6) | copy-done | bytes 1048600
  30.7 0.0 collective-permute-done.4.refs_8_
  30.7 0.0 collective-permute-done.5.refs_9_
  30.7 8.9 %packed_attention.1 = (bf16[128,2048]{1,0:T(8,128)(2,1)}, bf16[128,2048]{1,0:T(8,128)(2,1)}, f32[128,512]{1,0:T(8,128)S(1)}, bf16[1,2,128,512]{3,2,1,0:T(8,128)(...) custom-call(s32[1]{0:T(128)} %bitcast.1.kind.refs_0_.core, ...), custom_call_target="tpu_custom_call" | custom-call | flops 1 | bytes 1 | tf_op jit(solution)/shard_map/packed_attention/pallas_call | solution.py:707
  39.7 0.7 copy-done.15
  40.4 0.7 collective-permute-start.7
  41.1 0.0 collective-permute-done.8.refs_3_
  41.1 0.1 slice_bitcast_fusion
  41.2 0.7 collective-permute-start.9
  42.0 3.8 %collective-permute-done.6.refs_1_ = bf16[2,272,2048]{2,1,0:T(8,128)(2,1)S(1)} collective-permute-done((bf16[2,272,2048]{2,1,0:T(8,128)(2,1)S(1)}, bf16[2,272,2048]{2,1,0:T(8,128)(2,1)S(1)}, u32[]{:S(2)}, u32[]{:S(2)}) %collective-permute-start.6) | collective-permute-done | bytes 2228256 | tf_op jit(solution)/shard_map/ppermute | solution.py:743
  45.8 2.7 %collective-permute-start.11 = (bf16[1,2,128,512]{3,2,1,0:T(8,128)(2,1)S(1)}, bf16[1,2,128,512]{3,2,1,0:T(8,128)(2,1)S(1)}, u32[]{:S(2)}, u32[]{:S(2)}) collective-permute-start(bf16[1,2,128,512]{3,2,1,0:T(8,128)(2,1)S(1)} %get-tuple-element.86), channel_id=1, source_target_pairs={{0,4},{4,0},{8,12},{12,8},{16,20},{20,16},{24,28},{28,24},{1,5},{5... | collective-permute-start | bytes 786440 | tf_op jit(solution)/shard_map/ppermute | solution.py:737
  48.5 1.2 %collective-permute-done.11 = bf16[1,2,128,512]{3,2,1,0:T(8,128)(2,1)S(1)} collective-permute-done((bf16[1,2,128,512]{3,2,1,0:T(8,128)(2,1)S(1)}, bf16[1,2,128,512]{3,2,1,0:T(8,128)(2,1)S(1)}, u32[]{:S(2)}, u32[]{:S(2)}) %collective-permute-start.11) | collective-permute-done | bytes 262176 | tf_op jit(solution)/shard_map/ppermute | solution.py:737
  49.7 0.8 add_convert_fusion
  50.5 0.0 collective-permute-done.7.refs_2_
  50.5 8.7 %collective-permute-done.10.refs_4_ = bf16[2,272,2048]{2,1,0:T(8,128)(2,1)S(1)} collective-permute-done((bf16[2,272,2048]{2,1,0:T(8,128)(2,1)S(1)}, bf16[2,272,2048]{2,1,0:T(8,128)(2,1)S(1)}, u32[]{:S(2)}, u32[]{:S(2)}) %collective-permute-start.10) | collective-permute-done | bytes 2228256 | tf_op jit(solution)/shard_map/ppermute | solution.py:743
  59.2 0.0 collective-permute-done.9.refs_2_
  59.2 1.7 %carry_states.3 = (bf16[272,2048]{1,0:T(8,128)(2,1)S(1)}, bf16[272,2048]{1,0:T(8,128)(2,1)}) custom-call(bf16[272,4096]{1,0:T(8,128)(2,1)S(1)} %chunk_states.3.mine.refs_0_, bf16[2,272,2048]{2,1,0:T(8,128)(2,1)S(1)} %collective-permute-done.6.refs_1_, bf16[272,2048]{1,0:T(8,128)(2,1)S(1)} %collective-permute-done.7.refs_2_, ...), custom_call_target="tpu_custom_call" | custom-call | flops 1 | bytes 1 | tf_op jit(solution)/shard_map/carry_states/pallas_call | solution.py:257
  60.9 0.2 collective-permute-start.12
  61.1 1.7 %carry_states.2 = (bf16[272,2048]{1,0:T(8,128)(2,1)S(1)}, bf16[272,2048]{1,0:T(8,128)(2,1)}) custom-call(bf16[272,4096]{1,0:T(8,128)(2,1)S(1)} %chunk_states.3.mine.refs_0_, bf16[2,272,2048]{2,1,0:T(8,128)(2,1)S(1)} %collective-permute-done.6.refs_1_, bf16[272,2048]{1,0:T(8,128)(2,1)S(1)} %collective-permute-done.9.refs_2_, ...), custom_call_target="tpu_custom_call" | custom-call | flops 1 | bytes 1 | tf_op jit(solution)/shard_map/carry_states/pallas_call | solution.py:257
  62.8 1.0 %copy-done.2 = bf16[272,2048]{1,0:T(8,128)(2,1)} copy-done((bf16[272,2048]{1,0:T(8,128)(2,1)}, bf16[272,2048]{1,0:T(8,128)(2,1)S(1)}, u32[]{:S(2)}) %copy-start.2) | copy-done | bytes 1114136
  63.8 0.4 collective-permute-start.13
  64.2 4.0 %collective-permute-start.15 = (bf16[2,128,512]{2,1,0:T(8,128)(2,1)}, bf16[2,128,512]{2,1,0:T(8,128)(2,1)S(1)}, u32[]{:S(2)}, u32[]{:S(2)}) collective-permute-start(bf16[2,128,512]{2,1,0:T(8,128)(2,1)} %bitcast.6), channel_id=1, source_target_pairs={{8,0},{16,8},{20,4},{24,16},{28,12},{9,1},{17,9},{21,5},{25,17},{2... | collective-permute-start | bytes 786440 | tf_op jit(solution)/shard_map/ppermute | solution.py:743
  68.3 2.0 %across_sums.2.refs_5_ = f32[2,128,256]{2,1,0:T(8,128)S(1)} custom-call(s32[1]{0:T(128)} %bitcast.1.kind.refs_0_.core, bf16[128,4096]{1,0:T(8,128)(2,1)} %x.7, bf16[128,4096]{1,0:T(8,128)(2,1)} %dy.7, f32[3,128,64]{2,1,0:T(8,128)S(1)} %get-tuple-element.79.refs_3_.decays, bf16[272,2048]{1,0:T(8,128)(2,1)S(1)} %get-tuple-element.94.refs_4_, ...), custom_call_target="tpu_custom_call" | custom-call | flops 1 | bytes 1 | tf_op jit(solution)/shard_map/across_sums/pallas_call | solution.py:413
  70.4 2.0 %across_sums.3.acc_in = f32[2,128,256]{2,1,0:T(8,128)S(1)} custom-call(s32[1]{0:T(128)} %bitcast.1.kind.refs_0_.core, bf16[128,4096]{1,0:T(8,128)(2,1)} %x.7, bf16[128,4096]{1,0:T(8,128)(2,1)} %dy.7, f32[3,128,64]{2,1,0:T(8,128)S(1)} %get-tuple-element.79.refs_3_.decays, bf16[272,2048]{1,0:T(8,128)(2,1)S(1)} %copy-done.3, f32[2,128,256]{2,1,0:T(8,128)S(1)} %across_sums.2.refs_5_), custom_call_target="tpu_custom_call" | custom-call | flops 1 | bytes 1 | tf_op jit(solution)/shard_map/across_sums/pallas_call | solution.py:413
  72.3 0.0 collective-permute-done.12.low.refs_5_
  72.3 0.0 collective-permute-done.13.high.refs_5_
  72.3 0.0 copy-start.5
  72.3 0.0 copy-start.7
  72.4 3.0 %given_sums.1 = (f32[2,64,256]{2,1,0:T(8,128)S(1)}, bf16[2,64,256]{2,1,0:T(8,128)(2,1)S(1)}) custom-call(s32[1]{0:T(128)S(6)} %sub.8.kind.other, s32[1]{0:T(128)} %bitcast.4.side, bf16[128,4096]{1,0:T(8,128)(2,1)} %x.7, bf16[128,4096]{1,0:T(8,128)(2,1)} %dy.7, f32[3,128,64]{2,1,0:T(8,128)S(1)} %get-tuple-element.79.refs_3_.decays, ...), custom_call_target="tpu_custom_call" | custom-call | flops 1 | bytes 1 | tf_op jit(solution)/shard_map/given_sums/pallas_call | solution.py:468
  75.4 0.1 collective-permute-start.14
  75.5 1.8 %across_outputs.2 = (bf16[128,4096]{1,0:T(8,128)(2,1)}, bf16[128,4096]{1,0:T(8,128)(2,1)}) custom-call(s32[1]{0:T(128)} %bitcast.1.kind.refs_0_.core, bf16[128,256]{1,0:T(8,128)(2,1)S(1)} %copy-done.8, bf16[128,256]{1,0:T(8,128)(2,1)S(1)} %copy-done.9, f32[3,128,64]{2,1,0:T(8,128)S(1)} %get-tuple-element.79.refs_3_.decays, ...), custom_call_target="tpu_custom_call" | custom-call | flops 1 | bytes 1 | tf_op jit(solution)/shard_map/across_outputs/pallas_call | solution.py:547
  77.3 2.2 %collective-permute-done.14.moved = bf16[2,64,256]{2,1,0:T(8,128)(2,1)S(1)} collective-permute-done((bf16[2,64,256]{2,1,0:T(8,128)(2,1)S(1)}, bf16[2,64,256]{2,1,0:T(8,128)(2,1)S(1)}, u32[]{:S(2)}, u32[]{:S(2)}) %collective-permute-start.14) | collective-permute-done | bytes 65568 | tf_op jit(solution)/shard_map/ppermute | solution.py:857
  79.6 2.5 %collective-permute-start.17 = (bf16[128,512]{1,0:T(8,128)(2,1)S(1)}, bf16[128,512]{1,0:T(8,128)(2,1)S(1)}, u32[]{:S(2)}, u32[]{:S(2)}) collective-permute-start(bf16[128,512]{1,0:T(8,128)(2,1)S(1)} %partner_part.1), channel_id=1, source_target_pairs={{0,4},{4,0},{8,12},{12,8},{16,20},{20,16},{24,28},{28,24},{1,5},{5... | collective-permute-start | bytes 393224 | tf_op jit(solution)/shard_map/ppermute | solution.py:737
  82.1 1.9 %collective-permute-start.16 = (bf16[2,32,256]{2,1,0:T(8,128)(2,1)S(1)}, bf16[2,32,256]{2,1,0:T(8,128)(2,1)S(1)}, u32[]{:S(2)}, u32[]{:S(2)}) collective-permute-start(bf16[2,32,256]{2,1,0:T(8,128)(2,1)S(1)} %get-tuple-element.107), channel_id=1, source_target_pairs={{0,1},{1,0},{2,3},{3,2},{4,5},{5,4},{6,7},{7,6},{8,9},{9,8},{10,11... | collective-permute-start | bytes 98312 | tf_op jit(solution)/shard_map/ppermute | solution.py:857
  84.0 2.9 %across_outputs.3 = (bf16[128,4096]{1,0:T(8,128)(2,1)}, bf16[128,4096]{1,0:T(8,128)(2,1)}) custom-call(s32[1]{0:T(128)} %bitcast.1.kind.refs_0_.core, bf16[128,256]{1,0:T(8,128)(2,1)S(1)} %copy-done.8, bf16[128,256]{1,0:T(8,128)(2,1)S(1)} %copy-done.9, ...), custom_call_target="tpu_custom_call", output_to_operand_aliasing={{0}: (8, {}), {1}: (9, {})} | custom-call | flops 1 | bytes 1 | tf_op jit(solution)/shard_map/across_outputs/pallas_call | solution.py:547
  86.8 0.0 collective-permute-done.16.moved
  86.9 0.7 last_sums.1
  (25 shorter events, 0.1 us)
Async XLA Ops:
  4.5 9.4 %collective-permute-start.2 = (bf16[272,4096]{1,0:T(8,128)(2,1)S(1)}, bf16[272,4096]{1,0:T(8,128)(2,1)S(1)}, u32[]{:S(2)}, u32[]{:S(2)}) collective-permute-start(bf16[272,4096]{1,0:T(8,128)(2,1)S(1)} %get-tuple-element.71), channel_id=1, source_target_pairs={{0,4},{4,0},{8,12},{12,8},{16,20},{20,16},{24,28},{28,24},{1,5},{5... | collective-permute-start | bytes 6684680 | tf_op jit(solution)/shard_map/ppermute | solution.py:737
  5.2 7.3 %collective-permute-start = (bf16[144,512]{1,0:T(8,128)(2,1)S(1)}, bf16[144,512]{1,0:T(8,128)(2,1)S(1)}, u32[]{:S(2)}, u32[]{:S(2)}) collective-permute-start(bf16[144,512]{1,0:T(8,128)(2,1)S(1)} %get-tuple-element.69.refs_4_), channel_id=1, source_target_pairs={{0,8},{4,12},{8,16},{12,20},{16,24},{20,28},{1,9},{5,13},{9,17},{1... | collective-permute-start | bytes 442376 | tf_op jit(solution)/shard_map/ppermute | solution.py:732
  6.5 7.4 %collective-permute-start.1 = (bf16[144,512]{1,0:T(8,128)(2,1)S(1)}, bf16[144,512]{1,0:T(8,128)(2,1)S(1)}, u32[]{:S(2)}, u32[]{:S(2)}) collective-permute-start(bf16[144,512]{1,0:T(8,128)(2,1)S(1)} %get-tuple-element.69.refs_4_), channel_id=1, source_target_pairs={{0,16},{4,20},{8,24},{12,28},{1,17},{5,21},{9,25},{13,29},{2,18},{... | collective-permute-start | bytes 442376 | tf_op jit(solution)/shard_map/ppermute | solution.py:732
  11.6 13.2 %copy-start = (bf16[128,4096]{1,0:T(8,128)(2,1)S(1)}, bf16[128,4096]{1,0:T(8,128)(2,1)}, u32[]{:S(2)}) copy-start(bf16[128,4096]{1,0:T(8,128)(2,1)} %x.7) | copy-start | bytes 3145732
  11.6 13.2 %copy-start.1 = (bf16[128,4096]{1,0:T(8,128)(2,1)S(1)}, bf16[128,4096]{1,0:T(8,128)(2,1)}, u32[]{:S(2)}) copy-start(bf16[128,4096]{1,0:T(8,128)(2,1)} %dy.7) | copy-start | bytes 3145732
  11.6 13.2 %copy-start.8 = (bf16[128,256]{1,0:T(8,128)(2,1)S(1)}, bf16[128,256]{1,0:T(8,128)(2,1)}, u32[]{:S(2)}) copy-start(bf16[128,256]{1,0:T(8,128)(2,1)} %refs_1_.11) | copy-start | bytes 196612
  11.6 13.2 %copy-start.9 = (bf16[128,256]{1,0:T(8,128)(2,1)S(1)}, bf16[128,256]{1,0:T(8,128)(2,1)}, u32[]{:S(2)}) copy-start(bf16[128,256]{1,0:T(8,128)(2,1)} %refs_2_.9) | copy-start | bytes 196612
  11.6 13.2 %copy-start.12 = (f32[128,64]{0,1:T(8,128)S(1)}, f32[128,64]{0,1:T(8,128)}, u32[]{:S(2)}) copy-start(f32[128,64]{0,1:T(8,128)} %param.18) | copy-start | bytes 98308
  11.6 13.1 %copy-start.17 = (s32[128]{0:T(128)S(1)}, s32[128]{0:T(128)}, u32[]{:S(2)}) copy-start(s32[128]{0:T(128)} %param.14) | copy-start | bytes 1540
  14.6 16.2 %copy-start.10 = (bf16[128,2048]{1,0:T(8,128)(2,1)S(1)}, bf16[128,2048]{1,0:T(8,128)(2,1)}, u32[]{:S(2)}) copy-start(bf16[128,2048]{1,0:T(8,128)(2,1)} %refs_1_.7) | copy-start | bytes 1572868
  14.6 16.1 %copy-start.11 = (bf16[128,2048]{1,0:T(8,128)(2,1)S(1)}, bf16[128,2048]{1,0:T(8,128)(2,1)}, u32[]{:S(2)}) copy-start(bf16[128,2048]{1,0:T(8,128)(2,1)} %refs_2_.5) | copy-start | bytes 1572868
  14.6 26.5 %collective-permute-start.8 = (bf16[2,272,2048]{2,1,0:T(8,128)(2,1)S(1)}, bf16[2,272,2048]{2,1,0:T(8,128)(2,1)S(1)}, u32[]{:S(2)}, u32[]{:S(2)}) collective-permute-start(bf16[2,272,2048]{2,1,0:T(8,128)(2,1)S(1)} %get-tuple-element.72), channel_id=1, source_target_pairs={{8,24},{20,4},{9,25},{21,5},{10,26},{22,6},{11,27},{23,7}} | collective-permute-start | bytes 6684680 | tf_op jit(solution)/shard_map/ppermute | solution.py:743
  15.5 30.3 %collective-permute-start.6 = (bf16[2,272,2048]{2,1,0:T(8,128)(2,1)S(1)}, bf16[2,272,2048]{2,1,0:T(8,128)(2,1)S(1)}, u32[]{:S(2)}, u32[]{:S(2)}) collective-permute-start(bf16[2,272,2048]{2,1,0:T(8,128)(2,1)S(1)} %get-tuple-element.72), channel_id=1, source_target_pairs={{0,8},{12,4},{16,24},{28,20},{1,9},{13,5},{17,25},{29,21},{2,10},{... | collective-permute-start | bytes 6684680 | tf_op jit(solution)/shard_map/ppermute | solution.py:743
  21.6 37.6 %collective-permute-start.10 = (bf16[2,272,2048]{2,1,0:T(8,128)(2,1)S(1)}, bf16[2,272,2048]{2,1,0:T(8,128)(2,1)S(1)}, u32[]{:S(2)}, u32[]{:S(2)}) collective-permute-start(bf16[2,272,2048]{2,1,0:T(8,128)(2,1)S(1)} %get-tuple-element.72), channel_id=1, source_target_pairs={{0,16},{28,12},{1,17},{29,13},{2,18},{30,14},{3,19},{31,15}} | collective-permute-start | bytes 6684680 | tf_op jit(solution)/shard_map/ppermute | solution.py:743
  23.2 1.4 %collective-permute-start.3 = (bf16[144,512]{1,0:T(8,128)(2,1)S(1)}, bf16[144,512]{1,0:T(8,128)(2,1)S(1)}, u32[]{:S(2)}, u32[]{:S(2)}) collective-permute-start(bf16[144,512]{1,0:T(8,128)(2,1)S(1)} %get-tuple-element.69.refs_4_), channel_id=1, source_target_pairs={{0,4},{4,0},{8,12},{12,8},{16,20},{20,16},{24,28},{28,24},{1,5},{5... | collective-permute-start | bytes 442376 | tf_op jit(solution)/shard_map/ppermute | solution.py:737
  23.3 7.4 %collective-permute-start.4 = (bf16[144,512]{1,0:T(8,128)(2,1)S(1)}, bf16[144,512]{1,0:T(8,128)(2,1)S(1)}, u32[]{:S(2)}, u32[]{:S(2)}) collective-permute-start(bf16[144,512]{1,0:T(8,128)(2,1)S(1)} %collective-permute-done.refs_6_), channel_id=1, source_target_pairs={{0,4},{4,0},{8,12},{12,8},{16,20},{20,16},{24,28},{28,24},{1,5},{5... | collective-permute-start | bytes 442376 | tf_op jit(solution)/shard_map/ppermute | solution.py:737
  24.6 6.1 %collective-permute-start.5 = (bf16[144,512]{1,0:T(8,128)(2,1)S(1)}, bf16[144,512]{1,0:T(8,128)(2,1)S(1)}, u32[]{:S(2)}, u32[]{:S(2)}) collective-permute-start(bf16[144,512]{1,0:T(8,128)(2,1)S(1)} %collective-permute-done.1.refs_7_), channel_id=1, source_target_pairs={{0,4},{4,0},{8,12},{12,8},{16,20},{20,16},{24,28},{28,24},{1,5},{5... | collective-permute-start | bytes 442376 | tf_op jit(solution)/shard_map/ppermute | solution.py:737
  28.8 1.0 %copy-start.4 = (bf16[128,4096]{1,0:T(8,128)(2,1)}, bf16[128,4096]{1,0:T(8,128)(2,1)S(1)}, u32[]{:S(2)}) copy-start(bf16[128,4096]{1,0:T(8,128)(2,1)S(1)} %get-tuple-element.101.refs_6_) | copy-start | bytes 3145732
  29.7 1.0 %copy-start.6 = (bf16[128,4096]{1,0:T(8,128)(2,1)}, bf16[128,4096]{1,0:T(8,128)(2,1)S(1)}, u32[]{:S(2)}) copy-start(bf16[128,4096]{1,0:T(8,128)(2,1)S(1)} %get-tuple-element.102.refs_7_) | copy-start | bytes 3145732
  30.7 9.7 %copy-start.13 = (f32[2,128,256]{2,1,0:T(8,128)}, f32[2,128,256]{2,1,0:T(8,128)S(1)}, u32[]{:S(2)}) copy-start(f32[2,128,256]{2,1,0:T(8,128)S(1)} %get-tuple-element.95.refs_5_) | copy-start | bytes 786436
  39.7 0.7 copy-start.15
  40.4 10.1 %collective-permute-start.7 = (bf16[272,2048]{1,0:T(8,128)(2,1)S(1)}, bf16[272,2048]{1,0:T(8,128)(2,1)S(1)}, u32[]{:S(2)}, u32[]{:S(2)}) collective-permute-start(bf16[272,2048]{1,0:T(8,128)(2,1)S(1)} %get-tuple-element.84), channel_id=1, source_target_pairs={{8,16},{20,12},{9,17},{21,13},{10,18},{22,14},{11,19},{23,15}} | collective-permute-start | bytes 3342344 | tf_op jit(solution)/shard_map/ppermute | solution.py:743
  41.2 17.9 %collective-permute-start.9 = (bf16[272,2048]{1,0:T(8,128)(2,1)S(1)}, bf16[272,2048]{1,0:T(8,128)(2,1)S(1)}, u32[]{:S(2)}, u32[]{:S(2)}) collective-permute-start(bf16[272,2048]{1,0:T(8,128)(2,1)S(1)} %slice_bitcast_fusion), channel_id=1, source_target_pairs={{4,12},{24,16},{5,13},{25,17},{6,14},{26,18},{7,15},{27,19}} | collective-permute-start | bytes 3342344 | tf_op jit(solution)/shard_map/ppermute | solution.py:743
  45.8 3.9 %collective-permute-start.11 = (bf16[1,2,128,512]{3,2,1,0:T(8,128)(2,1)S(1)}, bf16[1,2,128,512]{3,2,1,0:T(8,128)(2,1)S(1)}, u32[]{:S(2)}, u32[]{:S(2)}) collective-permute-start(bf16[1,2,128,512]{3,2,1,0:T(8,128)(2,1)S(1)} %get-tuple-element.86), channel_id=1, source_target_pairs={{0,4},{4,0},{8,12},{12,8},{16,20},{20,16},{24,28},{28,24},{1,5},{5... | collective-permute-start | bytes 786440 | tf_op jit(solution)/shard_map/ppermute | solution.py:737
  60.9 7.4 %copy-start.14 = (f32[2,128,256]{2,1,0:T(8,128)S(1)}, f32[2,128,256]{2,1,0:T(8,128)}, u32[]{:S(2)}) copy-start(f32[2,128,256]{2,1,0:T(8,128)} %copy-done.13) | copy-start | bytes 786436
  60.9 11.4 %collective-permute-start.12 = (bf16[272,2048]{1,0:T(8,128)(2,1)}, bf16[272,2048]{1,0:T(8,128)(2,1)S(1)}, u32[]{:S(2)}, u32[]{:S(2)}) collective-permute-start(bf16[272,2048]{1,0:T(8,128)(2,1)} %get-tuple-element.96), channel_id=1, source_target_pairs={{0,4},{4,0},{8,12},{12,8},{16,20},{20,16},{24,28},{28,24},{1,5},{5... | collective-permute-start | bytes 3342344 | tf_op jit(solution)/shard_map/ppermute | solution.py:737
  62.8 1.0 %copy-start.2 = (bf16[272,2048]{1,0:T(8,128)(2,1)}, bf16[272,2048]{1,0:T(8,128)(2,1)S(1)}, u32[]{:S(2)}) copy-start(bf16[272,2048]{1,0:T(8,128)(2,1)S(1)} %get-tuple-element.92.refs_4_) | copy-start | bytes 3342340
  63.8 8.5 %collective-permute-start.13 = (bf16[272,2048]{1,0:T(8,128)(2,1)}, bf16[272,2048]{1,0:T(8,128)(2,1)}, u32[]{:S(2)}, u32[]{:S(2)}) collective-permute-start(bf16[272,2048]{1,0:T(8,128)(2,1)} %get-tuple-element.97), channel_id=1, source_target_pairs={{0,4},{4,0},{8,12},{12,8},{16,20},{20,16},{24,28},{28,24},{1,5},{5... | collective-permute-start | bytes 3342344 | tf_op jit(solution)/shard_map/ppermute | solution.py:737
  64.2 13.1 %collective-permute-start.15 = (bf16[2,128,512]{2,1,0:T(8,128)(2,1)}, bf16[2,128,512]{2,1,0:T(8,128)(2,1)S(1)}, u32[]{:S(2)}, u32[]{:S(2)}) collective-permute-start(bf16[2,128,512]{2,1,0:T(8,128)(2,1)} %bitcast.6), channel_id=1, source_target_pairs={{8,0},{16,8},{20,4},{24,16},{28,12},{9,1},{17,9},{21,5},{25,17},{2... | collective-permute-start | bytes 786440 | tf_op jit(solution)/shard_map/ppermute | solution.py:743
  68.3 2.1 %copy-start.3 = (bf16[272,2048]{1,0:T(8,128)(2,1)S(1)}, bf16[272,2048]{1,0:T(8,128)(2,1)}, u32[]{:S(2)}) copy-start(bf16[272,2048]{1,0:T(8,128)(2,1)} %copy-done.2) | copy-start | bytes 3342340
  72.3 3.2 %copy-start.5 = (bf16[128,4096]{1,0:T(8,128)(2,1)S(1)}, bf16[128,4096]{1,0:T(8,128)(2,1)}, u32[]{:S(2)}) copy-start(bf16[128,4096]{1,0:T(8,128)(2,1)} %copy-done.4) | copy-start | bytes 3145732
  72.3 3.2 %copy-start.7 = (bf16[128,4096]{1,0:T(8,128)(2,1)S(1)}, bf16[128,4096]{1,0:T(8,128)(2,1)}, u32[]{:S(2)}) copy-start(bf16[128,4096]{1,0:T(8,128)(2,1)} %copy-done.6) | copy-start | bytes 3145732
  75.4 4.1 %collective-permute-start.14 = (bf16[2,64,256]{2,1,0:T(8,128)(2,1)S(1)}, bf16[2,64,256]{2,1,0:T(8,128)(2,1)S(1)}, u32[]{:S(2)}, u32[]{:S(2)}) collective-permute-start(bf16[2,64,256]{2,1,0:T(8,128)(2,1)S(1)} %get-tuple-element.99), channel_id=1, source_target_pairs={{0,2},{1,3},{2,0},{3,1},{4,6},{5,7},{6,4},{7,5},{8,10},{9,11},{10,... | collective-permute-start | bytes 196616 | tf_op jit(solution)/shard_map/ppermute | solution.py:857
  79.6 7.3 %collective-permute-start.17 = (bf16[128,512]{1,0:T(8,128)(2,1)S(1)}, bf16[128,512]{1,0:T(8,128)(2,1)S(1)}, u32[]{:S(2)}, u32[]{:S(2)}) collective-permute-start(bf16[128,512]{1,0:T(8,128)(2,1)S(1)} %partner_part.1), channel_id=1, source_target_pairs={{0,4},{4,0},{8,12},{12,8},{16,20},{20,16},{24,28},{28,24},{1,5},{5... | collective-permute-start | bytes 393224 | tf_op jit(solution)/shard_map/ppermute | solution.py:737
  82.1 4.7 %collective-permute-start.16 = (bf16[2,32,256]{2,1,0:T(8,128)(2,1)S(1)}, bf16[2,32,256]{2,1,0:T(8,128)(2,1)S(1)}, u32[]{:S(2)}, u32[]{:S(2)}) collective-permute-start(bf16[2,32,256]{2,1,0:T(8,128)(2,1)S(1)} %get-tuple-element.107), channel_id=1, source_target_pairs={{0,1},{1,0},{2,3},{3,2},{4,5},{5,4},{6,7},{7,6},{8,9},{9,8},{10,11... | collective-permute-start | bytes 98312 | tf_op jit(solution)/shard_map/ppermute | solution.py:857
  84.0 2.9 %copy-start.16 = (f32[128,512]{1,0:T(8,128)S(1)}, f32[128,512]{1,0:T(8,128)}, u32[]{:S(2)}) copy-start(f32[128,512]{1,0:T(8,128)} %copy-done.15) | copy-start | bytes 786436

commit v3 on v2

--- a/solution.py
+++ b/solution.py
@@ -373,24 +373,24 @@
     return copies[0]
 
 
-def sums_kernel(half, kind, x, dy, decays, carried, acc_in, acc, z_in, sems):
+def sums_kernel(kind, x, dy, decays, low, high, acc_in, acc, z_in, sems):
     heads = decays.shape[2]
-    cols = carried.shape[1]
-    part = min(cols, 2 * WIDTH)
+    cols = x.shape[1]
+    part = min(cols // 2, 2 * WIDTH)
     forward = kind[0] == 0
     waits = []
     for n in range(cols // part):
-        source = [a.at[:, pl.ds(half * cols + n * part, part)] for a in (x, dy)]
-        waits.append(begin(forward, *source, z_in.at[:, pl.ds(n * part, part)], sems.at[n]))
-    weight = carried_weight(forward, carried, decays)
+        piece = (slice(None), pl.ds(n * part, part))
+        waits.append(begin(forward, x.at[piece], dy.at[piece], z_in.at[piece], sems.at[n]))
+    weight = carried_weight(forward, low, decays)
     total = 0.0
     for t in range(cols // WIDTH):
         if t * WIDTH % part == 0:
             waits[t * WIDTH // part].wait()
-        at = slice(t * WIDTH, (t + 1) * WIDTH)
-        e = spread(heads, half * (heads // 2) + t * GROUP)
-        z = (z_in[:, at].astype(F32) * dot(weight, e)).astype(BF16)
-        total = total + dot_nt(z, carried[:N, at])
+        half, first = t * WIDTH // (cols // 2), t * WIDTH % (cols // 2)
+        z = z_in[:, t * WIDTH : (t + 1) * WIDTH].astype(F32)
+        z = (z * dot(weight, spread(heads, t * GROUP))).astype(BF16)
+        total = total + dot_nt(z, (low, high)[half][:N, first : first + WIDTH])
     acc[0] = acc_in[0] + jnp.where(forward, 0.0, total)
     acc[1] = acc_in[1] + jnp.where(forward, total, 0.0)
 
@@ -406,23 +406,17 @@
     return [jax.ShapeDtypeStruct(shape, F32), jax.ShapeDtypeStruct(shape, BF16)]
 
 
-def across_sums(half, kind, x, dy, decays, carried, acc):
-    def kernel(*refs):
-        sums_kernel(half, *refs)
-
-    return pl.pallas_call(
-        kernel,
-        in_specs=[SCALAR, ANYWHERE, ANYWHERE, WHOLE, WHOLE, WHOLE],
+def across_sums(kind, x, dy, decays, low, high, acc):
+    return pl.pallas_call(
+        sums_kernel,
+        in_specs=[SCALAR, ANYWHERE, ANYWHERE] + [WHOLE] * 4,
         out_specs=WHOLE,
         out_shape=jax.ShapeDtypeStruct(acc.shape, F32),
-        scratch_shapes=[
-            pltpu.VMEM((x.shape[0], carried.shape[1]), BF16),
-            pltpu.SemaphoreType.DMA((4,)),
-        ],
-        compiler_params=params(5),
+        scratch_shapes=[pltpu.VMEM(x.shape, BF16), pltpu.SemaphoreType.DMA((8,))],
+        compiler_params=params(7),
         cost_estimate=BRIEF,
         name="across_sums",
-    )(kind, x, dy, decays, carried, acc)
+    )(kind, x, dy, decays, low, high, acc)
 
 
 def fetch_given(sources, buffer, sems):
@@ -833,8 +827,7 @@
     keep_low, give_low = carries(0, mine, near, straight, others)
     keep, give = carries(1, mine, near, relayed, others)
     given_low, given = swap(give_low), swap(give)
-    acc = across_sums(0, core, *pinned[:2], decays, keep_low, acc)
-    acc = across_sums(1, core, *pinned[:2], decays, keep, acc)
+    acc = across_sums(core, *pinned[:2], decays, keep_low, keep, acc)
 
     def outputs(half, after, keep, given, done=()):
         _, core_then = lax.optimization_barrier((after, core))

time: 87.9 us -> 89 us (1.013)
  local copies, waits for them, and re-layouts: 3.82 us -> 5.16 us
    unnamed x36 -> x40, local copies, waits for them, and re-layouts: 3.71 us -> 5.05 us
    pallas_call x2 -> x1, Pallas kernels: 4 us -> 2.71 us  [across_sums(): pl.pallas_call(sums_kernel, in_specs=[SCALAR, ANYWHERE, ANYWHERE] + [WHOL...]
    ppermute x8, starting transfers between devices: 7.22 us -> 5.94 us  [swap(): return lax.ppermute(x, 'ctx', [(i, i ^ 1) for i in range(count)])]
    pallas_call x1, Pallas kernels: 0.69 us -> 1.64 us  [finish(): pl.pallas_call(finish_kernel, in_specs=[SCALAR] + [WHOLE] * (4 + len(part...]
    pallas_call x1, Pallas kernels: 0.03 us -> 0.98 us  [partner_part(): pl.pallas_call(partner_kernel, in_specs=[SCALAR] + [WHOLE] * (1 + len(par...]
  transfers between devices with their start and end apart: 18 -> 18, of which waited for: 7 -> 7; matrix products, arithmetic and copies ran while one was open for 1% -> 1% of each run, Pallas kernels for 34% -> 33%
where the time goes in v3:
time: 89 us; the launch traced here: 88.6 us
  Pallas kernels  37.7 us (42%)
  starting transfers between devices  25.1 us (28%)
  waiting for transfers between devices  18.9 us (21%)
  local copies, waits for them, and re-layouts  5.16 us (6%)
  between operations  1.01 us (1%)
    ppermute x6, starting transfers between devices, onward(): lax.ppermute(x, 'ctx', [(i, k) for i, k in hops if 0 <= k < 2 * pairs])  14.5 us
    ppermute x6, waiting for transfers between devices, onward(): lax.ppermute(x, 'ctx', [(i, k) for i, k in hops if 0 <= k < 2 * pairs])  12.5 us
    pallas_call x1, Pallas kernels, attention(): pl.pallas_call(kernel, grid_spec=pltpu.PrefetchScalarGridSpec(num_scalar_...  8.93 us
    pallas_call x2, Pallas kernels, states(): pl.pallas_call(states_kernel, grid_spec=pltpu.PrefetchScalarGridSpec(num_...  7.61 us
    ppermute x8, starting transfers between devices, swap(): return lax.ppermute(x, 'ctx', [(i, i ^ 1) for i in range(count)])  5.94 us
    unnamed x40, local copies, waits for them, and re-layouts  5.05 us
    pallas_call x2, Pallas kernels, across_outputs(): pl.pallas_call(kernel, in_specs=[SCALAR] + [WHOLE] * 4 + [ANYWHERE] + [WH...  4.67 us
    pallas_call x1, Pallas kernels, inside(): pl.pallas_call(inside_kernel, grid=(cols // span,), in_specs=[block, bloc...  3.94 us
  transfers between devices with their start and end apart: 18, of which 7 were waited for; matrix products, arithmetic and copies ran while one was open for 1% of the time, Pallas kernels for 33%

profile of v3, /device:TPU:23, one launch (start us, length us, event | category | flops | bytes accessed | tf_op | source)
XLA Modules:
  0.0 88.6 jit_solution(5557714962021814347)
XLA Ops:
  0.6 3.8 %chunk_states.2 = (bf16[272,4096]{1,0:T(8,128)(2,1)S(1)}, bf16[144,512]{1,0:T(8,128)(2,1)S(1)}) custom-call(s32[1]{0:T(128)S(6)} %sub.8.kind.other, bf16[128,4096]{1,0:T(8,128)(2,1)} %x.9, bf16[128,4096]{1,0:T(8,128)(2,1)} %dy.9, bf16[128,256]{1,0:T(8,128)(2,1)} %refs_1_.7, bf16[128,256]{1,0:T(8,128)(2,1)} %refs_2_.5, f32[64,128]{1,0:T(8,128)} %bitcast.8, ...), custom_call_target="tpu_custom_call" | custom-call | flops 1 | bytes 1 | tf_op jit(solution)/shard_map/chunk_states/pallas_call | solution.py:161
  4.5 0.7 collective-permute-start.2
  5.2 1.3 %collective-permute-start = (bf16[144,512]{1,0:T(8,128)(2,1)S(1)}, bf16[144,512]{1,0:T(8,128)(2,1)S(1)}, u32[]{:S(2)}, u32[]{:S(2)}) collective-permute-start(bf16[144,512]{1,0:T(8,128)(2,1)S(1)} %get-tuple-element.69.refs_4_), channel_id=1, source_target_pairs={{0,8},{4,12},{8,16},{12,20},{16,24},{20,28},{1,9},{5,13},{9,17},{1... | collective-permute-start | bytes 442376 | tf_op jit(solution)/shard_map/ppermute | solution.py:726
  6.5 1.3 %collective-permute-start.1 = (bf16[144,512]{1,0:T(8,128)(2,1)S(1)}, bf16[144,512]{1,0:T(8,128)(2,1)S(1)}, u32[]{:S(2)}, u32[]{:S(2)}) collective-permute-start(bf16[144,512]{1,0:T(8,128)(2,1)S(1)} %get-tuple-element.69.refs_4_), channel_id=1, source_target_pairs={{0,16},{4,20},{8,24},{12,28},{1,17},{5,21},{9,25},{13,29},{2,18},{... | collective-permute-start | bytes 442376 | tf_op jit(solution)/shard_map/ppermute | solution.py:726
  7.8 3.8 %chunk_states.3.mine.refs_0_ = bf16[272,4096]{1,0:T(8,128)(2,1)S(1)} custom-call(s32[1]{0:T(128)} %bitcast.1.kind.refs_0_.core, bf16[128,4096]{1,0:T(8,128)(2,1)} %x.9, bf16[128,4096]{1,0:T(8,128)(2,1)} %dy.9, bf16[128,256]{1,0:T(8,128)(2,1)} %refs_1_.7, bf16[128,256]{1,0:T(8,128)(2,1)} %refs_2_.5, f32[64,128]{1,0:T(8,128)} %bitcast.9, s32[1,128]{1,0:T(1,128)} %bitcast.12), custom_call_target="tpu_custom_call" | custom-call | flops 1 | bytes 1 | tf_op jit(solution)/shard_map/chunk_states/pallas_call | solution.py:161
  11.6 0.0 copy-start
  11.6 0.0 copy-start.1
  11.6 0.0 copy-start.6
  11.6 0.0 copy-start.8
  11.6 0.0 copy-start.12
  11.6 0.0 copy-start.19
  11.7 0.9 collective-permute-done.refs_6_
  12.5 1.3 %collective-permute-done.1.refs_7_ = bf16[144,512]{1,0:T(8,128)(2,1)S(1)} collective-permute-done((bf16[144,512]{1,0:T(8,128)(2,1)S(1)}, bf16[144,512]{1,0:T(8,128)(2,1)S(1)}, u32[]{:S(2)}, u32[]{:S(2)}) %collective-permute-start.1) | collective-permute-done | bytes 147488 | tf_op jit(solution)/shard_map/ppermute | solution.py:726
  13.8 0.0 collective-permute-done.2.got
  13.8 0.7 pair_merge.1
  14.6 0.0 copy-start.10
  14.6 0.0 copy-start.11
  14.6 0.9 %collective-permute-start.8 = (bf16[2,272,2048]{2,1,0:T(8,128)(2,1)S(1)}, bf16[2,272,2048]{2,1,0:T(8,128)(2,1)S(1)}, u32[]{:S(2)}, u32[]{:S(2)}) collective-permute-start(bf16[2,272,2048]{2,1,0:T(8,128)(2,1)S(1)} %get-tuple-element.72), channel_id=1, source_target_pairs={{8,24},{20,4},{9,25},{21,5},{10,26},{22,6},{11,27},{23,7}} | collective-permute-start | bytes 6684680 | tf_op jit(solution)/shard_map/ppermute | solution.py:737
  15.5 6.0 %collective-permute-start.6 = (bf16[2,272,2048]{2,1,0:T(8,128)(2,1)S(1)}, bf16[2,272,2048]{2,1,0:T(8,128)(2,1)S(1)}, u32[]{:S(2)}, u32[]{:S(2)}) collective-permute-start(bf16[2,272,2048]{2,1,0:T(8,128)(2,1)S(1)} %get-tuple-element.72), channel_id=1, source_target_pairs={{0,8},{12,4},{16,24},{28,20},{1,9},{13,5},{17,25},{29,21},{2,10},{... | collective-permute-start | bytes 6684680 | tf_op jit(solution)/shard_map/ppermute | solution.py:737
  21.6 1.6 %collective-permute-start.10 = (bf16[2,272,2048]{2,1,0:T(8,128)(2,1)S(1)}, bf16[2,272,2048]{2,1,0:T(8,128)(2,1)S(1)}, u32[]{:S(2)}, u32[]{:S(2)}) collective-permute-start(bf16[2,272,2048]{2,1,0:T(8,128)(2,1)S(1)} %get-tuple-element.72), channel_id=1, source_target_pairs={{0,16},{28,12},{1,17},{29,13},{2,18},{30,14},{3,19},{31,15}} | collective-permute-start | bytes 6684680 | tf_op jit(solution)/shard_map/ppermute | solution.py:737
  23.2 0.1 collective-permute-start.3
  23.3 0.5 collective-permute-start.4
  23.8 0.9 collective-permute-done.3.refs_5_
  24.6 0.1 collective-permute-start.5
  24.8 3.9 %inside_chunk.1 = (bf16[128,4096]{1,0:T(8,128)(2,1)S(1)}, bf16[128,4096]{1,0:T(8,128)(2,1)S(1)}, f32[2,128,256]{2,1,0:T(8,128)S(1)}, f32[3,128,64]{2,1,0:T(8,128)S(1)}) custom-call(bf16[128,4096]{1,0:T(8,128)(2,1)S(1)} %copy-done, bf16[128,4096]{1,0:T(8,128)(2,1)S(1)} %copy-done.1, bf16[128,256]{1,0:T(8,128)(2,1)S(1)} %copy-done.6, ...), custom_call_target="tpu_custom_call" | custom-call | flops 1 | bytes 1 | tf_op jit(solution)/shard_map/inside_chunk/pallas_call | solution.py:339
  28.8 0.0 copy-start.2
  28.8 1.0 %copy-done.2 = bf16[128,4096]{1,0:T(8,128)(2,1)} copy-done((bf16[128,4096]{1,0:T(8,128)(2,1)}, bf16[128,4096]{1,0:T(8,128)(2,1)S(1)}, u32[]{:S(2)}) %copy-start.2) | copy-done | bytes 1048600
  29.7 1.0 %copy-done.4 = bf16[128,4096]{1,0:T(8,128)(2,1)} copy-done((bf16[128,4096]{1,0:T(8,128)(2,1)}, bf16[128,4096]{1,0:T(8,128)(2,1)S(1)}, u32[]{:S(2)}) %copy-start.4) | copy-done | bytes 1048600
  30.7 0.7 copy-done.15
  31.4 8.9 %packed_attention.1 = (bf16[128,2048]{1,0:T(8,128)(2,1)}, bf16[128,2048]{1,0:T(8,128)(2,1)}, f32[128,512]{1,0:T(8,128)S(1)}, bf16[1,2,128,512]{3,2,1,0:T(8,128)(...) custom-call(s32[1]{0:T(128)} %bitcast.1.kind.refs_0_.core, ...), custom_call_target="tpu_custom_call" | custom-call | flops 1 | bytes 1 | tf_op jit(solution)/shard_map/packed_attention/pallas_call | solution.py:701
  40.4 0.7 copy-done.13
  41.1 0.7 copy-done.17
  41.7 0.7 collective-permute-start.7
  42.5 0.0 collective-permute-done.8.refs_3_
  42.5 0.1 slice_bitcast_fusion
  42.6 0.7 collective-permute-start.9
  43.3 2.5 %collective-permute-done.6.refs_1_ = bf16[2,272,2048]{2,1,0:T(8,128)(2,1)S(1)} collective-permute-done((bf16[2,272,2048]{2,1,0:T(8,128)(2,1)S(1)}, bf16[2,272,2048]{2,1,0:T(8,128)(2,1)S(1)}, u32[]{:S(2)}, u32[]{:S(2)}) %collective-permute-start.6) | collective-permute-done | bytes 2228256 | tf_op jit(solution)/shard_map/ppermute | solution.py:737
  45.8 1.4 %collective-permute-start.11 = (bf16[1,2,128,512]{3,2,1,0:T(8,128)(2,1)S(1)}, bf16[1,2,128,512]{3,2,1,0:T(8,128)(2,1)S(1)}, u32[]{:S(2)}, u32[]{:S(2)}) collective-permute-start(bf16[1,2,128,512]{3,2,1,0:T(8,128)(2,1)S(1)} %get-tuple-element.86), channel_id=1, source_target_pairs={{0,4},{4,0},{8,12},{12,8},{16,20},{20,16},{24,28},{28,24},{1,5},{5... | collective-permute-start | bytes 786440 | tf_op jit(solution)/shard_map/ppermute | solution.py:731
  47.2 1.2 %collective-permute-done.11 = bf16[1,2,128,512]{3,2,1,0:T(8,128)(2,1)S(1)} collective-permute-done((bf16[1,2,128,512]{3,2,1,0:T(8,128)(2,1)S(1)}, bf16[1,2,128,512]{3,2,1,0:T(8,128)(2,1)S(1)}, u32[]{:S(2)}, u32[]{:S(2)}) %collective-permute-start.11) | collective-permute-done | bytes 262176 | tf_op jit(solution)/shard_map/ppermute | solution.py:731
  48.3 0.8 add_convert_fusion
  49.1 10.1 %collective-permute-done.10.refs_4_ = bf16[2,272,2048]{2,1,0:T(8,128)(2,1)S(1)} collective-permute-done((bf16[2,272,2048]{2,1,0:T(8,128)(2,1)S(1)}, bf16[2,272,2048]{2,1,0:T(8,128)(2,1)S(1)}, u32[]{:S(2)}, u32[]{:S(2)}) %collective-permute-start.10) | collective-permute-done | bytes 2228256 | tf_op jit(solution)/shard_map/ppermute | solution.py:737
  59.2 0.0 collective-permute-done.9.refs_2_
  59.2 1.7 %carry_states.3 = (bf16[272,2048]{1,0:T(8,128)(2,1)S(1)}, bf16[272,2048]{1,0:T(8,128)(2,1)}) custom-call(bf16[272,4096]{1,0:T(8,128)(2,1)S(1)} %chunk_states.3.mine.refs_0_, bf16[2,272,2048]{2,1,0:T(8,128)(2,1)S(1)} %collective-permute-done.6.refs_1_, bf16[272,2048]{1,0:T(8,128)(2,1)S(1)} %collective-permute-done.9.refs_2_, ...), custom_call_target="tpu_custom_call" | custom-call | flops 1 | bytes 1 | tf_op jit(solution)/shard_map/carry_states/pallas_call | solution.py:257
  60.9 0.2 collective-permute-start.13
  61.1 1.7 %carry_states.2 = (bf16[272,2048]{1,0:T(8,128)(2,1)S(1)}, bf16[272,2048]{1,0:T(8,128)(2,1)}) custom-call(bf16[272,4096]{1,0:T(8,128)(2,1)S(1)} %chunk_states.3.mine.refs_0_, bf16[2,272,2048]{2,1,0:T(8,128)(2,1)S(1)} %collective-permute-done.6.refs_1_, bf16[272,2048]{1,0:T(8,128)(2,1)S(1)} %collective-permute-done.7.refs_2_, ...), custom_call_target="tpu_custom_call" | custom-call | flops 1 | bytes 1 | tf_op jit(solution)/shard_map/carry_states/pallas_call | solution.py:257
  62.8 0.5 collective-permute-start.12
  63.3 4.5 %collective-permute-start.15 = (bf16[2,128,512]{2,1,0:T(8,128)(2,1)}, bf16[2,128,512]{2,1,0:T(8,128)(2,1)}, u32[]{:S(2)}, u32[]{:S(2)}) collective-permute-start(bf16[2,128,512]{2,1,0:T(8,128)(2,1)} %bitcast.6), channel_id=1, source_target_pairs={{8,0},{16,8},{20,4},{24,16},{28,12},{9,1},{17,9},{21,5},{25,17},{2... | collective-permute-start | bytes 786440 | tf_op jit(solution)/shard_map/ppermute | solution.py:737
  67.8 0.9 %copy-done.16 = f32[2,128,256]{2,1,0:T(8,128)S(1)} copy-done((f32[2,128,256]{2,1,0:T(8,128)S(1)}, f32[2,128,256]{2,1,0:T(8,128)}, u32[]{:S(2)}) %copy-start.16) | copy-done | bytes 262168
  68.7 2.7 %across_sums.1.acc_in = f32[2,128,256]{2,1,0:T(8,128)S(1)} custom-call(s32[1]{0:T(128)} %bitcast.1.kind.refs_0_.core, bf16[128,4096]{1,0:T(8,128)(2,1)} %x.9, bf16[128,4096]{1,0:T(8,128)(2,1)} %dy.9, f32[3,128,64]{2,1,0:T(8,128)S(1)} %get-tuple-element.79.decays.refs_3_, bf16[272,2048]{1,0:T(8,128)(2,1)S(1)} %get-tuple-element.92.low.refs_4_, ...), custom_call_target="tpu_custom_call" | custom-call | flops 1 | bytes 1 | tf_op jit(solution)/shard_map/across_sums/pallas_call | solution.py:410
  71.4 0.0 collective-permute-done.13.high.refs_5_
  71.5 0.0 collective-permute-done.12.low.refs_5_
  71.5 0.0 copy-start.3
  71.5 0.0 copy-start.5
  71.5 0.0 copy-start.7
  71.5 0.0 copy-start.9
  71.5 3.0 %given_sums.1 = (f32[2,64,256]{2,1,0:T(8,128)S(1)}, bf16[2,64,256]{2,1,0:T(8,128)(2,1)S(1)}) custom-call(s32[1]{0:T(128)S(6)} %sub.8.kind.other, s32[1]{0:T(128)} %bitcast.4.side, bf16[128,4096]{1,0:T(8,128)(2,1)} %x.9, bf16[128,4096]{1,0:T(8,128)(2,1)} %dy.9, f32[3,128,64]{2,1,0:T(8,128)S(1)} %get-tuple-element.79.decays.refs_3_, ...), custom_call_target="tpu_custom_call" | custom-call | flops 1 | bytes 1 | tf_op jit(solution)/shard_map/given_sums/pallas_call | solution.py:462
  74.6 0.1 collective-permute-start.14
  74.7 1.8 %across_outputs.2 = (bf16[128,4096]{1,0:T(8,128)(2,1)}, bf16[128,4096]{1,0:T(8,128)(2,1)}) custom-call(s32[1]{0:T(128)} %bitcast.1.kind.refs_0_.core, bf16[128,256]{1,0:T(8,128)(2,1)S(1)} %copy-done.7, bf16[128,256]{1,0:T(8,128)(2,1)S(1)} %copy-done.9, f32[3,128,64]{2,1,0:T(8,128)S(1)} %get-tuple-element.79.decays.refs_3_, ...), custom_call_target="tpu_custom_call" | custom-call | flops 1 | bytes 1 | tf_op jit(solution)/shard_map/across_outputs/pallas_call | solution.py:541
  76.6 2.2 %collective-permute-done.14.moved = bf16[2,64,256]{2,1,0:T(8,128)(2,1)S(1)} collective-permute-done((bf16[2,64,256]{2,1,0:T(8,128)(2,1)S(1)}, bf16[2,64,256]{2,1,0:T(8,128)(2,1)S(1)}, u32[]{:S(2)}, u32[]{:S(2)}) %collective-permute-start.14) | collective-permute-done | bytes 65568 | tf_op jit(solution)/shard_map/ppermute | solution.py:850
  78.7 1.0 %partner_part.1 = bf16[128,512]{1,0:T(8,128)(2,1)S(1)} custom-call(s32[1]{0:T(128)S(6)} %sub.8.kind.other, bf16[128,512]{1,0:T(8,128)(2,1)S(1)} %copy-done.18, bf16[2,128,512]{2,1,0:T(8,128)(2,1)} %collective-permute-done.15.refs_0_), custom_call_target="tpu_custom_call" | custom-call | flops 1 | bytes 1 | tf_op jit(solution)/shard_map/partner_part/pallas_call | solution.py:567
  79.7 2.5 %collective-permute-start.17 = (bf16[128,512]{1,0:T(8,128)(2,1)S(1)}, bf16[128,512]{1,0:T(8,128)(2,1)S(1)}, u32[]{:S(2)}, u32[]{:S(2)}) collective-permute-start(bf16[128,512]{1,0:T(8,128)(2,1)S(1)} %partner_part.1), channel_id=1, source_target_pairs={{0,4},{4,0},{8,12},{12,8},{16,20},{20,16},{24,28},{28,24},{1,5},{5... | collective-permute-start | bytes 393224 | tf_op jit(solution)/shard_map/ppermute | solution.py:731
  82.2 1.9 %collective-permute-start.16 = (bf16[2,32,256]{2,1,0:T(8,128)(2,1)S(1)}, bf16[2,32,256]{2,1,0:T(8,128)(2,1)S(1)}, u32[]{:S(2)}, u32[]{:S(2)}) collective-permute-start(bf16[2,32,256]{2,1,0:T(8,128)(2,1)S(1)} %get-tuple-element.107), channel_id=1, source_target_pairs={{0,1},{1,0},{2,3},{3,2},{4,5},{5,4},{6,7},{7,6},{8,9},{9,8},{10,11... | collective-permute-start | bytes 98312 | tf_op jit(solution)/shard_map/ppermute | solution.py:850
  84.1 2.8 %across_outputs.3 = (bf16[128,4096]{1,0:T(8,128)(2,1)}, bf16[128,4096]{1,0:T(8,128)(2,1)}) custom-call(s32[1]{0:T(128)} %bitcast.1.kind.refs_0_.core, bf16[128,256]{1,0:T(8,128)(2,1)S(1)} %copy-done.7, bf16[128,256]{1,0:T(8,128)(2,1)S(1)} %copy-done.9, ...), custom_call_target="tpu_custom_call", output_to_operand_aliasing={{0}: (8, {}), {1}: (9, {})} | custom-call | flops 1 | bytes 1 | tf_op jit(solution)/shard_map/across_outputs/pallas_call | solution.py:541
  87.0 1.6 %last_sums.1 = (bf16[128,256]{1,0:T(8,128)(2,1)}, bf16[128,256]{1,0:T(8,128)(2,1)}, bf16[32,256]{1,0:T(8,128)(2,1)}, bf16[32,256]{1,0:T(8,128)(2,1)}) custom-call(s32[1]{0:T(128)} %bitcast.1.kind.refs_0_.core, f32[128,512]{1,0:T(8,128)S(1)} %copy-done.14, bf16[128,512]{1,0:T(8,128)(2,1)S(1)} %collective-permute-done.17.swapped, ...), custom_call_target="tpu_custom_call" | custom-call | flops 1 | bytes 1 | tf_op jit(solution)/shard_map/last_sums/pallas_call | solution.py:593
  (28 shorter events, 0.1 us)
Async XLA Ops:
  4.5 9.4 %collective-permute-start.2 = (bf16[272,4096]{1,0:T(8,128)(2,1)S(1)}, bf16[272,4096]{1,0:T(8,128)(2,1)S(1)}, u32[]{:S(2)}, u32[]{:S(2)}) collective-permute-start(bf16[272,4096]{1,0:T(8,128)(2,1)S(1)} %get-tuple-element.71), channel_id=1, source_target_pairs={{0,4},{4,0},{8,12},{12,8},{16,20},{20,16},{24,28},{28,24},{1,5},{5... | collective-permute-start | bytes 6684680 | tf_op jit(solution)/shard_map/ppermute | solution.py:731
  5.2 7.3 %collective-permute-start = (bf16[144,512]{1,0:T(8,128)(2,1)S(1)}, bf16[144,512]{1,0:T(8,128)(2,1)S(1)}, u32[]{:S(2)}, u32[]{:S(2)}) collective-permute-start(bf16[144,512]{1,0:T(8,128)(2,1)S(1)} %get-tuple-element.69.refs_4_), channel_id=1, source_target_pairs={{0,8},{4,12},{8,16},{12,20},{16,24},{20,28},{1,9},{5,13},{9,17},{1... | collective-permute-start | bytes 442376 | tf_op jit(solution)/shard_map/ppermute | solution.py:726
  6.5 7.4 %collective-permute-start.1 = (bf16[144,512]{1,0:T(8,128)(2,1)S(1)}, bf16[144,512]{1,0:T(8,128)(2,1)S(1)}, u32[]{:S(2)}, u32[]{:S(2)}) collective-permute-start(bf16[144,512]{1,0:T(8,128)(2,1)S(1)} %get-tuple-element.69.refs_4_), channel_id=1, source_target_pairs={{0,16},{4,20},{8,24},{12,28},{1,17},{5,21},{9,25},{13,29},{2,18},{... | collective-permute-start | bytes 442376 | tf_op jit(solution)/shard_map/ppermute | solution.py:726
  11.6 13.2 %copy-start = (bf16[128,4096]{1,0:T(8,128)(2,1)S(1)}, bf16[128,4096]{1,0:T(8,128)(2,1)}, u32[]{:S(2)}) copy-start(bf16[128,4096]{1,0:T(8,128)(2,1)} %x.9) | copy-start | bytes 3145732
  11.6 13.2 %copy-start.1 = (bf16[128,4096]{1,0:T(8,128)(2,1)S(1)}, bf16[128,4096]{1,0:T(8,128)(2,1)}, u32[]{:S(2)}) copy-start(bf16[128,4096]{1,0:T(8,128)(2,1)} %dy.9) | copy-start | bytes 3145732
  11.6 13.2 %copy-start.6 = (bf16[128,256]{1,0:T(8,128)(2,1)S(1)}, bf16[128,256]{1,0:T(8,128)(2,1)}, u32[]{:S(2)}) copy-start(bf16[128,256]{1,0:T(8,128)(2,1)} %refs_1_.7) | copy-start | bytes 196612
  11.6 13.2 %copy-start.8 = (bf16[128,256]{1,0:T(8,128)(2,1)S(1)}, bf16[128,256]{1,0:T(8,128)(2,1)}, u32[]{:S(2)}) copy-start(bf16[128,256]{1,0:T(8,128)(2,1)} %refs_2_.5) | copy-start | bytes 196612
  11.6 13.2 %copy-start.12 = (f32[128,64]{0,1:T(8,128)S(1)}, f32[128,64]{0,1:T(8,128)}, u32[]{:S(2)}) copy-start(f32[128,64]{0,1:T(8,128)} %param.18) | copy-start | bytes 98308
  11.6 13.1 %copy-start.19 = (s32[128]{0:T(128)S(1)}, s32[128]{0:T(128)}, u32[]{:S(2)}) copy-start(s32[128]{0:T(128)} %param.14) | copy-start | bytes 1540
  14.6 16.9 %copy-start.10 = (bf16[128,2048]{1,0:T(8,128)(2,1)S(1)}, bf16[128,2048]{1,0:T(8,128)(2,1)}, u32[]{:S(2)}) copy-start(bf16[128,2048]{1,0:T(8,128)(2,1)} %refs_1_.5) | copy-start | bytes 1572868
  14.6 16.9 %copy-start.11 = (bf16[128,2048]{1,0:T(8,128)(2,1)S(1)}, bf16[128,2048]{1,0:T(8,128)(2,1)}, u32[]{:S(2)}) copy-start(bf16[128,2048]{1,0:T(8,128)(2,1)} %refs_2_.3) | copy-start | bytes 1572868
  14.6 27.9 %collective-permute-start.8 = (bf16[2,272,2048]{2,1,0:T(8,128)(2,1)S(1)}, bf16[2,272,2048]{2,1,0:T(8,128)(2,1)S(1)}, u32[]{:S(2)}, u32[]{:S(2)}) collective-permute-start(bf16[2,272,2048]{2,1,0:T(8,128)(2,1)S(1)} %get-tuple-element.72), channel_id=1, source_target_pairs={{8,24},{20,4},{9,25},{21,5},{10,26},{22,6},{11,27},{23,7}} | collective-permute-start | bytes 6684680 | tf_op jit(solution)/shard_map/ppermute | solution.py:737
  15.5 30.3 %collective-permute-start.6 = (bf16[2,272,2048]{2,1,0:T(8,128)(2,1)S(1)}, bf16[2,272,2048]{2,1,0:T(8,128)(2,1)S(1)}, u32[]{:S(2)}, u32[]{:S(2)}) collective-permute-start(bf16[2,272,2048]{2,1,0:T(8,128)(2,1)S(1)} %get-tuple-element.72), channel_id=1, source_target_pairs={{0,8},{12,4},{16,24},{28,20},{1,9},{13,5},{17,25},{29,21},{2,10},{... | collective-permute-start | bytes 6684680 | tf_op jit(solution)/shard_map/ppermute | solution.py:737
  21.6 37.6 %collective-permute-start.10 = (bf16[2,272,2048]{2,1,0:T(8,128)(2,1)S(1)}, bf16[2,272,2048]{2,1,0:T(8,128)(2,1)S(1)}, u32[]{:S(2)}, u32[]{:S(2)}) collective-permute-start(bf16[2,272,2048]{2,1,0:T(8,128)(2,1)S(1)} %get-tuple-element.72), channel_id=1, source_target_pairs={{0,16},{28,12},{1,17},{29,13},{2,18},{30,14},{3,19},{31,15}} | collective-permute-start | bytes 6684680 | tf_op jit(solution)/shard_map/ppermute | solution.py:737
  23.2 1.4 %collective-permute-start.3 = (bf16[144,512]{1,0:T(8,128)(2,1)S(1)}, bf16[144,512]{1,0:T(8,128)(2,1)S(1)}, u32[]{:S(2)}, u32[]{:S(2)}) collective-permute-start(bf16[144,512]{1,0:T(8,128)(2,1)S(1)} %get-tuple-element.69.refs_4_), channel_id=1, source_target_pairs={{0,4},{4,0},{8,12},{12,8},{16,20},{20,16},{24,28},{28,24},{1,5},{5... | collective-permute-start | bytes 442376 | tf_op jit(solution)/shard_map/ppermute | solution.py:731
  23.3 8.2 %collective-permute-start.4 = (bf16[144,512]{1,0:T(8,128)(2,1)S(1)}, bf16[144,512]{1,0:T(8,128)(2,1)S(1)}, u32[]{:S(2)}, u32[]{:S(2)}) collective-permute-start(bf16[144,512]{1,0:T(8,128)(2,1)S(1)} %collective-permute-done.refs_6_), channel_id=1, source_target_pairs={{0,4},{4,0},{8,12},{12,8},{16,20},{20,16},{24,28},{28,24},{1,5},{5... | collective-permute-start | bytes 442376 | tf_op jit(solution)/shard_map/ppermute | solution.py:731
  24.6 6.8 %collective-permute-start.5 = (bf16[144,512]{1,0:T(8,128)(2,1)S(1)}, bf16[144,512]{1,0:T(8,128)(2,1)S(1)}, u32[]{:S(2)}, u32[]{:S(2)}) collective-permute-start(bf16[144,512]{1,0:T(8,128)(2,1)S(1)} %collective-permute-done.1.refs_7_), channel_id=1, source_target_pairs={{0,4},{4,0},{8,12},{12,8},{16,20},{20,16},{24,28},{28,24},{1,5},{5... | collective-permute-start | bytes 442376 | tf_op jit(solution)/shard_map/ppermute | solution.py:731
  28.8 1.0 %copy-start.2 = (bf16[128,4096]{1,0:T(8,128)(2,1)}, bf16[128,4096]{1,0:T(8,128)(2,1)S(1)}, u32[]{:S(2)}) copy-start(bf16[128,4096]{1,0:T(8,128)(2,1)S(1)} %get-tuple-element.101.refs_6_) | copy-start | bytes 3145732
  29.7 1.0 %copy-start.4 = (bf16[128,4096]{1,0:T(8,128)(2,1)}, bf16[128,4096]{1,0:T(8,128)(2,1)S(1)}, u32[]{:S(2)}) copy-start(bf16[128,4096]{1,0:T(8,128)(2,1)S(1)} %get-tuple-element.102.refs_7_) | copy-start | bytes 3145732
  30.7 0.7 copy-start.15
  40.4 0.7 copy-start.13
  41.1 0.7 copy-start.17
  41.7 7.4 %collective-permute-start.7 = (bf16[272,2048]{1,0:T(8,128)(2,1)S(1)}, bf16[272,2048]{1,0:T(8,128)(2,1)S(1)}, u32[]{:S(2)}, u32[]{:S(2)}) collective-permute-start(bf16[272,2048]{1,0:T(8,128)(2,1)S(1)} %get-tuple-element.84), channel_id=1, source_target_pairs={{8,16},{20,12},{9,17},{21,13},{10,18},{22,14},{11,19},{23,15}} | collective-permute-start | bytes 3342344 | tf_op jit(solution)/shard_map/ppermute | solution.py:737
  42.6 16.6 %collective-permute-start.9 = (bf16[272,2048]{1,0:T(8,128)(2,1)S(1)}, bf16[272,2048]{1,0:T(8,128)(2,1)S(1)}, u32[]{:S(2)}, u32[]{:S(2)}) collective-permute-start(bf16[272,2048]{1,0:T(8,128)(2,1)S(1)} %slice_bitcast_fusion), channel_id=1, source_target_pairs={{4,12},{24,16},{5,13},{25,17},{6,14},{26,18},{7,15},{27,19}} | collective-permute-start | bytes 3342344 | tf_op jit(solution)/shard_map/ppermute | solution.py:737
  45.8 2.5 %collective-permute-start.11 = (bf16[1,2,128,512]{3,2,1,0:T(8,128)(2,1)S(1)}, bf16[1,2,128,512]{3,2,1,0:T(8,128)(2,1)S(1)}, u32[]{:S(2)}, u32[]{:S(2)}) collective-permute-start(bf16[1,2,128,512]{3,2,1,0:T(8,128)(2,1)S(1)} %get-tuple-element.86), channel_id=1, source_target_pairs={{0,4},{4,0},{8,12},{12,8},{16,20},{20,16},{24,28},{28,24},{1,5},{5... | collective-permute-start | bytes 786440 | tf_op jit(solution)/shard_map/ppermute | solution.py:731
  60.9 10.5 %collective-permute-start.13 = (bf16[272,2048]{1,0:T(8,128)(2,1)}, bf16[272,2048]{1,0:T(8,128)(2,1)}, u32[]{:S(2)}, u32[]{:S(2)}) collective-permute-start(bf16[272,2048]{1,0:T(8,128)(2,1)} %get-tuple-element.97), channel_id=1, source_target_pairs={{0,4},{4,0},{8,12},{12,8},{16,20},{20,16},{24,28},{28,24},{1,5},{5... | collective-permute-start | bytes 3342344 | tf_op jit(solution)/shard_map/ppermute | solution.py:731
  62.8 8.7 %collective-permute-start.12 = (bf16[272,2048]{1,0:T(8,128)(2,1)}, bf16[272,2048]{1,0:T(8,128)(2,1)S(1)}, u32[]{:S(2)}, u32[]{:S(2)}) collective-permute-start(bf16[272,2048]{1,0:T(8,128)(2,1)} %get-tuple-element.96), channel_id=1, source_target_pairs={{0,4},{4,0},{8,12},{12,8},{16,20},{20,16},{24,28},{28,24},{1,5},{5... | collective-permute-start | bytes 3342344 | tf_op jit(solution)/shard_map/ppermute | solution.py:731
  63.3 13.3 %collective-permute-start.15 = (bf16[2,128,512]{2,1,0:T(8,128)(2,1)}, bf16[2,128,512]{2,1,0:T(8,128)(2,1)}, u32[]{:S(2)}, u32[]{:S(2)}) collective-permute-start(bf16[2,128,512]{2,1,0:T(8,128)(2,1)} %bitcast.6), channel_id=1, source_target_pairs={{8,0},{16,8},{20,4},{24,16},{28,12},{9,1},{17,9},{21,5},{25,17},{2... | collective-permute-start | bytes 786440 | tf_op jit(solution)/shard_map/ppermute | solution.py:737
  67.8 0.9 %copy-start.16 = (f32[2,128,256]{2,1,0:T(8,128)S(1)}, f32[2,128,256]{2,1,0:T(8,128)}, u32[]{:S(2)}) copy-start(f32[2,128,256]{2,1,0:T(8,128)} %copy-done.15) | copy-start | bytes 786436
  71.5 3.2 %copy-start.3 = (bf16[128,4096]{1,0:T(8,128)(2,1)S(1)}, bf16[128,4096]{1,0:T(8,128)(2,1)}, u32[]{:S(2)}) copy-start(bf16[128,4096]{1,0:T(8,128)(2,1)} %copy-done.2) | copy-start | bytes 3145732
  71.5 3.2 %copy-start.5 = (bf16[128,4096]{1,0:T(8,128)(2,1)S(1)}, bf16[128,4096]{1,0:T(8,128)(2,1)}, u32[]{:S(2)}) copy-start(bf16[128,4096]{1,0:T(8,128)(2,1)} %copy-done.4) | copy-start | bytes 3145732
  71.5 3.2 %copy-start.7 = (bf16[128,256]{1,0:T(8,128)(2,1)S(1)}, bf16[128,256]{1,0:T(8,128)(2,1)}, u32[]{:S(2)}) copy-start(bf16[128,256]{1,0:T(8,128)(2,1)} %refs_1_.7) | copy-start | bytes 196612
  71.5 3.2 %copy-start.9 = (bf16[128,256]{1,0:T(8,128)(2,1)S(1)}, bf16[128,256]{1,0:T(8,128)(2,1)}, u32[]{:S(2)}) copy-start(bf16[128,256]{1,0:T(8,128)(2,1)} %refs_2_.5) | copy-start | bytes 196612
  74.6 4.1 %collective-permute-start.14 = (bf16[2,64,256]{2,1,0:T(8,128)(2,1)S(1)}, bf16[2,64,256]{2,1,0:T(8,128)(2,1)S(1)}, u32[]{:S(2)}, u32[]{:S(2)}) collective-permute-start(bf16[2,64,256]{2,1,0:T(8,128)(2,1)S(1)} %get-tuple-element.99), channel_id=1, source_target_pairs={{0,2},{1,3},{2,0},{3,1},{4,6},{5,7},{6,4},{7,5},{8,10},{9,11},{10,... | collective-permute-start | bytes 196616 | tf_op jit(solution)/shard_map/ppermute | solution.py:850
  74.7 4.0 %copy-start.18 = (bf16[128,512]{1,0:T(8,128)(2,1)S(1)}, bf16[128,512]{1,0:T(8,128)(2,1)}, u32[]{:S(2)}) copy-start(bf16[128,512]{1,0:T(8,128)(2,1)} %copy-done.17) | copy-start | bytes 393220
  79.7 7.3 %collective-permute-start.17 = (bf16[128,512]{1,0:T(8,128)(2,1)S(1)}, bf16[128,512]{1,0:T(8,128)(2,1)S(1)}, u32[]{:S(2)}, u32[]{:S(2)}) collective-permute-start(bf16[128,512]{1,0:T(8,128)(2,1)S(1)} %partner_part.1), channel_id=1, source_target_pairs={{0,4},{4,0},{8,12},{12,8},{16,20},{20,16},{24,28},{28,24},{1,5},{5... | collective-permute-start | bytes 393224 | tf_op jit(solution)/shard_map/ppermute | solution.py:731
  82.2 4.7 %collective-permute-start.16 = (bf16[2,32,256]{2,1,0:T(8,128)(2,1)S(1)}, bf16[2,32,256]{2,1,0:T(8,128)(2,1)S(1)}, u32[]{:S(2)}, u32[]{:S(2)}) collective-permute-start(bf16[2,32,256]{2,1,0:T(8,128)(2,1)S(1)} %get-tuple-element.107), channel_id=1, source_target_pairs={{0,1},{1,0},{2,3},{3,2},{4,5},{5,4},{6,7},{7,6},{8,9},{9,8},{10,11... | collective-permute-start | bytes 98312 | tf_op jit(solution)/shard_map/ppermute | solution.py:850
  84.1 2.9 %copy-start.14 = (f32[128,512]{1,0:T(8,128)S(1)}, f32[128,512]{1,0:T(8,128)}, u32[]{:S(2)}) copy-start(f32[128,512]{1,0:T(8,128)} %copy-done.13) | copy-start | bytes 786436
